TPU v7x, 128 devices: a whole 4x4x4 slice. The times are simulated.
128 devices in a mesh: frame: 8 (over x, y_hi), pair: 16 (over y_lo, z, core).
Axes of the slice: x: 4, y: 4 (y_hi: 2, y_lo: 2; y = y_hi * 2 + y_lo), z: 4, core: 2. Of those that a mesh axis runs over, the one named last changes fastest.
Arguments:
- columns: float32 [16384, 16384], P('frame', 'pair')
- rotations: float32 [2, 32, 512, 512], P(None, 'pair'), as said below
- plan: int32 [2, 16, 4], P(None, 'pair'), may hold values from 0 to 3, as said below
Outputs:
- final_columns: float32 [16384, 16384], P('frame', 'pair')
- pair_grams: float32 [2, 512, 32, 512], P(None, 'frame', 'pair')
Inputs may be any that keep to these rules, and one draw needn't show every extreme that they name: Each plan[s, h, :] is a permutation of 0 to 3. Each rotations[s, p] is the identity plus a random perturbation, well conditioned.
All inputs are finite; a program needn't handle non-finite values.
Results may differ from a plain program's by a relative error of at most 0.0001.
Values sent between devices are 32-bit elements; how exact they have to be, the bound alone decides.
No kernel may reach another device: no remote copies, remote signals or barrier semaphores. Data moves between devices by JAX's collectives and lax.ppermute only.
A program may use at most 320 MiB of HBM per device.

v0:
```python
import jax
import jax.numpy as jnp
from jax import lax
from jax.sharding import PartitionSpec as P

BW = 256
STEPS = 2


epsilon = 1e-06


def from_behind(x, axis, by):
    size = lax.axis_size(axis)
    return lax.ppermute(x, axis, [(i, (i + by) % size) for i in range(size)])


def local(columns, rotations, plan):
    rows = columns.shape[0]
    frames = lax.axis_size("frame")
    total_rows = rows * frames
    pairs_here = rotations.shape[1]
    width = 2 * BW // frames
    blocks = columns.reshape(rows, 2 * pairs_here, BW)
    grams_list = []
    for step in range(STEPS):
        arranged = jnp.take(blocks, plan[step, 0], axis=1)
        paired = arranged.reshape(rows, pairs_here, 2 * BW)
        rotation = rotations[step]
        local_gram = jnp.einsum("rpi,rpj->pij", paired, paired, precision=lax.Precision.HIGHEST)
        gram = lax.psum(local_gram, "frame")
        diagonal_sq = jnp.diagonal(gram, axis1=1, axis2=2)
        scale = jnp.sqrt(jnp.float32(total_rows)) * lax.rsqrt(diagonal_sq + epsilon)
        correlation = gram * scale[:, :, None] * scale[:, None, :] / total_rows
        left_part = jnp.einsum(
            "pki,pkj->pij", rotation, correlation, precision=lax.Precision.HIGHEST
        )
        turned = jnp.einsum("pik,pkj->pij", left_part, rotation, precision=lax.Precision.HIGHEST)
        start_row = lax.axis_index("frame") * width
        gram_rows = jnp.transpose(lax.dynamic_slice_in_dim(turned, start_row, width, 1), (1, 0, 2))
        updated = jnp.einsum(
            "rpi,pij->rpj", paired * scale[None], rotation, precision=lax.Precision.HIGHEST
        )
        grams_list.append(gram_rows)
        slots = updated.reshape(rows, 2 * pairs_here, BW)
        from_before = from_behind(slots[:, 1], "pair", 1)
        from_after = from_behind(slots[:, 3], "pair", -1)
        blocks = jnp.stack([slots[:, 0], slots[:, 2], from_before, from_after], axis=1)
    return (blocks.reshape(rows, 2 * pairs_here * BW), jnp.stack(grams_list))


def solution(mesh):
    in_specs = (P("frame", "pair"), P(None, "pair", None, None), P(None, "pair", None))
    out_specs = (P("frame", "pair"), P(None, "frame", "pair", None))
    return jax.shard_map(local, mesh=mesh, in_specs=in_specs, out_specs=out_specs, check_vma=False)
```

profile of v0, /device:TPU:12, one launch (start us, length us, event | category | flops | bytes accessed | tf_op | source)
XLA Modules:
  0.0 553.4 jit_solution(4695789009592098422)
XLA Ops:
  7.2 0.0 all-reduce.3.cloned.1.call-start
  7.2 0.7 compare_and_fusion
  7.9 9.1 %copy.40 = f32[2048,1024]{0,1:T(8,128)} copy(f32[2048,1024]{1,0:T(8,128)} %param.5) | data formatting | bytes 16777216 | tf_op args[0]
  17.0 7.7 %gather_fusion.2 = f32[4,2048,256]{1,2,0:T(8,128)} fusion(f32[2048,4,256]{0,2,1:T(8,128)} %bitcast.75, s32[1024]{0:T(1024)S(1)} %pad_clamp_fusion.1), kind=kCustom, calls=%fused_computation.clone | custom fusion | bytes 16777232 | tf_op jit(solution)/shard_map/jit(_take)/gather | solution.py:27
  24.7 4.3 broadcast_select_fusion.1
  29.0 0.0 copy-start
  29.1 3.4 copy-done
  32.4 14.8 %fusion.38 = f32[2,512,512]{2,1,0:T(8,128)} fusion(f32[2048,2,512]{0,2,1:T(8,128)S(1)} %bitcast.71), kind=kOutput, calls=%fused_computation.62 | convolution fusion | flops 12884901888 | bytes 10485760 | tf_op jit(solution)/shard_map/rpi,rpj->pij/dot_general | solution.py:30
  47.3 0.0 all-reduce.3.cloned.1.call-update
  47.3 0.6 all-reduce.5.cloned.1.call-start
  47.9 109.6 %all-reduce.3.cloned.1.call-done = f32[2,512,512]{2,1,0:T(8,128)} async-done(((f32[2,512,512]{2,1,0:T(8,128)}), f32[2,512,512]{2,1,0:T(8,128)}) %all-reduce.3.cloned.1.call-update) | async-done | bytes 2097168 | tf_op jit(solution)/shard_map/psum | solution.py:31
  157.5 60.1 %copy.42 = f32[2,512,512]{0,2,1:T(8,128)} copy(f32[2,512,512]{2,1,0:T(8,128)} %all-reduce.3.cloned.1.call-done) | data formatting | bytes 4194304 | tf_op jit(solution)/shard_map/psum | solution.py:31
  217.6 5.6 %gather_fusion = f32[512,2]{1,0:T(8,128)S(1)} fusion(f32[2,512,512]{0,2,1:T(8,128)} %copy.42, s32[512]{0:T(512)S(1)} %bitcast.69), kind=kCustom, calls=%fused_computation.2 | custom fusion | bytes 12288 | tf_op jit(solution)/shard_map/jit(diagonal)/gather | solution.py:32
  223.2 0.1 copy.76
  223.3 18.1 %fusion.2 = f32[2,2048,512]{1,2,0:T(8,128)S(1)} fusion(f32[2048,2,512]{0,2,1:T(8,128)} %bitcast.72, f32[2,512]{1,0:T(2,128)S(1)} %bitcast.81, f32[2,2,512,512]{3,2,1,0:T(8,128)} %param.6), kind=kOutput, calls=%fused_computation.8 | convolution fusion | flops 12886999040 | bytes 18878464 | tf_op jit(solution)/shard_map/rpi,pij->rpj/dot_general | solution.py:41
  241.3 1.1 fusion.37
  242.5 3.3 collective-permute-start.1
  245.8 0.2 collective-permute-start
  245.9 23.4 %collective-permute-done.1 = f32[2048,256]{0,1:T(8,128)S(1)} collective-permute-done((f32[2048,256]{0,1:T(8,128)S(1)}, f32[2048,256]{0,1:T(8,128)S(1)}, u32[]{:S(2)}, u32[]{:S(2)}) %collective-permute-start.1) | collective-permute-done | bytes 2097184 | tf_op jit(solution)/shard_map/ppermute | solution.py:15
  269.3 4.2 collective-permute-done
  273.5 3.7 pad_maximum_fusion
  277.2 7.7 %gather_fusion.3 = f32[4,2048,256]{1,2,0:T(8,128)} fusion(f32[2048,4,256]{0,2,1:T(8,128)} %pad_maximum_fusion, s32[1024]{0:T(1024)S(1)} %pad_clamp_fusion), kind=kCustom, calls=%fused_computation.1.clone | custom fusion | bytes 16777232 | tf_op jit(solution)/shard_map/jit(_take)/gather | solution.py:27
  284.9 4.3 broadcast_select_fusion
  289.2 0.0 copy-start.1
  289.3 3.4 copy-done.1
  292.6 14.8 %fusion.39 = f32[2,512,512]{2,1,0:T(8,128)} fusion(f32[2048,2,512]{0,2,1:T(8,128)S(1)} %bitcast.73), kind=kOutput, calls=%fused_computation.63 | convolution fusion | flops 12884901888 | bytes 10485760 | tf_op jit(solution)/shard_map/rpi,rpj->pij/dot_general | solution.py:30
  307.5 0.0 all-reduce.5.cloned.1.call-update
  307.5 105.2 %all-reduce.5.cloned.1.call-done = f32[2,512,512]{2,1,0:T(8,128)} async-done(((f32[2,512,512]{2,1,0:T(8,128)}), f32[2,512,512]{2,1,0:T(8,128)}) %all-reduce.5.cloned.1.call-update) | async-done | bytes 2097168 | tf_op jit(solution)/shard_map/psum | solution.py:31
  412.7 60.1 %copy.47 = f32[2,512,512]{0,2,1:T(8,128)} copy(f32[2,512,512]{2,1,0:T(8,128)} %all-reduce.5.cloned.1.call-done) | data formatting | bytes 4194304 | tf_op jit(solution)/shard_map/psum | solution.py:31
  472.8 5.6 %gather_fusion.1 = f32[512,2]{1,0:T(8,128)S(1)} fusion(f32[2,512,512]{0,2,1:T(8,128)} %copy.47, s32[512]{0:T(512)S(1)} %bitcast.70), kind=kCustom, calls=%fused_computation.3 | custom fusion | bytes 12288 | tf_op jit(solution)/shard_map/jit(diagonal)/gather | solution.py:32
  478.4 0.1 copy.77
  478.5 18.2 %fusion = f32[2,2048,512]{1,2,0:T(8,128)S(1)} fusion(f32[2048,2,512]{0,2,1:T(8,128)} %bitcast.74, f32[2,512]{1,0:T(2,128)S(1)} %bitcast.83, f32[2,2,512,512]{3,2,1,0:T(8,128)} %param.6), kind=kOutput, calls=%fused_computation.6 | convolution fusion | flops 12886999040 | bytes 18878464 | tf_op jit(solution)/shard_map/rpi,pij->rpj/dot_general | solution.py:41
  496.7 0.0 copy-start.3
  496.8 3.5 fusion.36
  500.2 3.3 collective-permute-start.3
  503.5 0.2 collective-permute-start.2
  503.8 0.0 copy-done.3
  503.8 0.0 copy-start.2
  503.8 5.8 %fusion.13 = f32[2,512,512]{1,2,0:T(8,128)S(1)} fusion(f32[2,512,512]{2,1,0:T(8,128)S(1)} %copy-done.3, f32[2,2,512,512]{3,2,1,0:T(8,128)} %param.6, f32[2,512]{1,0:T(2,128)S(1)} %bitcast.82), kind=kOutput, calls=%fused_computation.25 | convolution fusion | flops 3222798336 | bytes 6299648 | tf_op jit(solution)/shard_map/pki,pkj->pij/dot_general | solution.py:35
  509.6 0.0 copy-done.2
  509.6 0.0 copy-start.4
  509.6 3.5 fusion.11
  513.2 0.0 copy-done.4
  513.2 4.2 fusion.8
  517.4 0.0 copy-start.6
  517.4 3.9 fusion.6
  521.2 0.0 copy-start.5
  521.4 1.2 copy.60
  522.6 4.8 collective-permute-done.3
  527.4 4.2 collective-permute-done.2
  531.6 0.0 copy-done.6
  531.6 0.0 copy-done.5
  531.6 5.2 pad_maximum_fusion.1
  536.8 9.2 %copy.73 = f32[2048,1024]{1,0:T(8,128)} copy(f32[2048,1024]{0,1:T(8,128)} %bitcast.78) | data formatting | bytes 16777216 | tf_op jit(solution)/shard_map/reshape | solution.py:49
  (7 shorter events, 0.2 us)
Async XLA Ops:
  7.2 150.3 %all-reduce.3.cloned.1.call-start = ((), (), s32[]{:S(2)}) async-start(), calls=%async_computation | async-start | bytes 4194304 | tf_op jit(solution)/shard_map/psum | solution.py:31
  29.0 3.4 copy-start
  47.3 365.4 %all-reduce.5.cloned.1.call-start = ((), (), s32[]{:S(2)}) async-start(), calls=%async_computation.1 | async-start | bytes 4194304 | tf_op jit(solution)/shard_map/psum | solution.py:31
  242.5 26.9 %collective-permute-start.1 = (f32[2048,256]{0,1:T(8,128)S(1)}, f32[2048,256]{0,1:T(8,128)S(1)}, u32[]{:S(2)}, u32[]{:S(2)}) collective-permute-start(f32[2048,256]{0,1:T(8,128)S(1)} %get-tuple-element.18), channel_id=1, source_target_pairs={{0,15},{1,0},{2,1},{3,2},{4,3},{5,4},{6,5},{7,6},{8,7},{9,8},{10,9... | collective-permute-start | bytes 6291464 | tf_op jit(solution)/shard_map/ppermute | solution.py:15
  245.8 27.7 %collective-permute-start = (f32[2048,256]{0,1:T(8,128)S(1)}, f32[2048,256]{0,1:T(8,128)S(1)}, u32[]{:S(2)}, u32[]{:S(2)}) collective-permute-start(f32[2048,256]{0,1:T(8,128)S(1)} %get-tuple-element.19), channel_id=1, source_target_pairs={{0,1},{1,2},{2,3},{3,4},{4,5},{5,6},{6,7},{7,8},{8,9},{9,10},{10,1... | collective-permute-start | bytes 6291464 | tf_op jit(solution)/shard_map/ppermute | solution.py:15
  289.2 3.4 copy-start.1
  496.7 7.0 %copy-start.3 = (f32[2,512,512]{2,1,0:T(8,128)S(1)}, f32[2,512,512]{2,1,0:T(8,128)}, u32[]{:S(2)}) copy-start(f32[2,512,512]{2,1,0:T(8,128)} %all-reduce.3.cloned.1.call-done) | copy-start | bytes 6291460
  500.2 27.1 %collective-permute-start.3 = (f32[2048,256]{0,1:T(8,128)}, f32[2048,256]{0,1:T(8,128)}, u32[]{:S(2)}, u32[]{:S(2)}) collective-permute-start(f32[2048,256]{0,1:T(8,128)} %get-tuple-element.14), channel_id=1, source_target_pairs={{0,15},{1,0},{2,1},{3,2},{4,3},{5,4},{6,5},{7,6},{8,7},{9,8},{10,9... | collective-permute-start | bytes 6291464 | tf_op jit(solution)/shard_map/ppermute | solution.py:15
  503.5 28.1 %collective-permute-start.2 = (f32[2048,256]{0,1:T(8,128)}, f32[2048,256]{0,1:T(8,128)}, u32[]{:S(2)}, u32[]{:S(2)}) collective-permute-start(f32[2048,256]{0,1:T(8,128)} %get-tuple-element.15), channel_id=1, source_target_pairs={{0,1},{1,2},{2,3},{3,4},{4,5},{5,6},{6,7},{7,8},{8,9},{9,10},{10,1... | collective-permute-start | bytes 6291464 | tf_op jit(solution)/shard_map/ppermute | solution.py:15
  503.8 5.8 %copy-start.2 = (f32[2,2,512,512]{3,2,1,0:T(8,128)S(1)}, f32[2,2,512,512]{3,2,1,0:T(8,128)}, u32[]{:S(2)}) copy-start(f32[2,2,512,512]{3,2,1,0:T(8,128)} %param.6) | copy-start | bytes 12582916
  509.6 3.6 copy-start.4
  517.4 14.2 %copy-start.6 = (f32[2048,1,256]{0,2,1:T(8,128)S(1)}, f32[2048,1,256]{0,2,1:T(8,128)}, u32[]{:S(2)}) copy-start(f32[2048,1,256]{0,2,1:T(8,128)} %get-tuple-element.16) | copy-start | bytes 6291460
  521.2 10.4 %copy-start.5 = (f32[2048,1,256]{0,2,1:T(8,128)S(1)}, f32[2048,1,256]{0,2,1:T(8,128)}, u32[]{:S(2)}) copy-start(f32[2048,1,256]{0,2,1:T(8,128)} %get-tuple-element.13) | copy-start | bytes 6291460
Sparse Core Ops, SparseCore 0:
  47.4 110.0 all-reduce.2
  307.6 105.0 all-reduce.4
where the time goes:
time: 564 us; the launch traced here: 553 us
  waiting for transfers between devices  251 us (45%)
  local copies, waits for them, and re-layouts  178 us (32%)
  matrix products  83.3 us (15%)
  other arithmetic  18.4 us (3%)
  between operations  14.8 us (3%)
  starting transfers between devices  7.57 us (1%)
    psum x2, waiting for transfers between devices, local(): gram = lax.psum(local_gram, 'frame')  215 us
    psum x2, local copies, waits for them, and re-layouts, local(): gram = lax.psum(local_gram, 'frame')  120 us
    ppermute x4, waiting for transfers between devices, from_behind(): return lax.ppermute(x, axis, [(i, (i + by) % size) for i in range(size)])  36.6 us
    dot_general x2, matrix products, local(): jnp.einsum('rpi,pij->rpj', paired * scale[None], rotation, precision=lax....  36.3 us
    dot_general x2, matrix products, local(): jnp.einsum('rpi,rpj->pij', paired, paired, precision=lax.Precision.HIGHEST)  29.6 us
    unnamed x18, local copies, waits for them, and re-layouts  17.4 us
    gather x2, local copies, waits for them, and re-layouts, local(): arranged = jnp.take(blocks, plan[step, 0], axis=1)  15.4 us
  transfers between devices with their start and end apart: 6, of which 6 were waited for; matrix products, arithmetic and copies ran while one was open for 3% of the time, Pallas kernels for 0%

commit v1 on v0

v1 whole, which is shorter than its diff:
```python
import functools

import jax
import jax.numpy as jnp
from jax import lax
from jax.experimental import pallas as pl
from jax.experimental.pallas import tpu as pltpu
from jax.sharding import PartitionSpec as P

BW = 256
STEPS = 2
PARTS = 2
CHUNK = 256
VMEM = 48 * 1024 * 1024

epsilon = 1e-06


def params(grid_dims=1):
    return pltpu.CompilerParams(
        dimension_semantics=("arbitrary",) * grid_dims, vmem_limit_bytes=VMEM
    )


def split(x):
    high = x.astype(jnp.bfloat16)
    low = (x - high.astype(jnp.float32)).astype(jnp.bfloat16)
    return high, low


def dot(a, b):
    return jnp.dot(a, b, preferred_element_type=jnp.float32)


def add_squares(acc, slot, x):
    rows, cols = x.shape
    for half in range(cols // 128):
        piece = x[:, half * 128 : (half + 1) * 128]
        squares = (piece * piece).reshape(rows // 8, 8, 128)
        acc[2 * slot + half] += jnp.sum(squares, axis=0)


def put_sums(sums_ref, acc):
    for row in range(8):
        sums_ref[row : row + 1, :] = jnp.sum(acc[row], axis=0, keepdims=True)


def squares_kernel(x_ref, sums_ref, acc):
    @pl.when(pl.program_id(0) == 0)
    def _():
        acc[...] = jnp.zeros_like(acc)

    for slot in range(4):
        add_squares(acc, slot, x_ref[:, slot * BW : (slot + 1) * BW])

    @pl.when(pl.program_id(0) == pl.num_programs(0) - 1)
    def _():
        put_sums(sums_ref, acc)


def squares(columns):
    rows, cols = columns.shape
    return pl.pallas_call(
        squares_kernel,
        grid=(rows // CHUNK,),
        in_specs=[pl.BlockSpec((CHUNK, cols), lambda i: (i, 0))],
        out_specs=pl.BlockSpec((8, 128), lambda i: (0, 0)),
        out_shape=jax.ShapeDtypeStruct((8, 128), jnp.float32),
        scratch_shapes=[pltpu.VMEM((8, 8, 128), jnp.float32)],
        compiler_params=params(),
        cost_estimate=pl.CostEstimate(
            flops=2 * rows * cols, bytes_accessed=4 * rows * cols, transcendentals=0
        ),
    )(columns)


def scaled_parts(total_rows, plan_ref, x_refs, sums_ref, high, low):
    scale = jnp.sqrt(jnp.float32(total_rows)) * lax.rsqrt(sums_ref[...] + epsilon)
    for slot in range(4):
        place = jnp.int32(0)
        for k in range(4):
            place += jnp.where(plan_ref[k] == slot, k, 0)
        for half in range(2):
            lanes = slice(half * 128, (half + 1) * 128)
            row = 2 * slot + half
            x = x_refs[slot][:, lanes] * scale[row : row + 1, :]
            h, l = split(x)
            high[place, :, lanes] = h
            low[place, :, lanes] = l


def rotate(pair, high, low, rot_high, rot_low):
    out = None
    for k in range(2):
        h, l = high[2 * pair + k], low[2 * pair + k]
        rows = slice(k * BW, (k + 1) * BW)
        rh, rl = rot_high[pair, rows, :], rot_low[pair, rows, :]
        term = dot(h, rh) + dot(l, rh) + dot(h, rl)
        out = term if out is None else out + term
    return out


def send_kernel(total_rows, plan_ref, x0, x1, x2, x3, sums_ref, rot_ref, up_ref, down_ref,
                high, low, rot_high, rot_low):
    @pl.when(pl.program_id(0) == 0)
    def _():
        for pair in range(2):
            rot_high[pair], rot_low[pair] = split(rot_ref[pair])

    scaled_parts(total_rows, plan_ref, (x0, x1, x2, x3), sums_ref, high, low)
    up_ref[...] = rotate(0, high, low, rot_high, rot_low)
    down_ref[...] = rotate(1, high, low, rot_high, rot_low)


def keep_kernel(total_rows, plan_ref, x0, x1, x2, x3, sums_ref, rot_ref, up_ref, down_ref,
                out_ref, new_sums_ref, high, low, rot_high, rot_low, acc):
    @pl.when(pl.program_id(0) == 0)
    def _():
        acc[...] = jnp.zeros_like(acc)
        for pair in range(2):
            rot_high[pair], rot_low[pair] = split(rot_ref[pair])

    scaled_parts(total_rows, plan_ref, (x0, x1, x2, x3), sums_ref, high, low)
    for pair, sent in ((0, up_ref), (1, down_ref)):
        kept = rotate(pair, high, low, rot_high, rot_low)
        out_ref[:, pair * BW : (pair + 1) * BW] = kept
        add_squares(acc, 2 * pair, kept)
        add_squares(acc, 2 * pair + 1, sent[...])

    @pl.when(pl.program_id(0) == pl.num_programs(0) - 1)
    def _():
        put_sums(new_sums_ref, acc)


def x_spec(row0, col):
    return pl.BlockSpec((CHUNK, BW), lambda i, plan: (i + row0, col))


def scratch():
    return [
        pltpu.VMEM((4, CHUNK, BW), jnp.bfloat16),
        pltpu.VMEM((4, CHUNK, BW), jnp.bfloat16),
        pltpu.VMEM((2, 2 * BW, BW), jnp.bfloat16),
        pltpu.VMEM((2, 2 * BW, BW), jnp.bfloat16),
    ]


def send_part(total_rows, rows, xs, specs, sums, rotation, plan):
    shape = jax.ShapeDtypeStruct((rows, BW), jnp.float32)
    return pl.pallas_call(
        functools.partial(send_kernel, total_rows),
        grid_spec=pltpu.PrefetchScalarGridSpec(
            num_scalar_prefetch=1,
            grid=(rows // CHUNK,),
            in_specs=specs
            + [
                pl.BlockSpec((8, 128), lambda i, plan: (0, 0)),
                pl.BlockSpec((2, 2 * BW, BW), lambda i, plan: (0, 0, 1)),
            ],
            out_specs=[pl.BlockSpec((CHUNK, BW), lambda i, plan: (i, 0))] * 2,
            scratch_shapes=scratch(),
        ),
        out_shape=[shape, shape],
        compiler_params=params(),
        cost_estimate=pl.CostEstimate(
            flops=3 * 2 * rows * 2 * BW * 2 * BW,
            bytes_accessed=4 * rows * 6 * BW,
            transcendentals=0,
        ),
    )(plan, *xs, sums, rotation)


def keep_part(total_rows, rows, out_cols, xs, specs, sums, rotation, plan, up, down):
    return pl.pallas_call(
        functools.partial(keep_kernel, total_rows),
        grid_spec=pltpu.PrefetchScalarGridSpec(
            num_scalar_prefetch=1,
            grid=(rows // CHUNK,),
            in_specs=specs
            + [
                pl.BlockSpec((8, 128), lambda i, plan: (0, 0)),
                pl.BlockSpec((2, 2 * BW, BW), lambda i, plan: (0, 0, 0)),
                pl.BlockSpec((CHUNK, BW), lambda i, plan: (i, 0)),
                pl.BlockSpec((CHUNK, BW), lambda i, plan: (i, 0)),
            ],
            out_specs=[
                pl.BlockSpec((CHUNK, 2 * BW), lambda i, plan: (i, 0)),
                pl.BlockSpec((8, 128), lambda i, plan: (0, 0)),
            ],
            scratch_shapes=scratch() + [pltpu.VMEM((8, 8, 128), jnp.float32)],
        ),
        out_shape=[
            jax.ShapeDtypeStruct((rows, out_cols), jnp.float32),
            jax.ShapeDtypeStruct((8, 128), jnp.float32),
        ],
        compiler_params=params(),
        cost_estimate=pl.CostEstimate(
            flops=3 * 2 * rows * 2 * BW * 2 * BW,
            bytes_accessed=4 * rows * 8 * BW,
            transcendentals=0,
        ),
    )(plan, *xs, sums, rotation, up, down)


def gram_kernel(total_rows, k_ref, up_ref, down_ref, gram_ref, square, cross):
    @pl.when(pl.program_id(0) == 0)
    def _():
        square[...] = jnp.zeros_like(square)
        cross[...] = jnp.zeros_like(cross)

    for pair, sent in ((0, up_ref), (1, down_ref)):
        ah, al = split(k_ref[:, pair * BW : (pair + 1) * BW])
        bh, bl = split(sent[...])
        at, bt = ah.T, bh.T
        square[pair, 0] += dot(at, ah)
        square[pair, 1] += dot(at, bh)
        square[pair, 2] += dot(bt, bh)
        cross[pair, 0] += dot(at, al)
        cross[pair, 1] += dot(at, bl)
        cross[pair, 2] += dot(bt, al)
        cross[pair, 3] += dot(bt, bl)

    @pl.when(pl.program_id(0) == pl.num_programs(0) - 1)
    def _():
        inverse = jnp.float32(1.0 / total_rows)
        for pair in range(2):
            aa = (square[pair, 0] + (cross[pair, 0] + cross[pair, 0].T)) * inverse
            ab = (square[pair, 1] + (cross[pair, 1] + cross[pair, 2].T)) * inverse
            bb = (square[pair, 2] + (cross[pair, 3] + cross[pair, 3].T)) * inverse
            gram_ref[pair, :BW, :BW] = aa
            gram_ref[pair, :BW, BW:] = ab
            gram_ref[pair, BW:, :BW] = ab.T
            gram_ref[pair, BW:, BW:] = bb


def gram(total_rows, kept, up, down):
    rows = kept.shape[0]
    return pl.pallas_call(
        functools.partial(gram_kernel, total_rows),
        grid=(rows // CHUNK,),
        in_specs=[
            pl.BlockSpec((CHUNK, 2 * BW), lambda i: (i, 0)),
            pl.BlockSpec((CHUNK, BW), lambda i: (i, 0)),
            pl.BlockSpec((CHUNK, BW), lambda i: (i, 0)),
        ],
        out_specs=pl.BlockSpec((2, 2 * BW, 2 * BW), lambda i: (0, 0, 0)),
        out_shape=jax.ShapeDtypeStruct((2, 2 * BW, 2 * BW), jnp.float32),
        scratch_shapes=[
            pltpu.VMEM((2, 3, BW, BW), jnp.float32),
            pltpu.VMEM((2, 4, BW, BW), jnp.float32),
        ],
        compiler_params=params(),
        cost_estimate=pl.CostEstimate(
            flops=2 * 2 * rows * 7 * BW * BW, bytes_accessed=4 * rows * 4 * BW, transcendentals=0
        ),
    )(kept, up, down)


def fill_kernel(_, up_ref, down_ref, out_ref):
    out_ref[:, :BW] = up_ref[...]
    out_ref[:, BW:] = down_ref[...]


def fill(out, up, down, row0):
    rows = up.shape[0]
    first = row0 // CHUNK
    return pl.pallas_call(
        fill_kernel,
        grid=(rows // CHUNK,),
        in_specs=[
            pl.BlockSpec(memory_space=pl.ANY),
            pl.BlockSpec((CHUNK, BW), lambda i: (i, 0)),
            pl.BlockSpec((CHUNK, BW), lambda i: (i, 0)),
        ],
        out_specs=pl.BlockSpec((CHUNK, 2 * BW), lambda i: (i + first, 1)),
        out_shape=jax.ShapeDtypeStruct(out.shape, out.dtype),
        input_output_aliases={0: 0},
        compiler_params=params(),
        cost_estimate=pl.CostEstimate(
            flops=0, bytes_accessed=4 * rows * 4 * BW, transcendentals=0
        ),
    )(out, up, down)


def shift(x, by):
    size = lax.axis_size("pair")
    return lax.ppermute(x, "pair", [(i, (i + by) % size) for i in range(size)])


def swap(x, bit):
    size = lax.axis_size("frame")
    return lax.ppermute(x, "frame", [(i, i ^ bit) for i in range(size)])


def all_sum(x):
    bit = 1
    while bit < lax.axis_size("frame"):
        x = x + swap(x, bit)
        bit *= 2
    return x


def scatter_sum(g):
    frames = lax.axis_size("frame")
    width = 2 * BW // frames
    me = lax.axis_index("frame")
    total = lax.dynamic_slice_in_dim(g, me * width, width, 1)
    for k in range(1, frames):
        total = total + swap(lax.dynamic_slice_in_dim(g, (me ^ k) * width, width, 1), k)
    return jnp.transpose(total, (1, 0, 2))


def local(columns, rotations, plan):
    rows = columns.shape[0]
    total_rows = rows * lax.axis_size("frame")
    part = rows // PARTS
    tile = all_sum(squares(columns))

    def x_of(step, row0, count):
        first = row0 // CHUNK
        if step == 0:
            return [columns] * 4, [x_spec(first, slot) for slot in range(4)]
        kept, ups, downs = held
        return (
            [kept, kept, ups[row0 // part], downs[row0 // part]],
            [x_spec(first, 0), x_spec(first, 1), x_spec(0, 0), x_spec(0, 0)],
        )

    held = None
    grams_list = []
    for step in range(STEPS):
        ups, downs, got_up, got_down = [], [], [], []
        for p in range(PARTS):
            xs, specs = x_of(step, p * part, part)
            up, down = send_part(total_rows, part, xs, specs, tile, rotations[step], plan[step, 0])
            ups.append(up)
            downs.append(down)
            got_up.append(shift(up, 1))
            got_down.append(shift(down, -1))
        return_up = jnp.concatenate(ups)
        return_down = jnp.concatenate(downs)
        if step == 0:
            xs, specs = x_of(step, 0, rows)
        else:
            kept, a, b = held
            xs = [kept, kept, jnp.concatenate(a), jnp.concatenate(b)]
            specs = [x_spec(0, 0), x_spec(0, 1), x_spec(0, 0), x_spec(0, 0)]
        last = step == STEPS - 1
        kept, sums = keep_part(
            total_rows, rows, (4 if last else 2) * BW, xs, specs, tile, rotations[step],
            plan[step, 0], return_up, return_down,
        )
        if not last:
            before, after = shift(sums, 1), shift(sums, -1)
            tile = all_sum(jnp.concatenate([sums[0:2], sums[4:6], before[2:4], after[6:8]]))
        grams_list.append(scatter_sum(gram(total_rows, kept, return_up, return_down)))
        held = (kept, got_up, got_down)
    out, ups, downs = held
    for p in range(PARTS):
        out = fill(out, ups[p], downs[p], p * part)
    return out, jnp.stack(grams_list)


def solution(mesh):
    in_specs = (P("frame", "pair"), P(None, "pair", None, None), P(None, "pair", None))
    out_specs = (P("frame", "pair"), P(None, "frame", "pair", None))
    return jax.shard_map(local, mesh=mesh, in_specs=in_specs, out_specs=out_specs, check_vma=False)
```

time: 564 us -> 195 us (0.35)
  the two profiles are of different devices: /device:TPU:12 before, /device:TPU:0 now
where the time goes in v1:
time: 195 us; the launch traced here: 192 us
  Pallas kernels  81.1 us (42%)
  starting transfers between devices  56.8 us (29%)
  waiting for transfers between devices  34 us (17%)
  local copies, waits for them, and re-layouts  14.3 us (7%)
  other arithmetic  5.42 us (3%)
    ppermute x20, starting transfers between devices, swap(): return lax.ppermute(x, 'frame', [(i, i ^ bit) for i in range(size)])  40.9 us
    ppermute x20, waiting for transfers between devices, swap(): return lax.ppermute(x, 'frame', [(i, i ^ bit) for i in range(size)])  31.5 us
    pallas_call x4, Pallas kernels, send_part(): pl.pallas_call(functools.partial(send_kernel, total_rows), grid_spec=pltp...  26.1 us
    pallas_call x2, Pallas kernels, keep_part(): pl.pallas_call(functools.partial(keep_kernel, total_rows), grid_spec=pltp...  23.6 us
    pallas_call x2, Pallas kernels, gram(): pl.pallas_call(functools.partial(gram_kernel, total_rows), grid=(rows //...  17.9 us
    ppermute x10, starting transfers between devices, shift(): return lax.ppermute(x, 'pair', [(i, (i + by) % size) for i in range(size)])  15.9 us
    unnamed x42, local copies, waits for them, and re-layouts  7.83 us
    pallas_call x2, Pallas kernels, fill(): pl.pallas_call(fill_kernel, grid=(rows // CHUNK,), in_specs=[pl.BlockSpec...  7.34 us
  transfers between devices with their start and end apart: 30, of which 11 were waited for; matrix products, arithmetic and copies ran while one was open for 9% of the time, Pallas kernels for 30%

profile of v1, /device:TPU:0, one launch (start us, length us, event | category | flops | bytes accessed | tf_op | source)
XLA Modules:
  0.0 192.4 jit_solution(13725583802195076769)
XLA Ops:
  0.6 6.2 %shard_map.50 = f32[8,128]{1,0:T(8,128)S(1)} custom-call(f32[2048,1024]{1,0:T(8,128)} %x3.5), custom_call_target="tpu_custom_call" | custom-call | flops 4194304 | bytes 8388608 | tf_op jit(solution)/shard_map/pallas_call | solution.py:63
  6.8 3.4 %collective-permute-start = (f32[8,128]{1,0:T(8,128)S(1)}, f32[8,128]{1,0:T(8,128)S(1)}, u32[]{:S(2)}, u32[]{:S(2)}) collective-permute-start(f32[8,128]{1,0:T(8,128)S(1)} %shard_map.50), channel_id=1, source_target_pairs={{0,16},{16,0},{32,48},{48,32},{64,80},{80,64},{96,112},{112,96},{1... | collective-permute-start | bytes 12296 | tf_op jit(solution)/shard_map/ppermute | solution.py:292
  10.2 1.8 collective-permute-done
  12.0 1.6 collective-permute-start.1
  13.6 1.8 slice_bitcast_fusion
  15.4 0.2 collective-permute-done.1
  15.6 3.1 %collective-permute-start.2 = (f32[8,128]{1,0:T(8,128)S(1)}, f32[8,128]{1,0:T(8,128)S(1)}, u32[]{:S(2)}, u32[]{:S(2)}) collective-permute-start(f32[8,128]{1,0:T(8,128)S(1)} %add.93), channel_id=1, source_target_pairs={{0,64},{16,80},{32,96},{48,112},{64,0},{80,16},{96,32},{112,48},{1... | collective-permute-start | bytes 12296 | tf_op jit(solution)/shard_map/ppermute | solution.py:292
  18.7 2.0 %collective-permute-done.2 = f32[8,128]{1,0:T(8,128)S(1)} collective-permute-done((f32[8,128]{1,0:T(8,128)S(1)}, f32[8,128]{1,0:T(8,128)S(1)}, u32[]{:S(2)}, u32[]{:S(2)}) %collective-permute-start.2) | collective-permute-done | bytes 4128 | tf_op jit(solution)/shard_map/ppermute | solution.py:292
  20.7 5.7 %shard_map.52 = (f32[1024,256]{1,0:T(8,128)S(1)}, f32[1024,256]{1,0:T(8,128)S(1)}) custom-call(s32[4]{0:T(128)S(1)} %get-tuple-element.44.plan_ref, f32[2048,1024]{1,0:T(8,128)} %x3.5, f32[2048,1024]{1,0:T(8,128)} %x3.5, f32[2048,1024]{1,0:T(8,128)} %x3.5, f32[2048,1024]{1,0:T(8,128)} %x3.5, f32[8,128]{1,0:T(8,128)S(1)} %add.94.sums_ref, ...), custom_call_target="tpu_custom_call" | custom-call | flops 1610612736 | bytes 6291456 | tf_op jit(solution)/shard_map/pallas_call | solution.py:150
  26.4 6.8 %shard_map.51 = (f32[1024,256]{1,0:T(8,128)}, f32[1024,256]{1,0:T(8,128)}) custom-call(s32[4]{0:T(128)S(1)} %get-tuple-element.44.plan_ref, f32[2048,1024]{1,0:T(8,128)} %x3.5, f32[2048,1024]{1,0:T(8,128)} %x3.5, f32[2048,1024]{1,0:T(8,128)} %x3.5, f32[2048,1024]{1,0:T(8,128)} %x3.5, f32[8,128]{1,0:T(8,128)S(1)} %add.94.sums_ref, ...), custom_call_target="tpu_custom_call" | custom-call | flops 1610612736 | bytes 6291456 | tf_op jit(solution)/shard_map/pallas_call | solution.py:150
  33.3 3.9 %collective-permute-start.5 = (f32[1024,256]{1,0:T(8,128)}, f32[1024,256]{1,0:T(8,128)}, u32[]{:S(2)}, u32[]{:S(2)}) collective-permute-start(f32[1024,256]{1,0:T(8,128)} %get-tuple-element.15), channel_id=1, source_target_pairs={{0,15},{1,0},{2,1},{3,2},{4,3},{5,4},{6,5},{7,6},{8,7},{9,8},{10,9... | collective-permute-start | bytes 3145736 | tf_op jit(solution)/shard_map/ppermute | solution.py:287
  37.1 1.7 constant_dynamic-update-slice_fusion.1
  38.8 0.1 constant_dynamic-update-slice_fusion.up_ref
  38.9 0.1 constant_dynamic-update-slice_fusion.2.down_ref
  39.0 1.3 copy-done.6
  40.3 11.7 %shard_map.53 = (f32[2048,512]{1,0:T(8,128)}, f32[8,128]{1,0:T(8,128)S(1)}) custom-call(s32[4]{0:T(128)S(1)} %get-tuple-element.44.plan_ref, f32[2048,1024]{1,0:T(8,128)} %x3.5, f32[2048,1024]{1,0:T(8,128)} %x3.5, f32[2048,1024]{1,0:T(8,128)} %x3.5, f32[2048,1024]{1,0:T(8,128)} %x3.5, f32[8,128]{1,0:T(8,128)S(1)} %add.94.sums_ref, ...), custom_call_target="tpu_custom_call" | custom-call | flops 3221225472 | bytes 16777216 | tf_op jit(solution)/shard_map/pallas_call | solution.py:174
  52.0 3.9 %collective-permute-start.8 = (f32[8,128]{1,0:T(8,128)S(1)}, f32[8,128]{1,0:T(8,128)S(1)}, u32[]{:S(2)}, u32[]{:S(2)}) collective-permute-start(f32[8,128]{1,0:T(8,128)S(1)} %get-tuple-element.18), channel_id=1, source_target_pairs={{0,15},{1,0},{2,1},{3,2},{4,3},{5,4},{6,5},{7,6},{8,7},{9,8},{10,9... | collective-permute-start | bytes 12296 | tf_op jit(solution)/shard_map/ppermute | solution.py:287
  55.9 1.3 collective-permute-done.7
  57.2 3.4 %collective-permute-start.9 = (f32[8,128]{1,0:T(8,128)S(1)}, f32[8,128]{1,0:T(8,128)S(1)}, u32[]{:S(2)}, u32[]{:S(2)}) collective-permute-start(f32[8,128]{1,0:T(8,128)S(1)} %pad_maximum_fusion.3), channel_id=1, source_target_pairs={{0,16},{16,0},{32,48},{48,32},{64,80},{80,64},{96,112},{112,96},{1... | collective-permute-start | bytes 12296 | tf_op jit(solution)/shard_map/ppermute | solution.py:292
  60.6 3.9 %collective-permute-start.6 = (f32[1024,256]{1,0:T(8,128)}, f32[1024,256]{1,0:T(8,128)S(1)}, u32[]{:S(2)}, u32[]{:S(2)}) collective-permute-start(f32[1024,256]{1,0:T(8,128)} %copy-done.3), channel_id=1, source_target_pairs={{0,15},{1,0},{2,1},{3,2},{4,3},{5,4},{6,5},{7,6},{8,7},{9,8},{10,9... | collective-permute-start | bytes 3145736 | tf_op jit(solution)/shard_map/ppermute | solution.py:287
  64.4 1.6 collective-permute-start.10
  66.0 8.9 %shard_map.59 = f32[2,512,512]{2,1,0:T(8,128)S(1)} custom-call(f32[2048,512]{1,0:T(8,128)} %get-tuple-element.17.x0.x1.k_ref, f32[2048,256]{1,0:T(8,128)S(1)} %constant_dynamic-update-slice_fusion.up_ref, f32[2048,256]{1,0:T(8,128)} %copy-done.6), custom_call_target="tpu_custom_call" | custom-call | flops 3758096384 | bytes 8388608 | tf_op jit(solution)/shard_map/pallas_call | solution.py:238
  75.0 2.8 %collective-permute-start.11 = (f32[8,128]{1,0:T(8,128)S(1)}, f32[8,128]{1,0:T(8,128)S(1)}, u32[]{:S(2)}, u32[]{:S(2)}) collective-permute-start(f32[8,128]{1,0:T(8,128)S(1)} %add.96), channel_id=1, source_target_pairs={{0,64},{16,80},{32,96},{48,112},{64,0},{80,16},{96,32},{112,48},{1... | collective-permute-start | bytes 12296 | tf_op jit(solution)/shard_map/ppermute | solution.py:292
  77.8 0.2 constant_dynamic-slice_fusion.13
  78.0 2.2 %collective-permute-done.11 = f32[8,128]{1,0:T(8,128)S(1)} collective-permute-done((f32[8,128]{1,0:T(8,128)S(1)}, f32[8,128]{1,0:T(8,128)S(1)}, u32[]{:S(2)}, u32[]{:S(2)}) %collective-permute-start.11) | collective-permute-done | bytes 4128 | tf_op jit(solution)/shard_map/ppermute | solution.py:292
  80.2 1.3 collective-permute-start.16
  81.5 3.9 %collective-permute-start.22 = (f32[2,64,512]{2,1,0:T(8,128)S(1)}, f32[2,64,512]{2,1,0:T(8,128)S(1)}, u32[]{:S(2)}, u32[]{:S(2)}) collective-permute-start(f32[2,64,512]{2,1,0:T(8,128)S(1)} %get-tuple-element.29), channel_id=1, source_target_pairs={{0,112},{16,96},{32,80},{48,64},{64,48},{80,32},{96,16},{112,0},{1... | collective-permute-start | bytes 786440 | tf_op jit(solution)/shard_map/ppermute | solution.py:292
  85.4 1.1 collective-permute-start.21
  86.5 7.0 %shard_map.54 = (f32[1024,256]{1,0:T(8,128)}, f32[1024,256]{1,0:T(8,128)}) custom-call(s32[4]{0:T(128)S(1)} %get-tuple-element.45.plan_ref, f32[2048,512]{1,0:T(8,128)} %get-tuple-element.17.x0.x1.k_ref, f32[2048,512]{1,0:T(8,128)} %get-tuple-element.17.x0.x1.k_ref, f32[1024,256]{1,0:T(8,128)S(1)} %collective-permute-done.3.x2, ...), custom_call_target="tpu_custom_call" | custom-call | flops 1610612736 | bytes 6291456 | tf_op jit(solution)/shard_map/pallas_call | solution.py:150
  93.5 1.3 constant_dynamic-update-slice_fusion.5
  94.7 1.3 constant_dynamic-update-slice_fusion.7
  96.1 2.3 %collective-permute-start.20 = (f32[2,64,512]{2,1,0:T(8,128)S(1)}, f32[2,64,512]{2,1,0:T(8,128)S(1)}, u32[]{:S(2)}, u32[]{:S(2)}) collective-permute-start(f32[2,64,512]{2,1,0:T(8,128)S(1)} %get-tuple-element.31), channel_id=1, source_target_pairs={{0,80},{16,64},{32,112},{48,96},{64,16},{80,0},{96,48},{112,32},{1... | collective-permute-start | bytes 786440 | tf_op jit(solution)/shard_map/ppermute | solution.py:292
  98.4 2.0 %collective-permute-start.19 = (f32[2,64,512]{2,1,0:T(8,128)S(1)}, f32[2,64,512]{2,1,0:T(8,128)S(1)}, u32[]{:S(2)}, u32[]{:S(2)}) collective-permute-start(f32[2,64,512]{2,1,0:T(8,128)S(1)} %get-tuple-element.32), channel_id=1, source_target_pairs={{0,64},{16,80},{32,96},{48,112},{64,0},{80,16},{96,32},{112,48},{1... | collective-permute-start | bytes 786440 | tf_op jit(solution)/shard_map/ppermute | solution.py:292
  100.4 6.7 %shard_map.55 = (f32[1024,256]{1,0:T(8,128)}, f32[1024,256]{1,0:T(8,128)}) custom-call(s32[4]{0:T(128)S(1)} %get-tuple-element.45.plan_ref, f32[2048,512]{1,0:T(8,128)} %get-tuple-element.17.x0.x1.k_ref, f32[2048,512]{1,0:T(8,128)} %get-tuple-element.17.x0.x1.k_ref, f32[1024,256]{1,0:T(8,128)S(1)} %collective-permute-done.4.x2, ...), custom_call_target="tpu_custom_call" | custom-call | flops 1610612736 | bytes 6291456 | tf_op jit(solution)/shard_map/pallas_call | solution.py:150
  107.0 1.3 constant_dynamic-update-slice_fusion.4.up_ref
  108.3 2.1 %constant_dynamic-update-slice_fusion.6.down_ref = f32[2048,256]{1,0:T(8,128)S(1)} fusion(f32[2048,256]{1,0:T(8,128)S(1)} %constant_dynamic-update-slice_fusion.7, f32[1024,256]{1,0:T(8,128)} %get-tuple-element.22), kind=kLoop, calls=%fused_computation.13 | loop fusion | bytes 2097152 | tf_op jit(solution)/shard_map/concatenate | solution.py:341
  110.4 2.1 %pad_maximum_fusion.1.x3 = f32[2048,256]{1,0:T(8,128)S(1)} fusion(f32[1024,256]{1,0:T(8,128)S(1)} %collective-permute-done.6.x3, f32[1024,256]{1,0:T(8,128)} %collective-permute-done.5.x3), kind=kLoop, calls=%fused_computation.1 | loop fusion | flops 524288 | bytes 4194304 | tf_op jit(solution)/shard_map/concatenate | solution.py:346
  112.5 0.1 pad_maximum_fusion.x2
  112.7 11.8 %shard_map.56 = (f32[2048,1024]{1,0:T(8,128)}, f32[8,128]{1,0:T(8,128)}) custom-call(s32[4]{0:T(128)S(1)} %get-tuple-element.45.plan_ref, f32[2048,512]{1,0:T(8,128)} %get-tuple-element.17.x0.x1.k_ref, f32[2048,512]{1,0:T(8,128)} %get-tuple-element.17.x0.x1.k_ref, f32[2048,256]{1,0:T(8,128)S(1)} %pad_maximum_fusion.x2, ...), custom_call_target="tpu_custom_call" | custom-call | flops 3221225472 | bytes 16777216 | tf_op jit(solution)/shard_map/pallas_call | solution.py:174
  124.5 1.2 collective-permute-start.18
  125.8 8.9 %shard_map.60 = f32[2,512,512]{2,1,0:T(8,128)S(1)} custom-call(f32[2048,1024]{1,0:T(8,128)} %get-tuple-element.23._.k_ref, f32[2048,256]{1,0:T(8,128)S(1)} %copy-done.1, f32[2048,256]{1,0:T(8,128)} %copy-done.5), custom_call_target="tpu_custom_call" | custom-call | flops 3758096384 | bytes 8388608 | tf_op jit(solution)/shard_map/pallas_call | solution.py:238
  134.7 2.6 %collective-permute-start.17 = (f32[2,64,512]{2,1,0:T(8,128)S(1)}, f32[2,64,512]{2,1,0:T(8,128)S(1)}, u32[]{:S(2)}, u32[]{:S(2)}) collective-permute-start(f32[2,64,512]{2,1,0:T(8,128)S(1)} %get-tuple-element.34), channel_id=1, source_target_pairs={{0,32},{16,48},{32,0},{48,16},{64,96},{80,112},{96,64},{112,80},{1... | collective-permute-start | bytes 786440 | tf_op jit(solution)/shard_map/ppermute | solution.py:292
  137.4 1.0 constant_dynamic-slice_fusion.6
  138.4 1.3 collective-permute-start.23
  139.6 3.8 %collective-permute-start.29 = (f32[2,64,512]{2,1,0:T(8,128)S(1)}, f32[2,64,512]{2,1,0:T(8,128)S(1)}, u32[]{:S(2)}, u32[]{:S(2)}) collective-permute-start(f32[2,64,512]{2,1,0:T(8,128)S(1)} %get-tuple-element.36), channel_id=1, source_target_pairs={{0,112},{16,96},{32,80},{48,64},{64,48},{80,32},{96,16},{112,0},{1... | collective-permute-start | bytes 786440 | tf_op jit(solution)/shard_map/ppermute | solution.py:292
  143.5 1.1 collective-permute-start.28
  144.6 1.1 collective-permute-start.27
  145.7 3.2 %collective-permute-start.26 = (f32[2,64,512]{2,1,0:T(8,128)S(1)}, f32[2,64,512]{2,1,0:T(8,128)}, u32[]{:S(2)}, u32[]{:S(2)}) collective-permute-start(f32[2,64,512]{2,1,0:T(8,128)S(1)} %get-tuple-element.39), channel_id=1, source_target_pairs={{0,64},{16,80},{32,96},{48,112},{64,0},{80,16},{96,32},{112,48},{1... | collective-permute-start | bytes 786440 | tf_op jit(solution)/shard_map/ppermute | solution.py:292
  148.8 0.3 collective-permute-done.23
  149.2 9.5 %collective-permute-done.29 = f32[2,64,512]{2,1,0:T(8,128)S(1)} collective-permute-done((f32[2,64,512]{2,1,0:T(8,128)S(1)}, f32[2,64,512]{2,1,0:T(8,128)S(1)}, u32[]{:S(2)}, u32[]{:S(2)}) %collective-permute-start.29) | collective-permute-done | bytes 262176 | tf_op jit(solution)/shard_map/ppermute | solution.py:292
  158.7 0.5 collective-permute-start.13
  159.1 0.3 copy-done.14
  159.4 1.5 collective-permute-done.28
  160.9 0.7 copy-done.16
  161.6 3.9 %collective-permute-start.15 = (f32[1024,256]{1,0:T(8,128)}, f32[1024,256]{1,0:T(8,128)}, u32[]{:S(2)}, u32[]{:S(2)}) collective-permute-start(f32[1024,256]{1,0:T(8,128)} %get-tuple-element.22), channel_id=1, source_target_pairs={{0,15},{1,0},{2,1},{3,2},{4,3},{5,4},{6,5},{7,6},{8,7},{9,8},{10,9... | collective-permute-start | bytes 3145736 | tf_op jit(solution)/shard_map/ppermute | solution.py:287
  165.5 0.2 collective-permute-start.25
  165.7 9.0 %collective-permute-done.25 = f32[2,64,512]{2,1,0:T(8,128)} collective-permute-done((f32[2,64,512]{2,1,0:T(8,128)}, f32[2,64,512]{2,1,0:T(8,128)}, u32[]{:S(2)}, u32[]{:S(2)}) %collective-permute-start.25) | collective-permute-done | bytes 262176 | tf_op jit(solution)/shard_map/ppermute | solution.py:292
  174.7 1.7 add_bitcast_fusion.1
  176.3 4.9 %collective-permute-done.24 = f32[2,64,512]{2,1,0:T(8,128)S(1)} collective-permute-done((f32[2,64,512]{2,1,0:T(8,128)}, f32[2,64,512]{2,1,0:T(8,128)S(1)}, u32[]{:S(2)}, u32[]{:S(2)}) %collective-permute-start.24) | collective-permute-done | bytes 262176 | tf_op jit(solution)/shard_map/ppermute | solution.py:292
  181.3 1.4 add_bitcast_fusion
  182.7 1.2 copy.7
  183.9 3.6 %shard_map.57._ = f32[2048,1024]{1,0:T(8,128)} custom-call(f32[2048,1024]{1,0:T(8,128)} %get-tuple-element.23._.k_ref, f32[1024,256]{1,0:T(8,128)S(1)} %collective-permute-done.12.up_ref, f32[1024,256]{1,0:T(8,128)} %collective-permute-done.13.down_ref), custom_call_target="tpu_custom_call", output_to_operand_aliasing={{}: (0, {})} | custom-call | bytes 4194304 | tf_op jit(solution)/shard_map/pallas_call | solution.py:267
  187.5 1.1 collective-permute-done.15.down_ref
  188.6 3.8 %shard_map.58 = f32[2048,1024]{1,0:T(8,128)} custom-call(f32[2048,1024]{1,0:T(8,128)} %shard_map.57._, f32[1024,256]{1,0:T(8,128)} %collective-permute-done.14.up_ref, f32[1024,256]{1,0:T(8,128)} %collective-permute-done.15.down_ref), custom_call_target="tpu_custom_call", output_to_operand_aliasing={{}: (0, {})} | custom-call | bytes 4194304 | tf_op jit(solution)/shard_map/pallas_call | solution.py:267
  (72 shorter events, 0.3 us)
Async XLA Ops:
  0.6 12.9 %copy-start.7 = (f32[2,2,512,512]{3,2,1,0:T(8,128)S(1)}, f32[2,2,512,512]{3,2,1,0:T(8,128)}, u32[]{:S(2)}) copy-start(f32[2,2,512,512]{3,2,1,0:T(8,128)} %param.4) | copy-start | bytes 12582916
  6.8 5.2 %collective-permute-start = (f32[8,128]{1,0:T(8,128)S(1)}, f32[8,128]{1,0:T(8,128)S(1)}, u32[]{:S(2)}, u32[]{:S(2)}) collective-permute-start(f32[8,128]{1,0:T(8,128)S(1)} %shard_map.50), channel_id=1, source_target_pairs={{0,16},{16,0},{32,48},{48,32},{64,80},{80,64},{96,112},{112,96},{1... | collective-permute-start | bytes 12296 | tf_op jit(solution)/shard_map/ppermute | solution.py:292
  12.0 6.7 %copy-start.18 = (s32[2,1,4]{2,1,0:T(1,128)S(1)}, s32[2,1,4]{2,1,0:T(1,128)}, u32[]{:S(2)}) copy-start(s32[2,1,4]{2,1,0:T(1,128)} %param.5) | copy-start | bytes 100
  12.0 3.6 %collective-permute-start.1 = (f32[8,128]{1,0:T(8,128)S(1)}, f32[8,128]{1,0:T(8,128)S(1)}, u32[]{:S(2)}, u32[]{:S(2)}) collective-permute-start(f32[8,128]{1,0:T(8,128)S(1)} %add.92), channel_id=1, source_target_pairs={{0,32},{16,48},{32,0},{48,16},{64,96},{80,112},{96,64},{112,80},{1... | collective-permute-start | bytes 12296 | tf_op jit(solution)/shard_map/ppermute | solution.py:292
  15.6 5.1 %collective-permute-start.2 = (f32[8,128]{1,0:T(8,128)S(1)}, f32[8,128]{1,0:T(8,128)S(1)}, u32[]{:S(2)}, u32[]{:S(2)}) collective-permute-start(f32[8,128]{1,0:T(8,128)S(1)} %add.93), channel_id=1, source_target_pairs={{0,64},{16,80},{32,96},{48,112},{64,0},{80,16},{96,32},{112,48},{1... | collective-permute-start | bytes 12296 | tf_op jit(solution)/shard_map/ppermute | solution.py:292
  26.4 12.4 %copy-start.4 = (f32[1024,256]{1,0:T(8,128)}, f32[1024,256]{1,0:T(8,128)S(1)}, u32[]{:S(2)}) copy-start(f32[1024,256]{1,0:T(8,128)S(1)} %get-tuple-element.14) | copy-start | bytes 3145732
  26.4 12.4 %copy-start.3 = (f32[1024,256]{1,0:T(8,128)}, f32[1024,256]{1,0:T(8,128)S(1)}, u32[]{:S(2)}) copy-start(f32[1024,256]{1,0:T(8,128)S(1)} %get-tuple-element.16) | copy-start | bytes 3145732
  33.3 48.2 %collective-permute-start.3 = (f32[1024,256]{1,0:T(8,128)}, f32[1024,256]{1,0:T(8,128)S(1)}, u32[]{:S(2)}, u32[]{:S(2)}) collective-permute-start(f32[1024,256]{1,0:T(8,128)} %get-tuple-element.13), channel_id=1, source_target_pairs={{0,1},{1,2},{2,3},{3,4},{4,5},{5,6},{6,7},{7,8},{8,9},{9,10},{10,1... | collective-permute-start | bytes 3145736 | tf_op jit(solution)/shard_map/ppermute | solution.py:287
  33.3 52.1 %collective-permute-start.5 = (f32[1024,256]{1,0:T(8,128)}, f32[1024,256]{1,0:T(8,128)}, u32[]{:S(2)}, u32[]{:S(2)}) collective-permute-start(f32[1024,256]{1,0:T(8,128)} %get-tuple-element.15), channel_id=1, source_target_pairs={{0,15},{1,0},{2,1},{3,2},{4,3},{5,4},{6,5},{7,6},{8,7},{9,8},{10,9... | collective-permute-start | bytes 3145736 | tf_op jit(solution)/shard_map/ppermute | solution.py:287
  39.0 1.3 copy-start.6
  52.0 5.1 %collective-permute-start.7 = (f32[8,128]{1,0:T(8,128)S(1)}, f32[8,128]{1,0:T(8,128)S(1)}, u32[]{:S(2)}, u32[]{:S(2)}) collective-permute-start(f32[8,128]{1,0:T(8,128)S(1)} %get-tuple-element.18), channel_id=1, source_target_pairs={{0,1},{1,2},{2,3},{3,4},{4,5},{5,6},{6,7},{7,8},{8,9},{9,10},{10,1... | collective-permute-start | bytes 12296 | tf_op jit(solution)/shard_map/ppermute | solution.py:287
  52.0 5.2 %collective-permute-start.8 = (f32[8,128]{1,0:T(8,128)S(1)}, f32[8,128]{1,0:T(8,128)S(1)}, u32[]{:S(2)}, u32[]{:S(2)}) collective-permute-start(f32[8,128]{1,0:T(8,128)S(1)} %get-tuple-element.18), channel_id=1, source_target_pairs={{0,15},{1,0},{2,1},{3,2},{4,3},{5,4},{6,5},{7,6},{8,7},{9,8},{10,9... | collective-permute-start | bytes 12296 | tf_op jit(solution)/shard_map/ppermute | solution.py:287
  57.2 7.2 %collective-permute-start.9 = (f32[8,128]{1,0:T(8,128)S(1)}, f32[8,128]{1,0:T(8,128)S(1)}, u32[]{:S(2)}, u32[]{:S(2)}) collective-permute-start(f32[8,128]{1,0:T(8,128)S(1)} %pad_maximum_fusion.3), channel_id=1, source_target_pairs={{0,16},{16,0},{32,48},{48,32},{64,80},{80,64},{96,112},{112,96},{1... | collective-permute-start | bytes 12296 | tf_op jit(solution)/shard_map/ppermute | solution.py:292
  60.6 35.5 %collective-permute-start.4 = (f32[1024,256]{1,0:T(8,128)}, f32[1024,256]{1,0:T(8,128)S(1)}, u32[]{:S(2)}, u32[]{:S(2)}) collective-permute-start(f32[1024,256]{1,0:T(8,128)} %copy-done.4), channel_id=1, source_target_pairs={{0,1},{1,2},{2,3},{3,4},{4,5},{5,6},{6,7},{7,8},{8,9},{9,10},{10,1... | collective-permute-start | bytes 3145736 | tf_op jit(solution)/shard_map/ppermute | solution.py:287
  60.6 37.8 %collective-permute-start.6 = (f32[1024,256]{1,0:T(8,128)}, f32[1024,256]{1,0:T(8,128)S(1)}, u32[]{:S(2)}, u32[]{:S(2)}) collective-permute-start(f32[1024,256]{1,0:T(8,128)} %copy-done.3), channel_id=1, source_target_pairs={{0,15},{1,0},{2,1},{3,2},{4,3},{5,4},{6,5},{7,6},{8,7},{9,8},{10,9... | collective-permute-start | bytes 3145736 | tf_op jit(solution)/shard_map/ppermute | solution.py:287
  64.4 10.5 %collective-permute-start.10 = (f32[8,128]{1,0:T(8,128)S(1)}, f32[8,128]{1,0:T(8,128)S(1)}, u32[]{:S(2)}, u32[]{:S(2)}) collective-permute-start(f32[8,128]{1,0:T(8,128)S(1)} %fusion), channel_id=1, source_target_pairs={{0,32},{16,48},{32,0},{48,16},{64,96},{80,112},{96,64},{112,80},{1... | collective-permute-start | bytes 12296 | tf_op jit(solution)/shard_map/ppermute | solution.py:292
  75.0 6.5 %copy-start.2 = (f32[2,512,512]{2,1,0:T(8,128)}, f32[2,512,512]{2,1,0:T(8,128)S(1)}, u32[]{:S(2)}) copy-start(f32[2,512,512]{2,1,0:T(8,128)S(1)} %shard_map.59) | copy-start | bytes 6291460
  75.0 5.2 %collective-permute-start.11 = (f32[8,128]{1,0:T(8,128)S(1)}, f32[8,128]{1,0:T(8,128)S(1)}, u32[]{:S(2)}, u32[]{:S(2)}) collective-permute-start(f32[8,128]{1,0:T(8,128)S(1)} %add.96), channel_id=1, source_target_pairs={{0,64},{16,80},{32,96},{48,112},{64,0},{80,16},{96,32},{112,48},{1... | collective-permute-start | bytes 12296 | tf_op jit(solution)/shard_map/ppermute | solution.py:292
  80.2 44.3 %collective-permute-start.16 = (f32[2,64,512]{2,1,0:T(8,128)S(1)}, f32[2,64,512]{2,1,0:T(8,128)S(1)}, u32[]{:S(2)}, u32[]{:S(2)}) collective-permute-start(f32[2,64,512]{2,1,0:T(8,128)S(1)} %get-tuple-element.28), channel_id=1, source_target_pairs={{0,16},{16,0},{32,48},{48,32},{64,80},{80,64},{96,112},{112,96},{1... | collective-permute-start | bytes 786440 | tf_op jit(solution)/shard_map/ppermute | solution.py:292
  81.5 53.3 %collective-permute-start.22 = (f32[2,64,512]{2,1,0:T(8,128)S(1)}, f32[2,64,512]{2,1,0:T(8,128)S(1)}, u32[]{:S(2)}, u32[]{:S(2)}) collective-permute-start(f32[2,64,512]{2,1,0:T(8,128)S(1)} %get-tuple-element.29), channel_id=1, source_target_pairs={{0,112},{16,96},{32,80},{48,64},{64,48},{80,32},{96,16},{112,0},{1... | collective-permute-start | bytes 786440 | tf_op jit(solution)/shard_map/ppermute | solution.py:292
  85.4 53.0 %collective-permute-start.21 = (f32[2,64,512]{2,1,0:T(8,128)S(1)}, f32[2,64,512]{2,1,0:T(8,128)S(1)}, u32[]{:S(2)}, u32[]{:S(2)}) collective-permute-start(f32[2,64,512]{2,1,0:T(8,128)S(1)} %get-tuple-element.30), channel_id=1, source_target_pairs={{0,96},{16,112},{32,64},{48,80},{64,32},{80,48},{96,0},{112,16},{1... | collective-permute-start | bytes 786440 | tf_op jit(solution)/shard_map/ppermute | solution.py:292
  96.1 43.6 %collective-permute-start.20 = (f32[2,64,512]{2,1,0:T(8,128)S(1)}, f32[2,64,512]{2,1,0:T(8,128)S(1)}, u32[]{:S(2)}, u32[]{:S(2)}) collective-permute-start(f32[2,64,512]{2,1,0:T(8,128)S(1)} %get-tuple-element.31), channel_id=1, source_target_pairs={{0,80},{16,64},{32,112},{48,96},{64,16},{80,0},{96,48},{112,32},{1... | collective-permute-start | bytes 786440 | tf_op jit(solution)/shard_map/ppermute | solution.py:292
  98.4 45.1 %collective-permute-start.19 = (f32[2,64,512]{2,1,0:T(8,128)S(1)}, f32[2,64,512]{2,1,0:T(8,128)S(1)}, u32[]{:S(2)}, u32[]{:S(2)}) collective-permute-start(f32[2,64,512]{2,1,0:T(8,128)S(1)} %get-tuple-element.32), channel_id=1, source_target_pairs={{0,64},{16,80},{32,96},{48,112},{64,0},{80,16},{96,32},{112,48},{1... | collective-permute-start | bytes 786440 | tf_op jit(solution)/shard_map/ppermute | solution.py:292
  108.3 4.2 %copy-start = (f32[2048,256]{1,0:T(8,128)}, f32[2048,256]{1,0:T(8,128)S(1)}, u32[]{:S(2)}) copy-start(f32[2048,256]{1,0:T(8,128)S(1)} %constant_dynamic-update-slice_fusion.4.up_ref) | copy-start | bytes 6291460
  110.4 2.1 %copy-start.5 = (f32[2048,256]{1,0:T(8,128)}, f32[2048,256]{1,0:T(8,128)S(1)}, u32[]{:S(2)}) copy-start(f32[2048,256]{1,0:T(8,128)S(1)} %constant_dynamic-update-slice_fusion.6.down_ref) | copy-start | bytes 6291460
  112.7 13.1 %copy-start.1 = (f32[2048,256]{1,0:T(8,128)S(1)}, f32[2048,256]{1,0:T(8,128)}, u32[]{:S(2)}) copy-start(f32[2048,256]{1,0:T(8,128)} %copy-done) | copy-start | bytes 6291460
  124.5 20.1 %collective-permute-start.18 = (f32[2,64,512]{2,1,0:T(8,128)S(1)}, f32[2,64,512]{2,1,0:T(8,128)S(1)}, u32[]{:S(2)}, u32[]{:S(2)}) collective-permute-start(f32[2,64,512]{2,1,0:T(8,128)S(1)} %get-tuple-element.33), channel_id=1, source_target_pairs={{0,48},{16,32},{32,16},{48,0},{64,112},{80,96},{96,80},{112,64},{1... | collective-permute-start | bytes 786440 | tf_op jit(solution)/shard_map/ppermute | solution.py:292
  134.7 14.1 %copy-start.8 = (f32[2,64,512]{2,1,0:T(8,128)}, f32[2,64,512]{2,1,0:T(8,128)S(1)}, u32[]{:S(2)}) copy-start(f32[2,64,512]{2,1,0:T(8,128)S(1)} %collective-permute-done.22) | copy-start | bytes 786436
  134.7 10.9 %collective-permute-start.17 = (f32[2,64,512]{2,1,0:T(8,128)S(1)}, f32[2,64,512]{2,1,0:T(8,128)S(1)}, u32[]{:S(2)}, u32[]{:S(2)}) collective-permute-start(f32[2,64,512]{2,1,0:T(8,128)S(1)} %get-tuple-element.34), channel_id=1, source_target_pairs={{0,32},{16,48},{32,0},{48,16},{64,96},{80,112},{96,64},{112,80},{1... | collective-permute-start | bytes 786440 | tf_op jit(solution)/shard_map/ppermute | solution.py:292
  138.4 10.8 %copy-start.9 = (f32[2,64,512]{2,1,0:T(8,128)}, f32[2,64,512]{2,1,0:T(8,128)S(1)}, u32[]{:S(2)}) copy-start(f32[2,64,512]{2,1,0:T(8,128)S(1)} %collective-permute-done.21) | copy-start | bytes 786436
  138.4 10.8 %collective-permute-start.23 = (f32[2,64,512]{2,1,0:T(8,128)S(1)}, f32[2,64,512]{2,1,0:T(8,128)}, u32[]{:S(2)}, u32[]{:S(2)}) collective-permute-start(f32[2,64,512]{2,1,0:T(8,128)S(1)} %get-tuple-element.35), channel_id=1, source_target_pairs={{0,16},{16,0},{32,48},{48,32},{64,80},{80,64},{96,112},{112,96},{1... | collective-permute-start | bytes 786440 | tf_op jit(solution)/shard_map/ppermute | solution.py:292
  139.6 9.5 %copy-start.10 = (f32[2,64,512]{2,1,0:T(8,128)}, f32[2,64,512]{2,1,0:T(8,128)S(1)}, u32[]{:S(2)}) copy-start(f32[2,64,512]{2,1,0:T(8,128)S(1)} %collective-permute-done.20) | copy-start | bytes 786436
  139.6 19.0 %collective-permute-start.29 = (f32[2,64,512]{2,1,0:T(8,128)S(1)}, f32[2,64,512]{2,1,0:T(8,128)S(1)}, u32[]{:S(2)}, u32[]{:S(2)}) collective-permute-start(f32[2,64,512]{2,1,0:T(8,128)S(1)} %get-tuple-element.36), channel_id=1, source_target_pairs={{0,112},{16,96},{32,80},{48,64},{64,48},{80,32},{96,16},{112,0},{1... | collective-permute-start | bytes 786440 | tf_op jit(solution)/shard_map/ppermute | solution.py:292
  143.5 15.2 %copy-start.11 = (f32[2,64,512]{2,1,0:T(8,128)}, f32[2,64,512]{2,1,0:T(8,128)S(1)}, u32[]{:S(2)}) copy-start(f32[2,64,512]{2,1,0:T(8,128)S(1)} %collective-permute-done.19) | copy-start | bytes 786436
  143.5 17.4 %collective-permute-start.28 = (f32[2,64,512]{2,1,0:T(8,128)S(1)}, f32[2,64,512]{2,1,0:T(8,128)S(1)}, u32[]{:S(2)}, u32[]{:S(2)}) collective-permute-start(f32[2,64,512]{2,1,0:T(8,128)S(1)} %get-tuple-element.37), channel_id=1, source_target_pairs={{0,96},{16,112},{32,64},{48,80},{64,32},{80,48},{96,0},{112,16},{1... | collective-permute-start | bytes 786440 | tf_op jit(solution)/shard_map/ppermute | solution.py:292
  144.6 4.2 %copy-start.12 = (f32[2,64,512]{2,1,0:T(8,128)}, f32[2,64,512]{2,1,0:T(8,128)S(1)}, u32[]{:S(2)}) copy-start(f32[2,64,512]{2,1,0:T(8,128)S(1)} %collective-permute-done.18) | copy-start | bytes 786436
  144.6 17.0 %collective-permute-start.27 = (f32[2,64,512]{2,1,0:T(8,128)S(1)}, f32[2,64,512]{2,1,0:T(8,128)}, u32[]{:S(2)}, u32[]{:S(2)}) collective-permute-start(f32[2,64,512]{2,1,0:T(8,128)S(1)} %get-tuple-element.38), channel_id=1, source_target_pairs={{0,80},{16,64},{32,112},{48,96},{64,16},{80,0},{96,48},{112,32},{1... | collective-permute-start | bytes 786440 | tf_op jit(solution)/shard_map/ppermute | solution.py:292
  145.7 3.2 %copy-start.13 = (f32[2,64,512]{2,1,0:T(8,128)}, f32[2,64,512]{2,1,0:T(8,128)S(1)}, u32[]{:S(2)}) copy-start(f32[2,64,512]{2,1,0:T(8,128)S(1)} %collective-permute-done.17) | copy-start | bytes 786436
  145.7 19.8 %collective-permute-start.26 = (f32[2,64,512]{2,1,0:T(8,128)S(1)}, f32[2,64,512]{2,1,0:T(8,128)}, u32[]{:S(2)}, u32[]{:S(2)}) collective-permute-start(f32[2,64,512]{2,1,0:T(8,128)S(1)} %get-tuple-element.39), channel_id=1, source_target_pairs={{0,64},{16,80},{32,96},{48,112},{64,0},{80,16},{96,32},{112,48},{1... | collective-permute-start | bytes 786440 | tf_op jit(solution)/shard_map/ppermute | solution.py:292
  149.2 34.8 %collective-permute-start.12 = (f32[1024,256]{1,0:T(8,128)}, f32[1024,256]{1,0:T(8,128)S(1)}, u32[]{:S(2)}, u32[]{:S(2)}) collective-permute-start(f32[1024,256]{1,0:T(8,128)} %get-tuple-element.19), channel_id=1, source_target_pairs={{0,1},{1,2},{2,3},{3,4},{4,5},{5,6},{6,7},{7,8},{8,9},{9,10},{10,1... | collective-permute-start | bytes 3145736 | tf_op jit(solution)/shard_map/ppermute | solution.py:287
  158.7 0.7 copy-start.14
  158.7 25.3 %collective-permute-start.13 = (f32[1024,256]{1,0:T(8,128)}, f32[1024,256]{1,0:T(8,128)}, u32[]{:S(2)}, u32[]{:S(2)}) collective-permute-start(f32[1024,256]{1,0:T(8,128)} %get-tuple-element.21), channel_id=1, source_target_pairs={{0,15},{1,0},{2,1},{3,2},{4,3},{5,4},{6,5},{7,6},{8,7},{9,8},{10,9... | collective-permute-start | bytes 3145736 | tf_op jit(solution)/shard_map/ppermute | solution.py:287
  160.9 0.7 copy-start.16
  161.6 25.9 %collective-permute-start.14 = (f32[1024,256]{1,0:T(8,128)}, f32[1024,256]{1,0:T(8,128)}, u32[]{:S(2)}, u32[]{:S(2)}) collective-permute-start(f32[1024,256]{1,0:T(8,128)} %get-tuple-element.20), channel_id=1, source_target_pairs={{0,1},{1,2},{2,3},{3,4},{4,5},{5,6},{6,7},{7,8},{8,9},{9,10},{10,1... | collective-permute-start | bytes 3145736 | tf_op jit(solution)/shard_map/ppermute | solution.py:287
  161.6 27.0 %collective-permute-start.15 = (f32[1024,256]{1,0:T(8,128)}, f32[1024,256]{1,0:T(8,128)}, u32[]{:S(2)}, u32[]{:S(2)}) collective-permute-start(f32[1024,256]{1,0:T(8,128)} %get-tuple-element.22), channel_id=1, source_target_pairs={{0,15},{1,0},{2,1},{3,2},{4,3},{5,4},{6,5},{7,6},{8,7},{9,8},{10,9... | collective-permute-start | bytes 3145736 | tf_op jit(solution)/shard_map/ppermute | solution.py:287
  165.5 9.2 %collective-permute-start.25 = (f32[2,64,512]{2,1,0:T(8,128)}, f32[2,64,512]{2,1,0:T(8,128)}, u32[]{:S(2)}, u32[]{:S(2)}) collective-permute-start(f32[2,64,512]{2,1,0:T(8,128)} %get-tuple-element.40), channel_id=1, source_target_pairs={{0,48},{16,32},{32,16},{48,0},{64,112},{80,96},{96,80},{112,64},{1... | collective-permute-start | bytes 786440 | tf_op jit(solution)/shard_map/ppermute | solution.py:292
  165.7 15.6 %copy-start.15 = (f32[2,64,512]{2,1,0:T(8,128)S(1)}, f32[2,64,512]{2,1,0:T(8,128)}, u32[]{:S(2)}) copy-start(f32[2,64,512]{2,1,0:T(8,128)} %copy-done.14) | copy-start | bytes 786436
  165.7 15.6 %copy-start.17 = (f32[2,64,512]{2,1,0:T(8,128)S(1)}, f32[2,64,512]{2,1,0:T(8,128)}, u32[]{:S(2)}) copy-start(f32[2,64,512]{2,1,0:T(8,128)} %copy-done.16) | copy-start | bytes 786436
  174.7 6.6 %collective-permute-start.24 = (f32[2,64,512]{2,1,0:T(8,128)}, f32[2,64,512]{2,1,0:T(8,128)S(1)}, u32[]{:S(2)}, u32[]{:S(2)}) collective-permute-start(f32[2,64,512]{2,1,0:T(8,128)} %get-tuple-element.41), channel_id=1, source_target_pairs={{0,32},{16,48},{32,0},{48,16},{64,96},{80,112},{96,64},{112,80},{1... | collective-permute-start | bytes 786440 | tf_op jit(solution)/shard_map/ppermute | solution.py:292

commit v2 on v0

v2 whole, which is shorter than its diff:
```python
import functools

import jax
import jax.numpy as jnp
from jax import lax
from jax.experimental import pallas as pl
from jax.experimental.pallas import tpu as pltpu
from jax.sharding import PartitionSpec as P

BW = 256
STEPS = 2
FIRST_PART = 12
READ = 256
CHUNK = 768
VMEM = 16 * 1024 * 1024

epsilon = 1e-06

in_vmem = pl.BlockSpec(memory_space=pltpu.VMEM)
in_smem = pl.BlockSpec(memory_space=pltpu.SMEM)
in_hbm = pl.BlockSpec(memory_space=pltpu.HBM)
anywhere = pl.BlockSpec(memory_space=pl.ANY)


def f32(*shape):
    return jax.ShapeDtypeStruct(shape, jnp.float32)


def bf16(*shape):
    return jax.ShapeDtypeStruct(shape, jnp.bfloat16)


def params(limit=VMEM):
    return pltpu.CompilerParams(vmem_limit_bytes=limit)


def cost(flops, nbytes):
    return pl.CostEstimate(flops=flops, bytes_accessed=nbytes, transcendentals=0)


def split(x):
    high = x.astype(jnp.bfloat16)
    low = (x - high.astype(jnp.float32)).astype(jnp.bfloat16)
    return high, low


def add_squares(acc, slot, x):
    rows, cols = x.shape
    for half in range(cols // 128):
        piece = x[:, half * 128 : (half + 1) * 128]
        acc[2 * slot + half] += jnp.sum((piece * piece).reshape(rows // 8, 8, 128), axis=0)


def put_sums(sums_ref, acc):
    for row in range(8):
        sums_ref[row : row + 1, :] = jnp.sum(acc[row], axis=0, keepdims=True)


def first_kernel(x_ref, high_ref, low_ref, sums_ref, x, sem, acc):
    rows = x_ref.shape[0]
    copies = []
    for i in range(rows // READ):
        here = pl.ds(i * READ, READ)
        copies.append(pltpu.make_async_copy(x_ref.at[here, :], x.at[here, :], sem.at[i]))
    for copy in copies:
        copy.start()
    acc[...] = jnp.zeros_like(acc)
    for i, copy in enumerate(copies):
        here = slice(i * READ, (i + 1) * READ)
        copy.wait()
        for slot in range(4):
            piece = x[here, slot * BW : (slot + 1) * BW]
            add_squares(acc, slot, piece)
            high_ref[slot, here, :], low_ref[slot, here, :] = split(piece)
    put_sums(sums_ref, acc)


def first(columns):
    rows, cols = columns.shape
    return pl.pallas_call(
        first_kernel,
        in_specs=[in_hbm],
        out_specs=[in_vmem] * 3,
        out_shape=[bf16(4, rows, BW), bf16(4, rows, BW), f32(8, 128)],
        scratch_shapes=[
            pltpu.VMEM((rows, cols), jnp.float32),
            pltpu.SemaphoreType.DMA((rows // READ,)),
            pltpu.VMEM((8, 8, 128), jnp.float32),
        ],
        compiler_params=params(44 * 1024 * 1024),
        cost_estimate=cost(1 << 10, 1 << 10),
        name="first",
    )(columns)


def scale_kernel(total_rows, step, plan_ref, sums_ref, rot_ref, out_ref, scratch):
    scratch[...] = jnp.sqrt(jnp.float32(total_rows)) * lax.rsqrt(sums_ref[...] + epsilon)
    for k in range(4):
        pair, half = k // 2, k % 2
        for part in range(2):
            row = scratch[pl.ds(2 * plan_ref[step, 0, k] + part, 1), :]
            column = jnp.broadcast_to(row, (128, 128)).T
            top = half * BW + part * 128
            for c in range(4):
                lanes = slice(c * 128, (c + 1) * 128)
                h, l = split(rot_ref[step, pair, top : top + 128, lanes] * column)
                out_ref[pair, top : top + 128, lanes] = h
                out_ref[pair, 2 * BW + top : 2 * BW + top + 128, lanes] = h
                out_ref[pair, 4 * BW + top : 4 * BW + top + 128, lanes] = l


def scaled(total_rows, step, sums, rotations, plan):
    return pl.pallas_call(
        functools.partial(scale_kernel, total_rows, step),
        in_specs=[in_smem, in_vmem, in_vmem],
        out_specs=in_vmem,
        out_shape=bf16(2, 6 * BW, 2 * BW),
        scratch_shapes=[pltpu.VMEM((8, 128), jnp.float32)],
        compiler_params=params(),
        cost_estimate=cost(1 << 10, 1 << 10),
        name="scale",
    )(plan, sums, rotations)


def pieces(rows):
    count = -(-rows // CHUNK)
    return [(k * (rows // count), rows // count) for k in range(count)]


def stacked(high_ref, low_ref, plan_ref, step, pair, row, count):
    slots = [plan_ref[step, 0, 2 * pair + k] for k in range(2)]
    h = [high_ref[slot, row : row + count, :] for slot in slots]
    l = [low_ref[slot, row : row + count, :] for slot in slots]
    return jnp.concatenate(h + l + h, axis=1)


def half_gram(nh, nl):
    turned = nh.T
    return jnp.dot(
        jnp.concatenate([turned, turned], axis=1),
        jnp.concatenate([nh * jnp.bfloat16(0.5), nl], axis=0),
        preferred_element_type=jnp.float32,
    )


def cut_gram(total_rows, gram_acc, outs):
    for pair in range(2):
        half = gram_acc[pair]
        gram_acc[pair] = (half + half.T) * jnp.float32(1.0 / total_rows)
    x = lax.axis_index("frame") // 2
    near = x + 1 - 2 * (x % 2)
    blocks = ((x, 3 - x), (near, 3 - near)), ((x, near), (3 - x, 3 - near))
    for pair in range(2):
        for which in range(2):
            for k in range(2):
                row = pl.multiple_of(128 * blocks[pair][which][k], 128)
                outs[2 * pair + which][k] = gram_acc[pair, pl.ds(row, 128), :]


cut_shapes = [f32(2, 128, 2 * BW)] * 4


def send_kernel(parts, plan_ref, high_ref, low_ref, rot_ref, *refs):
    outs, acc = refs[:-1], refs[-1]
    acc[...] = jnp.zeros_like(acc)
    first_row = 0
    for p, rows in enumerate(parts):
        for r, count in pieces(rows):
            for pair in range(2):
                x = stacked(high_ref, low_ref, plan_ref, 0, pair, first_row + r, count)
                new = jnp.dot(x, rot_ref[pair, :, BW:], preferred_element_type=jnp.float32)
                outs[2 * p + pair][r : r + count, :] = new
                add_squares(acc, pair, new)
        first_row += rows
    for pair in range(2):
        top = parts[0]
        for half in range(2):
            lanes = slice(half * 128, (half + 1) * 128)
            outs[pair][top : top + 8, lanes] = acc[2 * pair + half]


def send(parts, plan, high, low, rot):
    extra = [8] + [0] * (len(parts) - 1)
    outs = [f32(rows + more, BW) for rows, more in zip(parts, extra) for _ in range(2)]
    outs = pl.pallas_call(
        functools.partial(send_kernel, parts),
        in_specs=[in_smem] + [in_vmem] * 3,
        out_specs=[in_vmem] * len(outs),
        out_shape=outs,
        scratch_shapes=[pltpu.VMEM((4, 8, 128), jnp.float32)],
        compiler_params=params(),
        cost_estimate=cost(1 << 10, 1 << 10),
        name="send",
    )(plan, high, low, rot)
    return outs[0::2], outs[1::2]


def stay_kernel(parts, plan_ref, high_ref, low_ref, rot_ref, *refs):
    outs, sums_ref, acc = refs[4:-2], refs[-2], refs[-1]
    acc[...] = jnp.zeros_like(acc)
    first_row = 0
    for p, rows in enumerate(parts):
        for r, count in pieces(rows):
            for pair in range(2):
                x = stacked(high_ref, low_ref, plan_ref, 0, pair, first_row + r, count)
                new = jnp.dot(x, rot_ref[pair, :, :BW], preferred_element_type=jnp.float32)
                h, l = split(new)
                outs[2 * p][pair, r : r + count, :] = h
                outs[2 * p + 1][pair, r : r + count, :] = l
                add_squares(acc, pair, new)
        first_row += rows
    for row in range(4):
        sums_ref[row : row + 1, :] = jnp.sum(acc[row], axis=0, keepdims=True)
    sums_ref[4:8] = jnp.zeros((4, 128), jnp.float32)


def stay(parts, plan, high, low, rot, up, down):
    outs = [up, down]
    outs += [bf16(2, rows, BW) for rows in parts for _ in range(2)] + [f32(8, 128)]
    outs = pl.pallas_call(
        functools.partial(stay_kernel, parts),
        in_specs=[in_smem] + [in_vmem] * 3 + [anywhere] * 2,
        out_specs=[anywhere] * 2 + [in_vmem] * (len(outs) - 2),
        out_shape=[jax.ShapeDtypeStruct(out.shape, out.dtype) for out in outs],
        input_output_aliases={4: 0, 5: 1},
        scratch_shapes=[pltpu.VMEM((4, 8, 128), jnp.float32)],
        compiler_params=params(),
        cost_estimate=cost(1 << 10, 1 << 10),
        name="stay",
    )(plan, high, low, rot, up, down)
    return list(zip(outs[2:-1:2], outs[3:-1:2])), outs[-1], outs[0], outs[1]


def gram_kernel(parts, *refs):
    ins, gram_acc = refs[:-1], refs[-1]
    for p, rows in enumerate(parts):
        kept_high, kept_low, up, down = ins[4 * p : 4 * p + 4]
        for r, count in pieces(rows):
            here = slice(r, r + count)
            for pair, sent in ((0, up), (1, down)):
                h, l = split(sent[here, :])
                gram = half_gram(
                    jnp.concatenate([kept_high[pair, here, :], h], axis=1),
                    jnp.concatenate([kept_low[pair, here, :], l], axis=1),
                )
                gram_acc[pair] = gram if p + r == 0 else gram + gram_acc[pair]


def gram(parts, kept, ups, downs):
    args = []
    for k, up, down in zip(kept, ups, downs):
        args += [*k, up, down]
    return pl.pallas_call(
        functools.partial(gram_kernel, parts),
        in_specs=[in_vmem] * len(args),
        out_specs=in_vmem,
        out_shape=f32(2, 2 * BW, 2 * BW),
        compiler_params=params(),
        cost_estimate=cost(1 << 10, 1 << 10),
        name="gram",
    )(*args)


def cut_kernel(total_rows, gram_ref, *refs):
    outs, gram_acc = refs[-5:-1], refs[-1]
    gram_acc[...] = gram_ref[...]
    cut_gram(total_rows, gram_acc, outs)


def cut(total_rows, half, after, later=()):
    shapes = [jax.ShapeDtypeStruct(x.shape, x.dtype) for x in later]
    count = len(later)
    outs = pl.pallas_call(
        functools.partial(cut_kernel, total_rows),
        in_specs=[in_vmem] + [anywhere] * (count + len(after)),
        out_specs=[anywhere] * count + [in_vmem] * 4,
        out_shape=shapes + cut_shapes,
        input_output_aliases={1 + k: k for k in range(count)},
        scratch_shapes=[pltpu.VMEM((2, 2 * BW, 2 * BW), jnp.float32)],
        compiler_params=params(),
        cost_estimate=cost(1 << 10, 1 << 10),
        name="cut",
    )(half, *later, *after)
    return outs[count:], outs[:count]


def update_kernel(parts, part, plan_ref, kept_high, kept_low, up_in, down_in,
                  rot_ref, *refs):
    refs = list(refs)
    if part:
        gram_in = refs.pop(0)
        refs.pop(0)
    result, out_up, out_down = refs.pop(0), refs.pop(0), refs.pop(0)
    gram_acc = refs.pop(0)
    high_ref, low_ref, kept_ref, sem = refs
    rows, top = parts[part], sum(parts[:part])
    for slot in range(2):
        high_ref[slot] = kept_high[slot]
        low_ref[slot] = kept_low[slot]
    high_ref[2], low_ref[2] = split(up_in[:rows, :])
    high_ref[3], low_ref[3] = split(down_in[:rows, :])

    copies = []
    for k, (r, count) in enumerate(pieces(rows)):
        here = slice(r, r + count)
        for pair, sent in ((0, out_up), (1, out_down)):
            x = stacked(high_ref, low_ref, plan_ref, 1, pair, r, count)
            new = jnp.dot(x, rot_ref[pair], preferred_element_type=jnp.float32)
            kept_ref[here, pair * BW : (pair + 1) * BW] = new[:, :BW]
            sent[here, :] = new[:, BW:]
            gram = half_gram(*split(new))
            if r:
                gram = gram + gram_acc[pair]
            elif part:
                gram = gram + gram_in[pair]
            gram_acc[pair] = gram
        copies.append(
            pltpu.make_async_copy(
                kept_ref.at[pl.ds(r, count), :],
                result.at[pl.ds(top + r, count), pl.ds(0, 2 * BW)],
                sem.at[k],
            )
        )
        copies[-1].start()
    for copy in copies:
        copy.wait()


def update(parts, part, plan, xs, rot, gram_in, result):
    rows = parts[part]
    args = [plan, *xs, rot]
    in_specs = [in_smem] + [in_vmem] * 5
    if part:
        args += [gram_in, result]
        in_specs += [in_vmem, in_hbm]
    outs = [f32(sum(parts), 4 * BW), f32(rows, BW), f32(rows, BW)]
    outs.append(f32(2, 2 * BW, 2 * BW))
    return pl.pallas_call(
        functools.partial(update_kernel, parts, part),
        in_specs=in_specs,
        out_specs=[in_hbm] + [in_vmem] * (len(outs) - 1),
        out_shape=outs,
        scratch_shapes=[
            pltpu.VMEM((4, rows, BW), jnp.bfloat16),
            pltpu.VMEM((4, rows, BW), jnp.bfloat16),
            pltpu.VMEM((rows, 2 * BW), jnp.float32),
            pltpu.SemaphoreType.DMA((len(pieces(rows)),)),
        ],
        input_output_aliases={len(args) - 1: 0} if part else {},
        compiler_params=params(),
        cost_estimate=cost(1 << 10, 1 << 10),
        name="update",
    )(*args)


def fill_kernel(row0, _, up, down, out, sem):
    rows = up.shape[0]
    copies = [
        pltpu.make_async_copy(
            ref, out.at[pl.ds(row0, rows), pl.ds((2 + k) * BW, BW)], sem.at[k]
        )
        for k, ref in enumerate((up, down))
    ]
    for copy in copies:
        copy.start()
    for copy in copies:
        copy.wait()


def fill(out, up, down, row0):
    return pl.pallas_call(
        functools.partial(fill_kernel, row0),
        in_specs=[in_hbm, in_vmem, in_vmem],
        out_specs=in_hbm,
        out_shape=jax.ShapeDtypeStruct(out.shape, out.dtype),
        input_output_aliases={0: 0},
        scratch_shapes=[pltpu.SemaphoreType.DMA((2,))],
        compiler_params=params(),
        cost_estimate=cost(1 << 10, 1 << 10),
        name="fill",
    )(out, up, down)


def mix_kernel(top, own, before, after, _, out):
    out[0:4] = own[0:4]
    for k, ref in enumerate((before, after)):
        for half in range(2):
            row = 4 + 2 * k + half
            lanes = slice(half * 128, (half + 1) * 128)
            out[row : row + 1, :] = jnp.sum(ref[top : top + 8, lanes], axis=0, keepdims=True)


def mix(top, own, before, after, done):
    return pl.pallas_call(
        functools.partial(mix_kernel, top),
        in_specs=[in_vmem] * 3 + [anywhere],
        out_specs=in_vmem,
        out_shape=f32(8, 128),
        compiler_params=params(),
        cost_estimate=cost(1 << 10, 1 << 10),
        name="mix",
    )(own, before, after, done)


def add_kernel(mine0, got0, mine1, got1, *refs):
    keep_ref, send0, send1 = refs[-3:]
    for pair, (mine, got, sent) in enumerate(((mine0, got0, send0), (mine1, got1, send1))):
        keep_ref[pair] = mine[0] + got[0]
        sent[...] = mine[1] + got[1]


def add_first(args, after):
    block = f32(128, 2 * BW)
    return pl.pallas_call(
        add_kernel,
        in_specs=[in_vmem] * 4 + [anywhere] * len(after),
        out_specs=[in_vmem] * 3,
        out_shape=[f32(2, 128, 2 * BW), block, block],
        compiler_params=params(),
        cost_estimate=cost(1 << 10, 1 << 10),
        name="add",
    )(*args, *after)


def halve_kernel(mine, got0, got1, *refs):
    keep_ref, send_ref = refs[-2:]
    bit = lax.axis_index("frame") % 2
    for pair, got in enumerate((got0, got1)):
        for ref, chosen in ((keep_ref, bit), (send_ref, 1 - bit)):
            rows = pl.ds(pl.multiple_of(64 * chosen, 64), 64)
            ref[pair] = mine[pair, rows, :] + got[rows, :]


def halve(args, after):
    return pl.pallas_call(
        halve_kernel,
        in_specs=[in_vmem] * 3 + [anywhere] * len(after),
        out_specs=[in_vmem] * 2,
        out_shape=[f32(2, 64, 2 * BW)] * 2,
        compiler_params=params(),
        cost_estimate=cost(1 << 10, 1 << 10),
        name="halve",
    )(*args, *after)


def finish_kernel(row0, _, up, down, *refs):
    out, grams, sem = refs[-3:]
    rows = up.shape[0]
    copies = [
        pltpu.make_async_copy(
            ref, out.at[pl.ds(row0, rows), pl.ds((2 + k) * BW, BW)], sem.at[k]
        )
        for k, ref in enumerate((up, down))
    ]
    for copy in copies:
        copy.start()
    for step in range(STEPS):
        mine, got = refs[2 * step], refs[2 * step + 1]
        for pair in range(2):
            grams[step, :, pair, :] = mine[pair] + got[pair]
    for copy in copies:
        copy.wait()


def finish(out, up, down, row0, pieces):
    args = [array for piece in pieces for array in piece]
    return pl.pallas_call(
        functools.partial(finish_kernel, row0),
        in_specs=[in_hbm] + [in_vmem] * (2 + len(args)),
        out_specs=[in_hbm, in_vmem],
        out_shape=[
            jax.ShapeDtypeStruct(out.shape, out.dtype),
            f32(STEPS, 64, 2, 2 * BW),
        ],
        input_output_aliases={0: 0},
        scratch_shapes=[pltpu.SemaphoreType.DMA((2,))],
        compiler_params=params(),
        cost_estimate=cost(1 << 10, 1 << 10),
        name="finish",
    )(out, up, down, *args)


def shift(x, by):
    size = lax.axis_size("pair")
    return lax.ppermute(x, "pair", [(i, (i + by) % size) for i in range(size)])


def swap(x, bit):
    size = lax.axis_size("frame")
    return lax.ppermute(x, "frame", [(i, i ^ bit) for i in range(size)])


def all_sum(x, bits):
    for bit in bits:
        x = x + swap(x, bit)
    return x


def local(columns, rotations, plan):
    rows = columns.shape[0]
    total_rows = rows * lax.axis_size("frame")
    parts = (rows * FIRST_PART // 32, rows * (32 - FIRST_PART) // 32)
    high, low, sums = first(columns)
    rot = scaled(total_rows, 0, all_sum(sums, (2, 6, 1)), rotations, plan)
    ups, downs = send(parts, plan, high, low, rot)
    kept, own, late_up, late_down = stay(parts, plan, high, low, rot, ups[1], downs[1])
    ups, downs = (ups[0], late_up), (downs[0], late_down)
    moved = [(shift(up, 1), shift(down, -1)) for up, down in zip(ups, downs)]
    half = gram(parts, kept, ups, downs)
    mixed = mix(parts[0], own, *moved[0], half)
    tile = all_sum(mixed, (1, 6, 2))
    halves, _ = cut(total_rows, half, (mixed,))
    got = swap(halves[1], 2), swap(halves[3], 6)
    keep0, send0, send1 = add_first((halves[0], got[0], halves[2], got[1]), ())

    rot = scaled(total_rows, 1, tile, rotations, plan)
    half = result = None
    sent = []
    for p in range(len(parts)):
        result, up, down, half = update(
            parts, p, plan, (*kept[p], *moved[p]), rot, half, result
        )
        sent.append((up, down))
    early = shift(sent[0][0], 1), shift(sent[0][1], -1)

    second = halve((keep0, swap(send0, 6), swap(send1, 2)), ())
    halves, sent = cut(total_rows, half, (*early, second[0]), sent[1])
    late = shift(sent[0], 1), shift(sent[1], -1)
    got = swap(halves[1], 2), swap(halves[3], 6)
    first_grams = (second[0], swap(second[1], 1))
    keep0, send0, send1 = add_first((halves[0], got[0], halves[2], got[1]), ())
    second = halve((keep0, swap(send0, 6), swap(send1, 2)), ())
    last_grams = (second[0], swap(second[1], 1))
    result = fill(result, *early, 0)
    return finish(result, *late, parts[0], (first_grams, last_grams))


def solution(mesh):
    in_specs = (P("frame", "pair"), P(None, "pair", None, None), P(None, "pair", None))
    out_specs = (P("frame", "pair"), P(None, "frame", "pair", None))
    return jax.shard_map(local, mesh=mesh, in_specs=in_specs, out_specs=out_specs, check_vma=False)
```

time: 564 us -> 123 us (0.22)
  the two profiles are of different devices: /device:TPU:12 before, /device:TPU:0 now
where the time goes in v2:
time: 123 us
  waiting for transfers between devices  43.8 us (36%)
  starting transfers between devices  39.2 us (32%)
  Pallas kernels  38.6 us (31%)
    ppermute x16, waiting for transfers between devices, swap(): return lax.ppermute(x, 'frame', [(i, i ^ bit) for i in range(size)])  43.8 us
    ppermute x16, starting transfers between devices, swap(): return lax.ppermute(x, 'frame', [(i, i ^ bit) for i in range(size)])  23.5 us
    ppermute x8, starting transfers between devices, shift(): return lax.ppermute(x, 'pair', [(i, (i + by) % size) for i in range(size)])  15.7 us
    pallas_call x2, Pallas kernels, update(): pl.pallas_call(functools.partial(update_kernel, parts, part), in_specs=in...  14.7 us
    pallas_call x1, Pallas kernels, gram(): pl.pallas_call(functools.partial(gram_kernel, parts), in_specs=[in_vmem]...  4.6 us
    pallas_call x1, Pallas kernels, stay(): pl.pallas_call(functools.partial(stay_kernel, parts), in_specs=[in_smem]...  4.06 us
    pallas_call x1, Pallas kernels, send(): pl.pallas_call(functools.partial(send_kernel, parts), in_specs=[in_smem]...  3.96 us
    pallas_call x1, Pallas kernels, first(): pl.pallas_call(first_kernel, in_specs=[in_hbm], out_specs=[in_vmem] * 3,...  3.84 us
  transfers between devices with their start and end apart: 24, of which 11 were waited for; matrix products, arithmetic and copies ran while one was open for 0% of the time, Pallas kernels for 22%

profile of v2, /device:TPU:0, one launch (start us, length us, event | category | flops | bytes accessed | tf_op | source)
XLA Modules:
  0.0 122.7 jit_solution(10743406007409774197)
XLA Ops:
  0.6 3.8 %first.1 = (bf16[4,2048,256]{2,1,0:T(8,128)(2,1)S(1)}, bf16[4,2048,256]{2,1,0:T(8,128)(2,1)S(1)}, f32[8,128]{1,0:T(8,128)S(1)}) custom-call(f32[2048,1024]{1,0:T(8,128)} %x_ref.1), custom_call_target="tpu_custom_call" | custom-call | flops 1024 | bytes 1024 | tf_op jit(solution)/shard_map/first/pallas_call | solution.py:80
  4.5 1.7 %collective-permute-start = (f32[8,128]{1,0:T(8,128)S(1)}, f32[8,128]{1,0:T(8,128)S(1)}, u32[]{:S(2)}, u32[]{:S(2)}) collective-permute-start(f32[8,128]{1,0:T(8,128)S(1)} %get-tuple-element.46), channel_id=1, source_target_pairs={{0,32},{16,48},{32,0},{48,16},{64,96},{80,112},{96,64},{112,80},{1... | collective-permute-start | bytes 12296 | tf_op jit(solution)/shard_map/ppermute | solution.py:490
  6.2 2.0 %collective-permute-done = f32[8,128]{1,0:T(8,128)S(1)} collective-permute-done((f32[8,128]{1,0:T(8,128)S(1)}, f32[8,128]{1,0:T(8,128)S(1)}, u32[]{:S(2)}, u32[]{:S(2)}) %collective-permute-start) | collective-permute-done | bytes 4128 | tf_op jit(solution)/shard_map/ppermute | solution.py:490
  8.2 2.8 %collective-permute-start.1 = (f32[8,128]{1,0:T(8,128)S(1)}, f32[8,128]{1,0:T(8,128)S(1)}, u32[]{:S(2)}, u32[]{:S(2)}) collective-permute-start(f32[8,128]{1,0:T(8,128)S(1)} %add.20), channel_id=1, source_target_pairs={{0,96},{16,112},{32,64},{48,80},{64,32},{80,48},{96,0},{112,16},{1... | collective-permute-start | bytes 12296 | tf_op jit(solution)/shard_map/ppermute | solution.py:490
  11.0 2.0 %collective-permute-done.1 = f32[8,128]{1,0:T(8,128)S(1)} collective-permute-done((f32[8,128]{1,0:T(8,128)S(1)}, f32[8,128]{1,0:T(8,128)S(1)}, u32[]{:S(2)}, u32[]{:S(2)}) %collective-permute-start.1) | collective-permute-done | bytes 4128 | tf_op jit(solution)/shard_map/ppermute | solution.py:490
  13.0 3.3 %collective-permute-start.2 = (f32[8,128]{1,0:T(8,128)S(1)}, f32[8,128]{1,0:T(8,128)S(1)}, u32[]{:S(2)}, u32[]{:S(2)}) collective-permute-start(f32[8,128]{1,0:T(8,128)S(1)} %add.21), channel_id=1, source_target_pairs={{0,16},{16,0},{32,48},{48,32},{64,80},{80,64},{96,112},{112,96},{1... | collective-permute-start | bytes 12296 | tf_op jit(solution)/shard_map/ppermute | solution.py:490
  16.3 1.8 %collective-permute-done.2 = f32[8,128]{1,0:T(8,128)S(1)} collective-permute-done((f32[8,128]{1,0:T(8,128)S(1)}, f32[8,128]{1,0:T(8,128)S(1)}, u32[]{:S(2)}, u32[]{:S(2)}) %collective-permute-start.2) | collective-permute-done | bytes 4128 | tf_op jit(solution)/shard_map/ppermute | solution.py:490
  18.1 1.1 scale.2.rot_ref
  19.2 4.0 %send.1 = (f32[776,256]{1,0:T(8,128)S(1)}, f32[776,256]{1,0:T(8,128)S(1)}, f32[1280,256]{1,0:T(8,128)S(1)}, f32[1280,256]{1,0:T(8,128)S(1)}) custom-call(s32[2,1,4]{2,1,0:T(1,128)S(1)} %copy-done.1, bf16[4,2048,256]{2,1,0:T(8,128)(2,1)S(1)} %get-tuple-element.44.high_ref, bf16[4,2048,256]{2,1,0:T(8,128)(2,1)S(1)} %get-tuple-element.45.low_ref, ...), custom_call_target="tpu_custom_call" | custom-call | flops 1024 | bytes 1024 | tf_op jit(solution)/shard_map/send/pallas_call | solution.py:185
  23.2 0.1 collective-permute-start.5
  23.3 3.8 %collective-permute-start.6 = (f32[776,256]{1,0:T(8,128)S(1)}, f32[776,256]{1,0:T(8,128)S(1)}, u32[]{:S(2)}, u32[]{:S(2)}) collective-permute-start(f32[776,256]{1,0:T(8,128)S(1)} %get-tuple-element.55.refs_3_), channel_id=1, source_target_pairs={{0,15},{1,0},{2,1},{3,2},{4,3},{5,4},{6,5},{7,6},{8,7},{9,8},{10,9... | collective-permute-start | bytes 2383880 | tf_op jit(solution)/shard_map/ppermute | solution.py:485
  27.1 4.1 %stay.1 = (f32[1280,256]{1,0:T(8,128)S(1)}, f32[1280,256]{1,0:T(8,128)S(1)}, bf16[2,768,256]{2,1,0:T(8,128)(2,1)S(1)}, bf16[2,768,256]{2,1,0:T(8,128)(2,1)S(1)},...) custom-call(s32[2,1,4]{2,1,0:T(1,128)S(1)} %copy-done.1, ...), custom_call_target="tpu_custom_call", output_to_operand_aliasing={{0}: (4, {}), {1}: (5, {})} | custom-call | flops 1024 | bytes 1024 | tf_op jit(solution)/shard_map/stay/pallas_call | solution.py:220
  31.2 0.1 collective-permute-start.3
  31.3 3.8 %collective-permute-start.4 = (f32[1280,256]{1,0:T(8,128)S(1)}, f32[1280,256]{1,0:T(8,128)S(1)}, u32[]{:S(2)}, u32[]{:S(2)}) collective-permute-start(f32[1280,256]{1,0:T(8,128)S(1)} %get-tuple-element.52.refs_7_), channel_id=1, source_target_pairs={{0,15},{1,0},{2,1},{3,2},{4,3},{5,4},{6,5},{7,6},{8,7},{9,8},{10,9... | collective-permute-start | bytes 3932168 | tf_op jit(solution)/shard_map/ppermute | solution.py:485
  35.1 4.6 %gram.1._.gram_ref = f32[2,512,512]{2,1,0:T(8,128)S(1)} custom-call(bf16[2,768,256]{2,1,0:T(8,128)(2,1)S(1)} %get-tuple-element.56.refs_0_.kept_high, bf16[2,768,256]{2,1,0:T(8,128)(2,1)S(1)} %get-tuple-element.57.refs_1_.kept_low, f32[776,256]{1,0:T(8,128)S(1)} %get-tuple-element.54.refs_2_, f32[776,256]{1,0:T(8,128)S(1)} %get-tuple-element.55.refs_3_, ...), custom_call_target="tpu_custom_call" | custom-call | flops 1024 | bytes 1024 | tf_op jit(solution)/shard_map/gram/pallas_call | solution.py:253
  39.7 0.0 collective-permute-done.5.before.up_in
  39.7 0.0 collective-permute-done.6.after.down_in
  39.7 0.7 cut.2
  40.5 0.4 collective-permute-start.12
  40.9 3.2 %collective-permute-start.7 = (f32[8,128]{1,0:T(8,128)S(1)}, f32[8,128]{1,0:T(8,128)S(1)}, u32[]{:S(2)}, u32[]{:S(2)}) collective-permute-start(f32[8,128]{1,0:T(8,128)S(1)} %mix.1.refs_0_), channel_id=1, source_target_pairs={{0,16},{16,0},{32,48},{48,32},{64,80},{80,64},{96,112},{112,96},{1... | collective-permute-start | bytes 12296 | tf_op jit(solution)/shard_map/ppermute | solution.py:490
  44.1 10.4 %collective-permute-done.7 = f32[8,128]{1,0:T(8,128)S(1)} collective-permute-done((f32[8,128]{1,0:T(8,128)S(1)}, f32[8,128]{1,0:T(8,128)S(1)}, u32[]{:S(2)}, u32[]{:S(2)}) %collective-permute-start.7) | collective-permute-done | bytes 4128 | tf_op jit(solution)/shard_map/ppermute | solution.py:490
  54.6 2.8 %collective-permute-start.8 = (f32[8,128]{1,0:T(8,128)S(1)}, f32[8,128]{1,0:T(8,128)S(1)}, u32[]{:S(2)}, u32[]{:S(2)}) collective-permute-start(f32[8,128]{1,0:T(8,128)S(1)} %add.23), channel_id=1, source_target_pairs={{0,96},{16,112},{32,64},{48,80},{64,32},{80,48},{96,0},{112,16},{1... | collective-permute-start | bytes 12296 | tf_op jit(solution)/shard_map/ppermute | solution.py:490
  57.3 2.1 %collective-permute-done.8 = f32[8,128]{1,0:T(8,128)S(1)} collective-permute-done((f32[8,128]{1,0:T(8,128)S(1)}, f32[8,128]{1,0:T(8,128)S(1)}, u32[]{:S(2)}, u32[]{:S(2)}) %collective-permute-start.8) | collective-permute-done | bytes 4128 | tf_op jit(solution)/shard_map/ppermute | solution.py:490
  59.4 0.0 collective-permute-start.9
  59.4 2.8 %collective-permute-start.13 = (f32[2,128,512]{2,1,0:T(8,128)S(1)}, f32[2,128,512]{2,1,0:T(8,128)S(1)}, u32[]{:S(2)}, u32[]{:S(2)}) collective-permute-start(f32[2,128,512]{2,1,0:T(8,128)S(1)} %get-tuple-element.69), channel_id=1, source_target_pairs={{0,96},{16,112},{32,64},{48,80},{64,32},{80,48},{96,0},{112,16},{1... | collective-permute-start | bytes 1572872 | tf_op jit(solution)/shard_map/ppermute | solution.py:490
  62.2 0.8 collective-permute-done.9
  63.0 1.1 scale.3.rot_ref
  64.1 5.7 %update.2 = (f32[2048,1024]{1,0:T(8,128)}, f32[768,256]{1,0:T(8,128)S(1)}, f32[768,256]{1,0:T(8,128)S(1)}, f32[2,512,512]{2,1,0:T(8,128)S(1)}) custom-call(s32[2,1,4]{2,1,0:T(1,128)S(1)} %copy-done.1, bf16[2,768,256]{2,1,0:T(8,128)(2,1)S(1)} %get-tuple-element.56.refs_0_.kept_high, bf16[2,768,256]{2,1,0:T(8,128)(2,1)S(1)} %get-tuple-element.57.refs_1_.kept_low, ...), custom_call_target="tpu_custom_call" | custom-call | flops 1024 | bytes 1024 | tf_op jit(solution)/shard_map/update/pallas_call | solution.py:338
  69.8 0.1 collective-permute-start.10
  69.8 0.0 collective-permute-done.12.got0
  69.8 3.8 %collective-permute-start.11 = (f32[768,256]{1,0:T(8,128)S(1)}, f32[768,256]{1,0:T(8,128)S(1)}, u32[]{:S(2)}, u32[]{:S(2)}) collective-permute-start(f32[768,256]{1,0:T(8,128)S(1)} %get-tuple-element.62), channel_id=1, source_target_pairs={{0,15},{1,0},{2,1},{3,2},{4,3},{5,4},{6,5},{7,6},{8,7},{9,8},{10,9... | collective-permute-start | bytes 2359304 | tf_op jit(solution)/shard_map/ppermute | solution.py:485
  73.7 0.0 collective-permute-done.13.got1
  73.7 0.1 add.26
  73.8 2.8 %collective-permute-start.14 = (f32[128,512]{1,0:T(8,128)S(1)}, f32[128,512]{1,0:T(8,128)S(1)}, u32[]{:S(2)}, u32[]{:S(2)}) collective-permute-start(f32[128,512]{1,0:T(8,128)S(1)} %get-tuple-element.71), channel_id=1, source_target_pairs={{0,96},{16,112},{32,64},{48,80},{64,32},{80,48},{96,0},{112,16},{1... | collective-permute-start | bytes 786440 | tf_op jit(solution)/shard_map/ppermute | solution.py:490
  76.6 0.0 collective-permute-done.3.up_in
  76.6 0.0 collective-permute-start.15
  76.6 0.0 collective-permute-done.4.down_in
  76.6 9.0 %update.3 = (f32[2048,1024]{1,0:T(8,128)}, f32[1280,256]{1,0:T(8,128)S(1)}, f32[1280,256]{1,0:T(8,128)S(1)}, f32[2,512,512]{2,1,0:T(8,128)S(1)}) custom-call(s32[2,1,4]{2,1,0:T(1,128)S(1)} %copy-done.1, bf16[2,1280,256]{2,1,0:T(8,128)(2,1)S(1)} %get-tuple-element.49.refs_4_.kept_high, ...), custom_call_target="tpu_custom_call", output_to_operand_aliasing={{0}: (7, {})} | custom-call | flops 1024 | bytes 1024 | tf_op jit(solution)/shard_map/update/pallas_call | solution.py:338
  85.7 0.0 collective-permute-done.14.got0
  85.7 0.0 collective-permute-done.15.got1
  85.7 0.1 halve.2
  85.8 0.0 collective-permute-done.10.up.refs_2_
  85.8 0.0 collective-permute-done.11.down.refs_3_
  85.8 0.7 cut.3
  86.6 0.1 collective-permute-start.16
  86.6 3.8 %collective-permute-start.17 = (f32[1280,256]{1,0:T(8,128)S(1)}, f32[1280,256]{1,0:T(8,128)S(1)}, u32[]{:S(2)}, u32[]{:S(2)}) collective-permute-start(f32[1280,256]{1,0:T(8,128)S(1)} %get-tuple-element.75), channel_id=1, source_target_pairs={{0,15},{1,0},{2,1},{3,2},{4,3},{5,4},{6,5},{7,6},{8,7},{9,8},{10,9... | collective-permute-start | bytes 3932168 | tf_op jit(solution)/shard_map/ppermute | solution.py:485
  90.5 2.0 %collective-permute-start.19 = (f32[2,128,512]{2,1,0:T(8,128)S(1)}, f32[2,128,512]{2,1,0:T(8,128)S(1)}, u32[]{:S(2)}, u32[]{:S(2)}) collective-permute-start(f32[2,128,512]{2,1,0:T(8,128)S(1)} %get-tuple-element.78), channel_id=1, source_target_pairs={{0,32},{16,48},{32,0},{48,16},{64,96},{80,112},{96,64},{112,80},{1... | collective-permute-start | bytes 1572872 | tf_op jit(solution)/shard_map/ppermute | solution.py:490
  92.5 0.5 collective-permute-start.20
  93.0 8.3 %collective-permute-done.19.got0 = f32[2,128,512]{2,1,0:T(8,128)S(1)} collective-permute-done((f32[2,128,512]{2,1,0:T(8,128)S(1)}, f32[2,128,512]{2,1,0:T(8,128)S(1)}, u32[]{:S(2)}, u32[]{:S(2)}) %collective-permute-start.19) | collective-permute-done | bytes 524320 | tf_op jit(solution)/shard_map/ppermute | solution.py:490
  101.3 3.1 %collective-permute-done.20.got1 = f32[2,128,512]{2,1,0:T(8,128)S(1)} collective-permute-done((f32[2,128,512]{2,1,0:T(8,128)S(1)}, f32[2,128,512]{2,1,0:T(8,128)S(1)}, u32[]{:S(2)}, u32[]{:S(2)}) %collective-permute-start.20) | collective-permute-done | bytes 524320 | tf_op jit(solution)/shard_map/ppermute | solution.py:490
  104.4 0.1 add.27
  104.5 0.6 collective-permute-start.21
  105.1 0.0 collective-permute-start.22
  105.1 0.3 collective-permute-start.18
  105.4 6.8 %collective-permute-done.21.got0 = f32[128,512]{1,0:T(8,128)S(1)} collective-permute-done((f32[128,512]{1,0:T(8,128)S(1)}, f32[128,512]{1,0:T(8,128)S(1)}, u32[]{:S(2)}, u32[]{:S(2)}) %collective-permute-start.21) | collective-permute-done | bytes 262176 | tf_op jit(solution)/shard_map/ppermute | solution.py:490
  112.2 0.0 collective-permute-done.22.got1
  112.2 0.1 halve.3
  112.3 0.4 collective-permute-start.23
  112.7 1.2 fill.1._
  113.8 1.2 %collective-permute-done.18.refs_1_ = f32[2,64,512]{2,1,0:T(8,128)S(1)} collective-permute-done((f32[2,64,512]{2,1,0:T(8,128)S(1)}, f32[2,64,512]{2,1,0:T(8,128)S(1)}, u32[]{:S(2)}, u32[]{:S(2)}) %collective-permute-start.18) | collective-permute-done | bytes 262176 | tf_op jit(solution)/shard_map/ppermute | solution.py:490
  115.1 5.1 %collective-permute-done.23.refs_3_ = f32[2,64,512]{2,1,0:T(8,128)S(1)} collective-permute-done((f32[2,64,512]{2,1,0:T(8,128)S(1)}, f32[2,64,512]{2,1,0:T(8,128)S(1)}, u32[]{:S(2)}, u32[]{:S(2)}) %collective-permute-start.23) | collective-permute-done | bytes 262176 | tf_op jit(solution)/shard_map/ppermute | solution.py:490
  120.2 0.0 collective-permute-done.16.up
  120.2 0.0 collective-permute-done.17.down
  120.2 2.3 %finish.1 = (f32[2048,1024]{1,0:T(8,128)}, f32[2,64,2,512]{3,2,1,0:T(2,128)}) custom-call(f32[2048,1024]{1,0:T(8,128)} %fill.1._, f32[1280,256]{1,0:T(8,128)S(1)} %collective-permute-done.16.up, f32[1280,256]{1,0:T(8,128)S(1)} %collective-permute-done.17.down, f32[2,64,512]{2,1,0:T(8,128)S(1)} %get-tuple-element.73.refs_4_.refs_0_, ...), custom_call_target="tpu_custom_call", output_to_operand_aliasing={{0}: (0, {})} | custom-call | flops 1024 | bytes 1024 | tf_op jit(solution)/shard_map/finish/pallas_call | solution.py:467
  (11 shorter events, 0.0 us)
Async XLA Ops:
  0.6 17.5 %copy-start.1 = (s32[2,1,4]{2,1,0:T(1,128)S(1)}, s32[2,1,4]{2,1,0:T(1,128)}, u32[]{:S(2)}) copy-start(s32[2,1,4]{2,1,0:T(1,128)} %plan_ref.11) | copy-start | bytes 100
  0.6 17.5 %copy-start = (f32[2,2,512,512]{3,2,1,0:T(8,128)S(1)}, f32[2,2,512,512]{3,2,1,0:T(8,128)}, u32[]{:S(2)}) copy-start(f32[2,2,512,512]{3,2,1,0:T(8,128)} %rot_ref.3) | copy-start | bytes 12582916
  4.5 3.7 %collective-permute-start = (f32[8,128]{1,0:T(8,128)S(1)}, f32[8,128]{1,0:T(8,128)S(1)}, u32[]{:S(2)}, u32[]{:S(2)}) collective-permute-start(f32[8,128]{1,0:T(8,128)S(1)} %get-tuple-element.46), channel_id=1, source_target_pairs={{0,32},{16,48},{32,0},{48,16},{64,96},{80,112},{96,64},{112,80},{1... | collective-permute-start | bytes 12296 | tf_op jit(solution)/shard_map/ppermute | solution.py:490
  8.2 4.8 %collective-permute-start.1 = (f32[8,128]{1,0:T(8,128)S(1)}, f32[8,128]{1,0:T(8,128)S(1)}, u32[]{:S(2)}, u32[]{:S(2)}) collective-permute-start(f32[8,128]{1,0:T(8,128)S(1)} %add.20), channel_id=1, source_target_pairs={{0,96},{16,112},{32,64},{48,80},{64,32},{80,48},{96,0},{112,16},{1... | collective-permute-start | bytes 12296 | tf_op jit(solution)/shard_map/ppermute | solution.py:490
  13.0 5.1 %collective-permute-start.2 = (f32[8,128]{1,0:T(8,128)S(1)}, f32[8,128]{1,0:T(8,128)S(1)}, u32[]{:S(2)}, u32[]{:S(2)}) collective-permute-start(f32[8,128]{1,0:T(8,128)S(1)} %add.21), channel_id=1, source_target_pairs={{0,16},{16,0},{32,48},{48,32},{64,80},{80,64},{96,112},{112,96},{1... | collective-permute-start | bytes 12296 | tf_op jit(solution)/shard_map/ppermute | solution.py:490
  23.2 16.5 %collective-permute-start.5 = (f32[776,256]{1,0:T(8,128)S(1)}, f32[776,256]{1,0:T(8,128)S(1)}, u32[]{:S(2)}, u32[]{:S(2)}) collective-permute-start(f32[776,256]{1,0:T(8,128)S(1)} %get-tuple-element.54.refs_2_), channel_id=1, source_target_pairs={{0,1},{1,2},{2,3},{3,4},{4,5},{5,6},{6,7},{7,8},{8,9},{9,10},{10,1... | collective-permute-start | bytes 2383880 | tf_op jit(solution)/shard_map/ppermute | solution.py:485
  23.3 16.5 %collective-permute-start.6 = (f32[776,256]{1,0:T(8,128)S(1)}, f32[776,256]{1,0:T(8,128)S(1)}, u32[]{:S(2)}, u32[]{:S(2)}) collective-permute-start(f32[776,256]{1,0:T(8,128)S(1)} %get-tuple-element.55.refs_3_), channel_id=1, source_target_pairs={{0,15},{1,0},{2,1},{3,2},{4,3},{5,4},{6,5},{7,6},{8,7},{9,8},{10,9... | collective-permute-start | bytes 2383880 | tf_op jit(solution)/shard_map/ppermute | solution.py:485
  31.2 45.5 %collective-permute-start.3 = (f32[1280,256]{1,0:T(8,128)S(1)}, f32[1280,256]{1,0:T(8,128)S(1)}, u32[]{:S(2)}, u32[]{:S(2)}) collective-permute-start(f32[1280,256]{1,0:T(8,128)S(1)} %get-tuple-element.51.refs_6_), channel_id=1, source_target_pairs={{0,1},{1,2},{2,3},{3,4},{4,5},{5,6},{6,7},{7,8},{8,9},{9,10},{10,1... | collective-permute-start | bytes 3932168 | tf_op jit(solution)/shard_map/ppermute | solution.py:485
  31.3 45.4 %collective-permute-start.4 = (f32[1280,256]{1,0:T(8,128)S(1)}, f32[1280,256]{1,0:T(8,128)S(1)}, u32[]{:S(2)}, u32[]{:S(2)}) collective-permute-start(f32[1280,256]{1,0:T(8,128)S(1)} %get-tuple-element.52.refs_7_), channel_id=1, source_target_pairs={{0,15},{1,0},{2,1},{3,2},{4,3},{5,4},{6,5},{7,6},{8,7},{9,8},{10,9... | collective-permute-start | bytes 3932168 | tf_op jit(solution)/shard_map/ppermute | solution.py:485
  40.5 29.3 %collective-permute-start.12 = (f32[2,128,512]{2,1,0:T(8,128)S(1)}, f32[2,128,512]{2,1,0:T(8,128)S(1)}, u32[]{:S(2)}, u32[]{:S(2)}) collective-permute-start(f32[2,128,512]{2,1,0:T(8,128)S(1)} %get-tuple-element.67), channel_id=1, source_target_pairs={{0,32},{16,48},{32,0},{48,16},{64,96},{80,112},{96,64},{112,80},{1... | collective-permute-start | bytes 1572872 | tf_op jit(solution)/shard_map/ppermute | solution.py:490
  40.9 13.6 %collective-permute-start.7 = (f32[8,128]{1,0:T(8,128)S(1)}, f32[8,128]{1,0:T(8,128)S(1)}, u32[]{:S(2)}, u32[]{:S(2)}) collective-permute-start(f32[8,128]{1,0:T(8,128)S(1)} %mix.1.refs_0_), channel_id=1, source_target_pairs={{0,16},{16,0},{32,48},{48,32},{64,80},{80,64},{96,112},{112,96},{1... | collective-permute-start | bytes 12296 | tf_op jit(solution)/shard_map/ppermute | solution.py:490
  54.6 4.8 %collective-permute-start.8 = (f32[8,128]{1,0:T(8,128)S(1)}, f32[8,128]{1,0:T(8,128)S(1)}, u32[]{:S(2)}, u32[]{:S(2)}) collective-permute-start(f32[8,128]{1,0:T(8,128)S(1)} %add.23), channel_id=1, source_target_pairs={{0,96},{16,112},{32,64},{48,80},{64,32},{80,48},{96,0},{112,16},{1... | collective-permute-start | bytes 12296 | tf_op jit(solution)/shard_map/ppermute | solution.py:490
  59.4 3.6 %collective-permute-start.9 = (f32[8,128]{1,0:T(8,128)S(1)}, f32[8,128]{1,0:T(8,128)S(1)}, u32[]{:S(2)}, u32[]{:S(2)}) collective-permute-start(f32[8,128]{1,0:T(8,128)S(1)} %add.24), channel_id=1, source_target_pairs={{0,32},{16,48},{32,0},{48,16},{64,96},{80,112},{96,64},{112,80},{1... | collective-permute-start | bytes 12296 | tf_op jit(solution)/shard_map/ppermute | solution.py:490
  59.4 14.3 %collective-permute-start.13 = (f32[2,128,512]{2,1,0:T(8,128)S(1)}, f32[2,128,512]{2,1,0:T(8,128)S(1)}, u32[]{:S(2)}, u32[]{:S(2)}) collective-permute-start(f32[2,128,512]{2,1,0:T(8,128)S(1)} %get-tuple-element.69), channel_id=1, source_target_pairs={{0,96},{16,112},{32,64},{48,80},{64,32},{80,48},{96,0},{112,16},{1... | collective-permute-start | bytes 1572872 | tf_op jit(solution)/shard_map/ppermute | solution.py:490
  69.8 16.0 %collective-permute-start.10 = (f32[768,256]{1,0:T(8,128)S(1)}, f32[768,256]{1,0:T(8,128)S(1)}, u32[]{:S(2)}, u32[]{:S(2)}) collective-permute-start(f32[768,256]{1,0:T(8,128)S(1)} %get-tuple-element.61), channel_id=1, source_target_pairs={{0,1},{1,2},{2,3},{3,4},{4,5},{5,6},{6,7},{7,8},{8,9},{9,10},{10,1... | collective-permute-start | bytes 2359304 | tf_op jit(solution)/shard_map/ppermute | solution.py:485
  69.8 16.0 %collective-permute-start.11 = (f32[768,256]{1,0:T(8,128)S(1)}, f32[768,256]{1,0:T(8,128)S(1)}, u32[]{:S(2)}, u32[]{:S(2)}) collective-permute-start(f32[768,256]{1,0:T(8,128)S(1)} %get-tuple-element.62), channel_id=1, source_target_pairs={{0,15},{1,0},{2,1},{3,2},{4,3},{5,4},{6,5},{7,6},{8,7},{9,8},{10,9... | collective-permute-start | bytes 2359304 | tf_op jit(solution)/shard_map/ppermute | solution.py:485
  73.8 11.9 %collective-permute-start.14 = (f32[128,512]{1,0:T(8,128)S(1)}, f32[128,512]{1,0:T(8,128)S(1)}, u32[]{:S(2)}, u32[]{:S(2)}) collective-permute-start(f32[128,512]{1,0:T(8,128)S(1)} %get-tuple-element.71), channel_id=1, source_target_pairs={{0,96},{16,112},{32,64},{48,80},{64,32},{80,48},{96,0},{112,16},{1... | collective-permute-start | bytes 786440 | tf_op jit(solution)/shard_map/ppermute | solution.py:490
  76.6 9.1 %collective-permute-start.15 = (f32[128,512]{1,0:T(8,128)S(1)}, f32[128,512]{1,0:T(8,128)S(1)}, u32[]{:S(2)}, u32[]{:S(2)}) collective-permute-start(f32[128,512]{1,0:T(8,128)S(1)} %get-tuple-element.72), channel_id=1, source_target_pairs={{0,32},{16,48},{32,0},{48,16},{64,96},{80,112},{96,64},{112,80},{1... | collective-permute-start | bytes 786440 | tf_op jit(solution)/shard_map/ppermute | solution.py:490
  86.6 33.6 %collective-permute-start.16 = (f32[1280,256]{1,0:T(8,128)S(1)}, f32[1280,256]{1,0:T(8,128)S(1)}, u32[]{:S(2)}, u32[]{:S(2)}) collective-permute-start(f32[1280,256]{1,0:T(8,128)S(1)} %get-tuple-element.74), channel_id=1, source_target_pairs={{0,1},{1,2},{2,3},{3,4},{4,5},{5,6},{6,7},{7,8},{8,9},{9,10},{10,1... | collective-permute-start | bytes 3932168 | tf_op jit(solution)/shard_map/ppermute | solution.py:485
  86.6 33.6 %collective-permute-start.17 = (f32[1280,256]{1,0:T(8,128)S(1)}, f32[1280,256]{1,0:T(8,128)S(1)}, u32[]{:S(2)}, u32[]{:S(2)}) collective-permute-start(f32[1280,256]{1,0:T(8,128)S(1)} %get-tuple-element.75), channel_id=1, source_target_pairs={{0,15},{1,0},{2,1},{3,2},{4,3},{5,4},{6,5},{7,6},{8,7},{9,8},{10,9... | collective-permute-start | bytes 3932168 | tf_op jit(solution)/shard_map/ppermute | solution.py:485
  90.5 10.9 %collective-permute-start.19 = (f32[2,128,512]{2,1,0:T(8,128)S(1)}, f32[2,128,512]{2,1,0:T(8,128)S(1)}, u32[]{:S(2)}, u32[]{:S(2)}) collective-permute-start(f32[2,128,512]{2,1,0:T(8,128)S(1)} %get-tuple-element.78), channel_id=1, source_target_pairs={{0,32},{16,48},{32,0},{48,16},{64,96},{80,112},{96,64},{112,80},{1... | collective-permute-start | bytes 1572872 | tf_op jit(solution)/shard_map/ppermute | solution.py:490
  92.5 11.9 %collective-permute-start.20 = (f32[2,128,512]{2,1,0:T(8,128)S(1)}, f32[2,128,512]{2,1,0:T(8,128)S(1)}, u32[]{:S(2)}, u32[]{:S(2)}) collective-permute-start(f32[2,128,512]{2,1,0:T(8,128)S(1)} %get-tuple-element.80), channel_id=1, source_target_pairs={{0,96},{16,112},{32,64},{48,80},{64,32},{80,48},{96,0},{112,16},{1... | collective-permute-start | bytes 1572872 | tf_op jit(solution)/shard_map/ppermute | solution.py:490
  104.5 7.7 %collective-permute-start.21 = (f32[128,512]{1,0:T(8,128)S(1)}, f32[128,512]{1,0:T(8,128)S(1)}, u32[]{:S(2)}, u32[]{:S(2)}) collective-permute-start(f32[128,512]{1,0:T(8,128)S(1)} %get-tuple-element.82), channel_id=1, source_target_pairs={{0,96},{16,112},{32,64},{48,80},{64,32},{80,48},{96,0},{112,16},{1... | collective-permute-start | bytes 786440 | tf_op jit(solution)/shard_map/ppermute | solution.py:490
  105.1 7.1 %collective-permute-start.22 = (f32[128,512]{1,0:T(8,128)S(1)}, f32[128,512]{1,0:T(8,128)S(1)}, u32[]{:S(2)}, u32[]{:S(2)}) collective-permute-start(f32[128,512]{1,0:T(8,128)S(1)} %get-tuple-element.83), channel_id=1, source_target_pairs={{0,32},{16,48},{32,0},{48,16},{64,96},{80,112},{96,64},{112,80},{1... | collective-permute-start | bytes 786440 | tf_op jit(solution)/shard_map/ppermute | solution.py:490
  105.1 10.0 %collective-permute-start.18 = (f32[2,64,512]{2,1,0:T(8,128)S(1)}, f32[2,64,512]{2,1,0:T(8,128)S(1)}, u32[]{:S(2)}, u32[]{:S(2)}) collective-permute-start(f32[2,64,512]{2,1,0:T(8,128)S(1)} %get-tuple-element.76), channel_id=1, source_target_pairs={{0,16},{16,0},{32,48},{48,32},{64,80},{80,64},{96,112},{112,96},{1... | collective-permute-start | bytes 786440 | tf_op jit(solution)/shard_map/ppermute | solution.py:490
  112.3 8.0 %collective-permute-start.23 = (f32[2,64,512]{2,1,0:T(8,128)S(1)}, f32[2,64,512]{2,1,0:T(8,128)S(1)}, u32[]{:S(2)}, u32[]{:S(2)}) collective-permute-start(f32[2,64,512]{2,1,0:T(8,128)S(1)} %get-tuple-element.85), channel_id=1, source_target_pairs={{0,16},{16,0},{32,48},{48,32},{64,80},{80,64},{96,112},{112,96},{1... | collective-permute-start | bytes 786440 | tf_op jit(solution)/shard_map/ppermute | solution.py:490

commit v3 on v0

v3 whole, which is shorter than its diff:
```python
import functools

import jax
import jax.numpy as jnp
from jax import lax
from jax.experimental import pallas as pl
from jax.experimental.pallas import tpu as pltpu
from jax.sharding import PartitionSpec as P

BW = 256
STEPS = 2
READ = 256
CHUNK = 512
VMEM = 16 * 1024 * 1024

epsilon = 1e-06

in_vmem = pl.BlockSpec(memory_space=pltpu.VMEM)
in_smem = pl.BlockSpec(memory_space=pltpu.SMEM)
in_hbm = pl.BlockSpec(memory_space=pltpu.HBM)
anywhere = pl.BlockSpec(memory_space=pl.ANY)


def f32(*shape):
    return jax.ShapeDtypeStruct(shape, jnp.float32)


def bf16(*shape):
    return jax.ShapeDtypeStruct(shape, jnp.bfloat16)


def params(limit=VMEM):
    return pltpu.CompilerParams(vmem_limit_bytes=limit)


def cost(flops, nbytes):
    return pl.CostEstimate(flops=flops, bytes_accessed=nbytes, transcendentals=0)


def split(x):
    high = x.astype(jnp.bfloat16)
    low = (x - high.astype(jnp.float32)).astype(jnp.bfloat16)
    return high, low


def add_squares(acc, slot, x):
    rows, cols = x.shape
    for half in range(cols // 128):
        piece = x[:, half * 128 : (half + 1) * 128]
        acc[2 * slot + half] += jnp.sum((piece * piece).reshape(rows // 8, 8, 128), axis=0)


def put_sums(sums_ref, acc):
    for row in range(8):
        sums_ref[row : row + 1, :] = jnp.sum(acc[row], axis=0, keepdims=True)


def first_kernel(x_ref, high_ref, low_ref, sums_ref, x, sem, acc):
    rows = x_ref.shape[0]
    copies = []
    for i in range(rows // READ):
        here = pl.ds(i * READ, READ)
        copies.append(pltpu.make_async_copy(x_ref.at[here, :], x.at[here, :], sem.at[i]))
    for copy in copies:
        copy.start()
    acc[...] = jnp.zeros_like(acc)
    for i, copy in enumerate(copies):
        here = slice(i * READ, (i + 1) * READ)
        copy.wait()
        for slot in range(4):
            piece = x[here, slot * BW : (slot + 1) * BW]
            add_squares(acc, slot, piece)
            high_ref[slot, here, :], low_ref[slot, here, :] = split(piece)
    put_sums(sums_ref, acc)


def first(columns):
    rows, cols = columns.shape
    return pl.pallas_call(
        first_kernel,
        in_specs=[in_hbm],
        out_specs=[in_vmem] * 3,
        out_shape=[bf16(4, rows, BW), bf16(4, rows, BW), f32(8, 128)],
        scratch_shapes=[
            pltpu.VMEM((rows, cols), jnp.float32),
            pltpu.SemaphoreType.DMA((rows // READ,)),
            pltpu.VMEM((8, 8, 128), jnp.float32),
        ],
        compiler_params=params(44 * 1024 * 1024),
        cost_estimate=cost(1 << 10, 1 << 10),
        name="first",
    )(columns)


def scale_kernel(total_rows, step, plan_ref, here_ref, there_ref, rot_ref, *refs):
    out_ref, scratch = refs[-2:]
    sums = here_ref[...] + there_ref[...]
    scratch[...] = jnp.sqrt(jnp.float32(total_rows)) * lax.rsqrt(sums + epsilon)
    for k in range(4):
        pair, half = k // 2, k % 2
        for part in range(2):
            row = scratch[pl.ds(2 * plan_ref[step, 0, k] + part, 1), :]
            column = jnp.broadcast_to(row, (128, 128)).T
            top = half * BW + part * 128
            for c in range(4):
                lanes = slice(c * 128, (c + 1) * 128)
                h, l = split(rot_ref[step, pair, top : top + 128, lanes] * column)
                out_ref[pair, top : top + 128, lanes] = h
                out_ref[pair, 2 * BW + top : 2 * BW + top + 128, lanes] = h
                out_ref[pair, 4 * BW + top : 4 * BW + top + 128, lanes] = l


def scaled(total_rows, step, sums, rotations, plan, after=()):
    return pl.pallas_call(
        functools.partial(scale_kernel, total_rows, step),
        in_specs=[in_smem] + [in_vmem] * 3 + [anywhere] * len(after),
        out_specs=in_vmem,
        out_shape=bf16(2, 6 * BW, 2 * BW),
        scratch_shapes=[pltpu.VMEM((8, 128), jnp.float32)],
        compiler_params=params(),
        cost_estimate=cost(1 << 10, 1 << 10),
        name="scale",
    )(plan, *sums, rotations, *after)


def pieces(rows):
    count = -(-rows // CHUNK)
    return [(k * (rows // count), rows // count) for k in range(count)]


def stacked(high_ref, low_ref, plan_ref, step, pair, row, count):
    slots = [plan_ref[step, 0, 2 * pair + k] for k in range(2)]
    h = [high_ref[slot, row : row + count, :] for slot in slots]
    l = [low_ref[slot, row : row + count, :] for slot in slots]
    return jnp.concatenate(h + l + h, axis=1)


def half_gram(nh, nl):
    turned = nh.T
    return jnp.dot(
        jnp.concatenate([turned, turned], axis=1),
        jnp.concatenate([nh * jnp.bfloat16(0.5), nl], axis=0),
        preferred_element_type=jnp.float32,
    )


def cut_gram(total_rows, pair, gram_acc, mine, other):
    half = gram_acc[pair]
    gram_acc[pair] = (half + half.T) * jnp.float32(1.0 / total_rows)
    x = lax.axis_index("frame") // 2
    near = x + 1 - 2 * (x % 2)
    blocks = (((x, 3 - x), (near, 3 - near)), ((x, near), (3 - x, 3 - near)))[pair]
    for ref, rows in zip((mine, other), blocks):
        for k in range(2):
            row = pl.multiple_of(128 * rows[k], 128)
            ref[k] = gram_acc[pair, pl.ds(row, 128), :]


def send_kernel(plan_ref, high_ref, low_ref, rot_ref, up, down, up_sums, down_sums, acc):
    acc[...] = jnp.zeros_like(acc)
    for r, count in pieces(up.shape[0]):
        for pair, sent in enumerate((up, down)):
            x = stacked(high_ref, low_ref, plan_ref, 0, pair, r, count)
            new = jnp.dot(x, rot_ref[pair, :, BW:], preferred_element_type=jnp.float32)
            sent[r : r + count, :] = new
            add_squares(acc, pair, new)
    for pair, sums in enumerate((up_sums, down_sums)):
        for half in range(2):
            sums[:, half * 128 : (half + 1) * 128] = acc[2 * pair + half]


def send(plan, high, low, rot):
    rows = high.shape[1]
    return pl.pallas_call(
        send_kernel,
        in_specs=[in_smem] + [in_vmem] * 3,
        out_specs=[in_vmem] * 4,
        out_shape=[f32(rows, BW)] * 2 + [f32(8, BW)] * 2,
        scratch_shapes=[pltpu.VMEM((4, 8, 128), jnp.float32)],
        compiler_params=params(),
        cost_estimate=cost(1 << 10, 1 << 10),
        name="send",
    )(plan, high, low, rot)


def stay_kernel(plan_ref, high_ref, low_ref, rot_ref, kept_high, kept_low, sums_ref, acc):
    acc[...] = jnp.zeros_like(acc)
    for r, count in pieces(high_ref.shape[1]):
        for pair in range(2):
            x = stacked(high_ref, low_ref, plan_ref, 0, pair, r, count)
            new = jnp.dot(x, rot_ref[pair, :, :BW], preferred_element_type=jnp.float32)
            h, l = split(new)
            kept_high[pair, r : r + count, :] = h
            kept_low[pair, r : r + count, :] = l
            add_squares(acc, pair, new)
    for row in range(4):
        sums_ref[row : row + 1, :] = jnp.sum(acc[row], axis=0, keepdims=True)
    sums_ref[4:8] = jnp.zeros((4, 128), jnp.float32)


def stay(plan, high, low, rot):
    rows = high.shape[1]
    *kept, sums = pl.pallas_call(
        stay_kernel,
        in_specs=[in_smem] + [in_vmem] * 3,
        out_specs=[in_vmem] * 3,
        out_shape=[bf16(2, rows, BW)] * 2 + [f32(8, 128)],
        scratch_shapes=[pltpu.VMEM((4, 8, 128), jnp.float32)],
        compiler_params=params(),
        cost_estimate=cost(1 << 10, 1 << 10),
        name="stay",
    )(plan, high, low, rot)
    return kept, sums


def gram_kernel(total_rows, kept_high, kept_low, up, down, *refs):
    outs, gram_acc = refs[:4], refs[4]
    for r, count in pieces(up.shape[0]):
        here = slice(r, r + count)
        for pair, sent in enumerate((up, down)):
            h, l = split(sent[here, :])
            gram = half_gram(
                jnp.concatenate([kept_high[pair, here, :], h], axis=1),
                jnp.concatenate([kept_low[pair, here, :], l], axis=1),
            )
            gram_acc[pair] = gram + gram_acc[pair] if r else gram
    for pair in range(2):
        cut_gram(total_rows, pair, gram_acc, *outs[2 * pair : 2 * pair + 2])


def gram(total_rows, kept, up, down):
    outs = pl.pallas_call(
        functools.partial(gram_kernel, total_rows),
        in_specs=[in_vmem] * 4,
        out_specs=[in_vmem] * 4,
        out_shape=[f32(2, 128, 2 * BW)] * 4,
        scratch_shapes=[pltpu.VMEM((2, 2 * BW, 2 * BW), jnp.float32)],
        compiler_params=params(),
        cost_estimate=cost(1 << 10, 1 << 10),
        name="gram",
    )(*kept, up, down)
    return outs[:2], outs[2:]


def send_again_kernel(plan_ref, kept_high, kept_low, up_in, down_in, rot_ref, _,
                      out_up, out_down, high_ref, low_ref):
    for slot in range(2):
        high_ref[slot] = kept_high[slot]
        low_ref[slot] = kept_low[slot]
    high_ref[2], low_ref[2] = split(up_in[...])
    high_ref[3], low_ref[3] = split(down_in[...])
    for r, count in pieces(up_in.shape[0]):
        for pair, sent in enumerate((out_up, out_down)):
            x = stacked(high_ref, low_ref, plan_ref, 1, pair, r, count)
            sent[r : r + count, :] = jnp.dot(
                x, rot_ref[pair, :, BW:], preferred_element_type=jnp.float32
            )


def send_again(plan, kept, up, down, rot, after):
    rows = up.shape[0]
    return pl.pallas_call(
        send_again_kernel,
        in_specs=[in_smem] + [in_vmem] * 5 + [anywhere],
        out_specs=[in_vmem] * 4,
        out_shape=[f32(rows, BW)] * 2 + [bf16(4, rows, BW)] * 2,
        compiler_params=params(),
        cost_estimate=cost(1 << 10, 1 << 10),
        name="send_again",
    )(plan, *kept, up, down, rot, after)


def stay_again_kernel(total_rows, plan_ref, high_ref, low_ref, rot_ref, up, down, result, *refs):
    outs, (gram_acc, kept_ref, sem) = refs[:4], refs[4:]
    copies = []
    for k, (r, count) in enumerate(pieces(up.shape[0])):
        here = slice(r, r + count)
        for pair, sent in enumerate((up, down)):
            x = stacked(high_ref, low_ref, plan_ref, 1, pair, r, count)
            new = jnp.dot(x, rot_ref[pair, :, :BW], preferred_element_type=jnp.float32)
            kept_ref[here, pair * BW : (pair + 1) * BW] = new
            h, l = split(new)
            sent_h, sent_l = split(sent[here, :])
            gram = half_gram(
                jnp.concatenate([h, sent_h], axis=1), jnp.concatenate([l, sent_l], axis=1)
            )
            gram_acc[pair] = gram + gram_acc[pair] if r else gram
        copies.append(
            pltpu.make_async_copy(
                kept_ref.at[pl.ds(r, count), :],
                result.at[pl.ds(r, count), pl.ds(0, 2 * BW)],
                sem.at[k],
            )
        )
        copies[-1].start()
    for pair in range(2):
        cut_gram(total_rows, pair, gram_acc, *outs[2 * pair : 2 * pair + 2])
    for copy in copies:
        copy.wait()


def stay_again(total_rows, plan, high, low, rot, up, down):
    rows = up.shape[0]
    result, *outs = pl.pallas_call(
        functools.partial(stay_again_kernel, total_rows),
        in_specs=[in_smem] + [in_vmem] * 5,
        out_specs=[in_hbm] + [in_vmem] * 4,
        out_shape=[f32(rows, 4 * BW)] + [f32(2, 128, 2 * BW)] * 4,
        scratch_shapes=[
            pltpu.VMEM((2, 2 * BW, 2 * BW), jnp.float32),
            pltpu.VMEM((rows, 2 * BW), jnp.float32),
            pltpu.SemaphoreType.DMA((len(pieces(rows)),)),
        ],
        compiler_params=params(),
        cost_estimate=cost(1 << 10, 1 << 10),
        name="stay_again",
    )(plan, high, low, rot, up, down)
    return result, (outs[:2], outs[2:])


def mix_kernel(own, before, after, out):
    out[0:4] = own[0:4]
    for k, ref in enumerate((before, after)):
        for half in range(2):
            row = 4 + 2 * k + half
            lanes = slice(half * 128, (half + 1) * 128)
            out[row : row + 1, :] = jnp.sum(ref[:, lanes], axis=0, keepdims=True)


def mix(own, before, after):
    return pl.pallas_call(
        mix_kernel,
        in_specs=[in_vmem] * 3,
        out_specs=in_vmem,
        out_shape=f32(8, 128),
        compiler_params=params(),
        cost_estimate=cost(1 << 10, 1 << 10),
        name="mix",
    )(own, before, after)


def add_kernel(mine, got, *refs):
    keep_ref, send_ref = refs[-2:]
    keep_ref[...] = mine[0] + got[0]
    send_ref[...] = mine[1] + got[1]


def add_first(mine, got, after):
    return pl.pallas_call(
        add_kernel,
        in_specs=[in_vmem] * 2 + [anywhere] * len(after),
        out_specs=[in_vmem] * 2,
        out_shape=[f32(128, 2 * BW)] * 2,
        compiler_params=params(),
        cost_estimate=cost(1 << 10, 1 << 10),
        name="add",
    )(mine, got, *after)


def halve_kernel(mine0, got0, mine1, got1, keep_ref, send_ref):
    bit = lax.axis_index("frame") % 2
    for pair, (mine, got) in enumerate(((mine0, got0), (mine1, got1))):
        for ref, chosen in ((keep_ref, bit), (send_ref, 1 - bit)):
            rows = pl.ds(pl.multiple_of(64 * chosen, 64), 64)
            ref[pair] = mine[rows, :] + got[rows, :]


def halve(mine0, got0, mine1, got1):
    return pl.pallas_call(
        halve_kernel,
        in_specs=[in_vmem] * 4,
        out_specs=[in_vmem] * 2,
        out_shape=[f32(2, 64, 2 * BW)] * 2,
        compiler_params=params(),
        cost_estimate=cost(1 << 10, 1 << 10),
        name="halve",
    )(mine0, got0, mine1, got1)


def fill_kernel(_, up, down, out, done, sem):
    copies = [
        pltpu.make_async_copy(ref, out.at[:, pl.ds((2 + k) * BW, BW)], sem.at[k])
        for k, ref in enumerate((up, down))
    ]
    for copy in copies:
        copy.start()
    done[...] = jnp.zeros_like(done)
    for copy in copies:
        copy.wait()


def fill(out, up, down):
    return pl.pallas_call(
        fill_kernel,
        in_specs=[in_hbm, in_vmem, in_vmem],
        out_specs=[in_hbm, in_vmem],
        out_shape=[jax.ShapeDtypeStruct(out.shape, out.dtype), f32(8, 128)],
        input_output_aliases={0: 0},
        scratch_shapes=[pltpu.SemaphoreType.DMA((2,))],
        compiler_params=params(),
        cost_estimate=cost(1 << 10, 1 << 10),
        name="fill",
    )(out, up, down)


def finish_kernel(*refs):
    out = refs[-1]
    for step in range(STEPS):
        mine, got = refs[2 * step], refs[2 * step + 1]
        for pair in range(2):
            out[step, :, pair, :] = mine[pair] + got[pair]


def finish(pieces, after):
    args = [array for piece in pieces for array in piece]
    return pl.pallas_call(
        finish_kernel,
        in_specs=[in_vmem] * len(args) + [anywhere],
        out_specs=in_vmem,
        out_shape=f32(STEPS, 64, 2, 2 * BW),
        compiler_params=params(),
        cost_estimate=cost(1 << 10, 1 << 10),
        name="finish",
    )(*args, after)


def shift(x, by):
    size = lax.axis_size("pair")
    return lax.ppermute(x, "pair", [(i, (i + by) % size) for i in range(size)])


def swap(x, bit):
    size = lax.axis_size("frame")
    return lax.ppermute(x, "frame", [(i, i ^ bit) for i in range(size)])


def shift_aside(x, by):
    frames, holders = lax.axis_size("frame"), lax.axis_size("pair")
    pairs = [
        (f * holders + h, (f ^ 6) * holders + (h + by) % holders)
        for f in range(frames)
        for h in range(holders)
    ]
    return lax.ppermute(x, ("frame", "pair"), pairs)


def all_sum(x, across):
    x = (x + swap(x, 2)) + (swap(x, 6) + swap(x, 4))
    return x, swap(x, across)


NEAR = ((2, 6), (6, 2))


def begin_sum(halves, after=()):
    return [
        add_first(mine, swap(other, NEAR[pair][0]), after)
        for pair, (mine, other) in enumerate(halves)
    ]


def end_sum(begun):
    args = [(kept, swap(sent, NEAR[pair][1])) for pair, (kept, sent) in enumerate(begun)]
    mine, other = halve(*args[0], *args[1])
    return mine, swap(other, 1)


def local(columns, rotations, plan):
    total_rows = columns.shape[0] * lax.axis_size("frame")
    high, low, sums = first(columns)
    rot = scaled(total_rows, 0, all_sum(sums, 1), rotations, plan)
    up, down, up_sums, down_sums = send(plan, high, low, rot)
    moved = shift(up, 1), shift(down, -1)
    kept, own = stay(plan, high, low, rot)
    mixed = mix(own, shift_aside(up_sums, 1), shift_aside(down_sums, -1))
    halves = gram(total_rows, kept, up, down)
    rot = scaled(total_rows, 1, all_sum(mixed, 7), rotations, plan, (halves[0][0],))
    up, down, high, low = send_again(plan, kept, *moved, rot, halves[0][0])
    moved = shift(up, 1), shift(down, -1)
    result, halves_again = stay_again(total_rows, plan, high, low, rot, up, down)
    first_grams = end_sum(begin_sum(halves, (halves_again[0][0],)))
    last_grams = end_sum(begin_sum(halves_again))
    result, done = fill(result, *moved)
    return result, finish((first_grams, last_grams), done)


def solution(mesh):
    in_specs = (P("frame", "pair"), P(None, "pair", None, None), P(None, "pair", None))
    out_specs = (P("frame", "pair"), P(None, "frame", "pair", None))
    return jax.shard_map(local, mesh=mesh, in_specs=in_specs, out_specs=out_specs, check_vma=False)
```

time: 564 us -> 110 us (0.20)
  the two profiles are of different devices: /device:TPU:12 before, /device:TPU:104 now
where the time goes in v3:
time: 110 us; the launch traced here: 109 us
  Pallas kernels  37.9 us (34%)
  waiting for transfers between devices  35.6 us (32%)
  starting transfers between devices  35.1 us (32%)
    ppermute x18, waiting for transfers between devices, swap(): return lax.ppermute(x, 'frame', [(i, i ^ bit) for i in range(size)])  34.9 us
    ppermute x18, starting transfers between devices, swap(): return lax.ppermute(x, 'frame', [(i, i ^ bit) for i in range(size)])  27.5 us
    pallas_call x1, Pallas kernels, stay_again(): pl.pallas_call(functools.partial(stay_again_kernel, total_rows), in_specs...  10.3 us
    pallas_call x1, Pallas kernels, send_again(): pl.pallas_call(send_again_kernel, in_specs=[in_smem] + [in_vmem] * 5 + [a...  5.3 us
    pallas_call x1, Pallas kernels, gram(): pl.pallas_call(functools.partial(gram_kernel, total_rows), in_specs=[in_v...  4.94 us
    pallas_call x1, Pallas kernels, stay(): pl.pallas_call(stay_kernel, in_specs=[in_smem] + [in_vmem] * 3, out_specs...  4.06 us
    pallas_call x1, Pallas kernels, send(): pl.pallas_call(send_kernel, in_specs=[in_smem] + [in_vmem] * 3, out_specs...  3.97 us
    ppermute x2, starting transfers between devices, shift_aside(): return lax.ppermute(x, ('frame', 'pair'), pairs)  3.86 us
  transfers between devices with their start and end apart: 24, of which 14 were waited for; matrix products, arithmetic and copies ran while one was open for 0% of the time, Pallas kernels for 21%

profile of v3, /device:TPU:104, one launch (start us, length us, event | category | flops | bytes accessed | tf_op | source)
XLA Modules:
  0.0 109.4 jit_solution(9532315310597948777)
XLA Ops:
  0.6 3.8 %first.1 = (bf16[4,2048,256]{2,1,0:T(8,128)(2,1)S(1)}, bf16[4,2048,256]{2,1,0:T(8,128)(2,1)S(1)}, f32[8,128]{1,0:T(8,128)S(1)}) custom-call(f32[2048,1024]{1,0:T(8,128)} %x_ref.1), custom_call_target="tpu_custom_call" | custom-call | flops 1024 | bytes 1024 | tf_op jit(solution)/shard_map/first/pallas_call | solution.py:79
  4.5 3.1 %collective-permute-start.2 = (f32[8,128]{1,0:T(8,128)S(1)}, f32[8,128]{1,0:T(8,128)S(1)}, u32[]{:S(2)}, u32[]{:S(2)}) collective-permute-start(f32[8,128]{1,0:T(8,128)S(1)} %get-tuple-element.41), channel_id=1, source_target_pairs={{0,64},{16,80},{32,96},{48,112},{64,0},{80,16},{96,32},{112,48},{1... | collective-permute-start | bytes 12296 | tf_op jit(solution)/shard_map/ppermute | solution.py:434
  7.6 1.1 %collective-permute-start.1 = (f32[8,128]{1,0:T(8,128)S(1)}, f32[8,128]{1,0:T(8,128)S(1)}, u32[]{:S(2)}, u32[]{:S(2)}) collective-permute-start(f32[8,128]{1,0:T(8,128)S(1)} %get-tuple-element.41), channel_id=1, source_target_pairs={{0,96},{16,112},{32,64},{48,80},{64,32},{80,48},{96,0},{112,16},{1... | collective-permute-start | bytes 12296 | tf_op jit(solution)/shard_map/ppermute | solution.py:434
  8.7 0.0 collective-permute-start
  8.7 0.9 collective-permute-done.2
  9.7 2.7 %collective-permute-done.1 = f32[8,128]{1,0:T(8,128)S(1)} collective-permute-done((f32[8,128]{1,0:T(8,128)S(1)}, f32[8,128]{1,0:T(8,128)S(1)}, u32[]{:S(2)}, u32[]{:S(2)}) %collective-permute-start.1) | collective-permute-done | bytes 4128 | tf_op jit(solution)/shard_map/ppermute | solution.py:434
  12.4 0.0 collective-permute-done
  12.4 2.4 %collective-permute-start.3 = (f32[8,128]{1,0:T(8,128)S(1)}, f32[8,128]{1,0:T(8,128)S(1)}, u32[]{:S(2)}, u32[]{:S(2)}) collective-permute-start(f32[8,128]{1,0:T(8,128)S(1)} %add_add_fusion.1.here_ref), channel_id=1, source_target_pairs={{0,16},{16,0},{32,48},{48,32},{64,80},{80,64},{96,112},{112,96},{1... | collective-permute-start | bytes 12296 | tf_op jit(solution)/shard_map/ppermute | solution.py:434
  14.8 2.8 %collective-permute-done.3.there_ref = f32[8,128]{1,0:T(8,128)S(1)} collective-permute-done((f32[8,128]{1,0:T(8,128)S(1)}, f32[8,128]{1,0:T(8,128)S(1)}, u32[]{:S(2)}, u32[]{:S(2)}) %collective-permute-start.3) | collective-permute-done | bytes 4128 | tf_op jit(solution)/shard_map/ppermute | solution.py:434
  17.6 1.1 scale.2.rot_ref
  18.7 4.0 %send.1 = (f32[2048,256]{1,0:T(8,128)S(1)}, f32[2048,256]{1,0:T(8,128)S(1)}, f32[8,256]{1,0:T(8,128)S(1)}, f32[8,256]{1,0:T(8,128)S(1)}) custom-call(s32[2,1,4]{2,1,0:T(1,128)S(1)} %copy-done.1, bf16[4,2048,256]{2,1,0:T(8,128)(2,1)S(1)} %get-tuple-element.39.high_ref, bf16[4,2048,256]{2,1,0:T(8,128)(2,1)S(1)} %get-tuple-element.40.low_ref, ...), custom_call_target="tpu_custom_call" | custom-call | flops 1024 | bytes 1024 | tf_op jit(solution)/shard_map/send/pallas_call | solution.py:174
  22.7 0.1 collective-permute-start.4
  22.8 1.7 %collective-permute-start.5 = (f32[2048,256]{1,0:T(8,128)S(1)}, f32[2048,256]{1,0:T(8,128)S(1)}, u32[]{:S(2)}, u32[]{:S(2)}) collective-permute-start(f32[2048,256]{1,0:T(8,128)S(1)} %get-tuple-element.45.down), channel_id=1, source_target_pairs={{0,15},{1,0},{2,1},{3,2},{4,3},{5,4},{6,5},{7,6},{8,7},{9,8},{10,9... | collective-permute-start | bytes 6291464 | tf_op jit(solution)/shard_map/ppermute | solution.py:429
  24.5 0.4 collective-permute-start.6
  24.9 3.5 %collective-permute-start.7 = (f32[8,256]{1,0:T(8,128)S(1)}, f32[8,256]{1,0:T(8,128)S(1)}, u32[]{:S(2)}, u32[]{:S(2)}) collective-permute-start(f32[8,256]{1,0:T(8,128)S(1)} %get-tuple-element.48), channel_id=1, source_target_pairs={{0,111},{1,96},{2,97},{3,98},{4,99},{5,100},{6,101},{7,102},{8,103... | collective-permute-start | bytes 24584 | tf_op jit(solution)/shard_map/ppermute | solution.py:444
  28.4 4.1 %stay.1 = (bf16[2,2048,256]{2,1,0:T(8,128)(2,1)S(1)}, bf16[2,2048,256]{2,1,0:T(8,128)(2,1)S(1)}, f32[8,128]{1,0:T(8,128)S(1)}) custom-call(s32[2,1,4]{2,1,0:T(1,128)S(1)} %copy-done.1, bf16[4,2048,256]{2,1,0:T(8,128)(2,1)S(1)} %get-tuple-element.39.high_ref, bf16[4,2048,256]{2,1,0:T(8,128)(2,1)S(1)} %get-tuple-element.40.low_ref, ...), custom_call_target="tpu_custom_call" | custom-call | flops 1024 | bytes 1024 | tf_op jit(solution)/shard_map/stay/pallas_call | solution.py:203
  32.4 0.0 collective-permute-done.6.before
  32.4 0.0 collective-permute-done.7.after
  32.5 0.2 collective-permute-start.10
  32.7 1.9 %collective-permute-start.9 = (f32[8,128]{1,0:T(8,128)S(1)}, f32[8,128]{1,0:T(8,128)S(1)}, u32[]{:S(2)}, u32[]{:S(2)}) collective-permute-start(f32[8,128]{1,0:T(8,128)S(1)} %mix.1), channel_id=1, source_target_pairs={{0,96},{16,112},{32,64},{48,80},{64,32},{80,48},{96,0},{112,16},{1... | collective-permute-start | bytes 12296 | tf_op jit(solution)/shard_map/ppermute | solution.py:434
  34.6 1.5 %collective-permute-start.8 = (f32[8,128]{1,0:T(8,128)S(1)}, f32[8,128]{1,0:T(8,128)S(1)}, u32[]{:S(2)}, u32[]{:S(2)}) collective-permute-start(f32[8,128]{1,0:T(8,128)S(1)} %mix.1), channel_id=1, source_target_pairs={{0,32},{16,48},{32,0},{48,16},{64,96},{80,112},{96,64},{112,80},{1... | collective-permute-start | bytes 12296 | tf_op jit(solution)/shard_map/ppermute | solution.py:434
  36.0 1.6 %collective-permute-done.10 = f32[8,128]{1,0:T(8,128)S(1)} collective-permute-done((f32[8,128]{1,0:T(8,128)S(1)}, f32[8,128]{1,0:T(8,128)S(1)}, u32[]{:S(2)}, u32[]{:S(2)}) %collective-permute-start.10) | collective-permute-done | bytes 4128 | tf_op jit(solution)/shard_map/ppermute | solution.py:434
  37.7 0.0 collective-permute-done.9
  37.7 0.5 collective-permute-done.8
  38.2 3.4 %collective-permute-start.11 = (f32[8,128]{1,0:T(8,128)S(1)}, f32[8,128]{1,0:T(8,128)S(1)}, u32[]{:S(2)}, u32[]{:S(2)}) collective-permute-start(f32[8,128]{1,0:T(8,128)S(1)} %add_add_fusion.here_ref), channel_id=1, source_target_pairs={{0,112},{16,96},{32,80},{48,64},{64,48},{80,32},{96,16},{112,0},{1... | collective-permute-start | bytes 12296 | tf_op jit(solution)/shard_map/ppermute | solution.py:434
  41.6 4.9 %gram.1 = (f32[2,128,512]{2,1,0:T(8,128)S(1)}, f32[2,128,512]{2,1,0:T(8,128)S(1)}, f32[2,128,512]{2,1,0:T(8,128)S(1)}, f32[2,128,512]{2,1,0:T(8,128)S(1)}) custom-call(bf16[2,2048,256]{2,1,0:T(8,128)(2,1)S(1)} %get-tuple-element.42.kept_high, bf16[2,2048,256]{2,1,0:T(8,128)(2,1)S(1)} %get-tuple-element.43.kept_low, f32[2048,256]{1,0:T(8,128)S(1)} %get-tuple-element.44.up, ...), custom_call_target="tpu_custom_call" | custom-call | flops 1024 | bytes 1024 | tf_op jit(solution)/shard_map/gram/pallas_call | solution.py:232
  46.6 0.0 collective-permute-done.11.there_ref
  46.6 1.1 scale.3.rot_ref
  47.6 0.7 collective-permute-done.4.up_in
  48.3 0.0 collective-permute-done.5.down_in
  48.3 5.3 %send_again.1 = (f32[2048,256]{1,0:T(8,128)S(1)}, f32[2048,256]{1,0:T(8,128)S(1)}, bf16[4,2048,256]{2,1,0:T(8,128)(2,1)S(1)}, bf16[4,2048,256]{2,1,0:T(8,128)(2,1)S(1)}) custom-call(s32[2,1,4]{2,1,0:T(1,128)S(1)} %copy-done.1, bf16[2,2048,256]{2,1,0:T(8,128)(2,1)S(1)} %get-tuple-element.42.kept_high, bf16[2,2048,256]{2,1,0:T(8,128)(2,1)S(1)} %get-tuple-element.43.kept_low, ...), custom_call_target="tpu_custom_call" | custom-call | flops 1024 | bytes 1024 | tf_op jit(solution)/shard_map/send_again/pallas_call | solution.py:262
  53.6 1.5 %collective-permute-start.12 = (f32[2048,256]{1,0:T(8,128)S(1)}, f32[2048,256]{1,0:T(8,128)S(1)}, u32[]{:S(2)}, u32[]{:S(2)}) collective-permute-start(f32[2048,256]{1,0:T(8,128)S(1)} %get-tuple-element.52.up), channel_id=1, source_target_pairs={{0,1},{1,2},{2,3},{3,4},{4,5},{5,6},{6,7},{7,8},{8,9},{9,10},{10,1... | collective-permute-start | bytes 6291464 | tf_op jit(solution)/shard_map/ppermute | solution.py:429
  55.1 0.4 collective-permute-start.13
  55.5 1.9 %collective-permute-start.16 = (f32[2,128,512]{2,1,0:T(8,128)S(1)}, f32[2,128,512]{2,1,0:T(8,128)S(1)}, u32[]{:S(2)}, u32[]{:S(2)}) collective-permute-start(f32[2,128,512]{2,1,0:T(8,128)S(1)} %get-tuple-element.61), channel_id=1, source_target_pairs={{0,96},{16,112},{32,64},{48,80},{64,32},{80,48},{96,0},{112,16},{1... | collective-permute-start | bytes 1572872 | tf_op jit(solution)/shard_map/ppermute | solution.py:434
  57.4 0.0 collective-permute-start.14
  57.5 10.3 %stay_again.1 = (f32[2048,1024]{1,0:T(8,128)}, f32[2,128,512]{2,1,0:T(8,128)S(1)}, f32[2,128,512]{2,1,0:T(8,128)S(1)}, f32[2,128,512]{2,1,0:T(8,128)S(1)}, f32[2,128,512]{2,1,0:T(8,128)S(1)}) custom-call(s32[2,1,4]{2,1,0:T(1,128)S(1)} %copy-done.1, bf16[4,2048,256]{2,1,0:T(8,128)(2,1)S(1)} %get-tuple-element.50.high_ref, ...), custom_call_target="tpu_custom_call" | custom-call | flops 1024 | bytes 1024 | tf_op jit(solution)/shard_map/stay_again/pallas_call | solution.py:304
  67.8 2.1 %collective-permute-start.19 = (f32[2,128,512]{2,1,0:T(8,128)S(1)}, f32[2,128,512]{2,1,0:T(8,128)S(1)}, u32[]{:S(2)}, u32[]{:S(2)}) collective-permute-start(f32[2,128,512]{2,1,0:T(8,128)S(1)} %get-tuple-element.66), channel_id=1, source_target_pairs={{0,32},{16,48},{32,0},{48,16},{64,96},{80,112},{96,64},{112,80},{1... | collective-permute-start | bytes 1572872 | tf_op jit(solution)/shard_map/ppermute | solution.py:434
  69.9 0.7 collective-permute-done.16.got
  70.6 2.4 %collective-permute-start.21 = (f32[2,128,512]{2,1,0:T(8,128)S(1)}, f32[2,128,512]{2,1,0:T(8,128)S(1)}, u32[]{:S(2)}, u32[]{:S(2)}) collective-permute-start(f32[2,128,512]{2,1,0:T(8,128)S(1)} %get-tuple-element.70), channel_id=1, source_target_pairs={{0,96},{16,112},{32,64},{48,80},{64,32},{80,48},{96,0},{112,16},{1... | collective-permute-start | bytes 1572872 | tf_op jit(solution)/shard_map/ppermute | solution.py:434
  73.0 0.1 add.35
  73.1 0.0 collective-permute-done.14.got
  73.1 0.1 collective-permute-start.17
  73.2 0.1 add.34
  73.3 10.0 %collective-permute-done.19.got = f32[2,128,512]{2,1,0:T(8,128)S(1)} collective-permute-done((f32[2,128,512]{2,1,0:T(8,128)S(1)}, f32[2,128,512]{2,1,0:T(8,128)S(1)}, u32[]{:S(2)}, u32[]{:S(2)}) %collective-permute-start.19) | collective-permute-done | bytes 524320 | tf_op jit(solution)/shard_map/ppermute | solution.py:434
  83.3 1.0 collective-permute-start.15
  84.2 0.1 add.36
  84.3 2.1 %collective-permute-done.21.got = f32[2,128,512]{2,1,0:T(8,128)S(1)} collective-permute-done((f32[2,128,512]{2,1,0:T(8,128)S(1)}, f32[2,128,512]{2,1,0:T(8,128)S(1)}, u32[]{:S(2)}, u32[]{:S(2)}) %collective-permute-start.21) | collective-permute-done | bytes 524320 | tf_op jit(solution)/shard_map/ppermute | solution.py:434
  86.4 1.9 %collective-permute-start.20 = (f32[128,512]{1,0:T(8,128)S(1)}, f32[128,512]{1,0:T(8,128)S(1)}, u32[]{:S(2)}, u32[]{:S(2)}) collective-permute-start(f32[128,512]{1,0:T(8,128)S(1)} %get-tuple-element.68), channel_id=1, source_target_pairs={{0,96},{16,112},{32,64},{48,80},{64,32},{80,48},{96,0},{112,16},{1... | collective-permute-start | bytes 786440 | tf_op jit(solution)/shard_map/ppermute | solution.py:434
  88.3 0.1 add.37
  88.4 0.5 collective-permute-done.17.got1
  88.9 1.4 %collective-permute-start.22 = (f32[128,512]{1,0:T(8,128)S(1)}, f32[128,512]{1,0:T(8,128)S(1)}, u32[]{:S(2)}, u32[]{:S(2)}) collective-permute-start(f32[128,512]{1,0:T(8,128)S(1)} %get-tuple-element.72), channel_id=1, source_target_pairs={{0,32},{16,48},{32,0},{48,16},{64,96},{80,112},{96,64},{112,80},{1... | collective-permute-start | bytes 786440 | tf_op jit(solution)/shard_map/ppermute | solution.py:434
  90.3 3.3 %collective-permute-done.15.got0 = f32[128,512]{1,0:T(8,128)S(1)} collective-permute-done((f32[128,512]{1,0:T(8,128)S(1)}, f32[128,512]{1,0:T(8,128)S(1)}, u32[]{:S(2)}, u32[]{:S(2)}) %collective-permute-start.15) | collective-permute-done | bytes 262176 | tf_op jit(solution)/shard_map/ppermute | solution.py:434
  93.6 0.1 halve.2
  93.6 2.6 %collective-permute-start.18 = (f32[2,64,512]{2,1,0:T(8,128)S(1)}, f32[2,64,512]{2,1,0:T(8,128)S(1)}, u32[]{:S(2)}, u32[]{:S(2)}) collective-permute-start(f32[2,64,512]{2,1,0:T(8,128)S(1)} %get-tuple-element.65), channel_id=1, source_target_pairs={{0,16},{16,0},{32,48},{48,32},{64,80},{80,64},{96,112},{112,96},{1... | collective-permute-start | bytes 786440 | tf_op jit(solution)/shard_map/ppermute | solution.py:434
  96.2 2.6 %collective-permute-done.20.got0 = f32[128,512]{1,0:T(8,128)S(1)} collective-permute-done((f32[128,512]{1,0:T(8,128)S(1)}, f32[128,512]{1,0:T(8,128)S(1)}, u32[]{:S(2)}, u32[]{:S(2)}) %collective-permute-start.20) | collective-permute-done | bytes 262176 | tf_op jit(solution)/shard_map/ppermute | solution.py:434
  98.9 0.0 collective-permute-done.22.got1
  98.9 0.1 halve.3
  98.9 0.5 collective-permute-start.23
  99.4 0.0 collective-permute-done.12.up
  99.4 0.0 collective-permute-done.13.down
  99.4 2.0 %fill.1 = (f32[2048,1024]{1,0:T(8,128)}, f32[8,128]{1,0:T(8,128)S(1)}) custom-call(f32[2048,1024]{1,0:T(8,128)} %get-tuple-element.54._, f32[2048,256]{1,0:T(8,128)S(1)} %collective-permute-done.12.up, f32[2048,256]{1,0:T(8,128)S(1)} %collective-permute-done.13.down), custom_call_target="tpu_custom_call", output_to_operand_aliasing={{0}: (0, {})} | custom-call | flops 1024 | bytes 1024 | tf_op jit(solution)/shard_map/fill/pallas_call | solution.py:393
  101.5 1.4 %collective-permute-done.18.refs_1_ = f32[2,64,512]{2,1,0:T(8,128)S(1)} collective-permute-done((f32[2,64,512]{2,1,0:T(8,128)S(1)}, f32[2,64,512]{2,1,0:T(8,128)S(1)}, u32[]{:S(2)}, u32[]{:S(2)}) %collective-permute-start.18) | collective-permute-done | bytes 262176 | tf_op jit(solution)/shard_map/ppermute | solution.py:434
  102.9 5.6 %collective-permute-done.23.refs_3_ = f32[2,64,512]{2,1,0:T(8,128)S(1)} collective-permute-done((f32[2,64,512]{2,1,0:T(8,128)S(1)}, f32[2,64,512]{2,1,0:T(8,128)S(1)}, u32[]{:S(2)}, u32[]{:S(2)}) %collective-permute-start.23) | collective-permute-done | bytes 262176 | tf_op jit(solution)/shard_map/ppermute | solution.py:434
  108.5 0.9 finish.1
  (7 shorter events, 0.0 us)
Async XLA Ops:
  0.6 17.0 %copy-start.1 = (s32[2,1,4]{2,1,0:T(1,128)S(1)}, s32[2,1,4]{2,1,0:T(1,128)}, u32[]{:S(2)}) copy-start(s32[2,1,4]{2,1,0:T(1,128)} %plan_ref.11) | copy-start | bytes 100
  0.6 17.0 %copy-start = (f32[2,2,512,512]{3,2,1,0:T(8,128)S(1)}, f32[2,2,512,512]{3,2,1,0:T(8,128)}, u32[]{:S(2)}) copy-start(f32[2,2,512,512]{3,2,1,0:T(8,128)} %rot_ref.3) | copy-start | bytes 12582916
  4.5 5.2 %collective-permute-start.2 = (f32[8,128]{1,0:T(8,128)S(1)}, f32[8,128]{1,0:T(8,128)S(1)}, u32[]{:S(2)}, u32[]{:S(2)}) collective-permute-start(f32[8,128]{1,0:T(8,128)S(1)} %get-tuple-element.41), channel_id=1, source_target_pairs={{0,64},{16,80},{32,96},{48,112},{64,0},{80,16},{96,32},{112,48},{1... | collective-permute-start | bytes 12296 | tf_op jit(solution)/shard_map/ppermute | solution.py:434
  7.6 4.8 %collective-permute-start.1 = (f32[8,128]{1,0:T(8,128)S(1)}, f32[8,128]{1,0:T(8,128)S(1)}, u32[]{:S(2)}, u32[]{:S(2)}) collective-permute-start(f32[8,128]{1,0:T(8,128)S(1)} %get-tuple-element.41), channel_id=1, source_target_pairs={{0,96},{16,112},{32,64},{48,80},{64,32},{80,48},{96,0},{112,16},{1... | collective-permute-start | bytes 12296 | tf_op jit(solution)/shard_map/ppermute | solution.py:434
  8.7 3.7 %collective-permute-start = (f32[8,128]{1,0:T(8,128)S(1)}, f32[8,128]{1,0:T(8,128)S(1)}, u32[]{:S(2)}, u32[]{:S(2)}) collective-permute-start(f32[8,128]{1,0:T(8,128)S(1)} %get-tuple-element.41), channel_id=1, source_target_pairs={{0,32},{16,48},{32,0},{48,16},{64,96},{80,112},{96,64},{112,80},{1... | collective-permute-start | bytes 12296 | tf_op jit(solution)/shard_map/ppermute | solution.py:434
  12.4 5.2 %collective-permute-start.3 = (f32[8,128]{1,0:T(8,128)S(1)}, f32[8,128]{1,0:T(8,128)S(1)}, u32[]{:S(2)}, u32[]{:S(2)}) collective-permute-start(f32[8,128]{1,0:T(8,128)S(1)} %add_add_fusion.1.here_ref), channel_id=1, source_target_pairs={{0,16},{16,0},{32,48},{48,32},{64,80},{80,64},{96,112},{112,96},{1... | collective-permute-start | bytes 12296 | tf_op jit(solution)/shard_map/ppermute | solution.py:434
  22.7 25.6 %collective-permute-start.4 = (f32[2048,256]{1,0:T(8,128)S(1)}, f32[2048,256]{1,0:T(8,128)S(1)}, u32[]{:S(2)}, u32[]{:S(2)}) collective-permute-start(f32[2048,256]{1,0:T(8,128)S(1)} %get-tuple-element.44.up), channel_id=1, source_target_pairs={{0,1},{1,2},{2,3},{3,4},{4,5},{5,6},{6,7},{7,8},{8,9},{9,10},{10,1... | collective-permute-start | bytes 6291464 | tf_op jit(solution)/shard_map/ppermute | solution.py:429
  22.8 25.5 %collective-permute-start.5 = (f32[2048,256]{1,0:T(8,128)S(1)}, f32[2048,256]{1,0:T(8,128)S(1)}, u32[]{:S(2)}, u32[]{:S(2)}) collective-permute-start(f32[2048,256]{1,0:T(8,128)S(1)} %get-tuple-element.45.down), channel_id=1, source_target_pairs={{0,15},{1,0},{2,1},{3,2},{4,3},{5,4},{6,5},{7,6},{8,7},{9,8},{10,9... | collective-permute-start | bytes 6291464 | tf_op jit(solution)/shard_map/ppermute | solution.py:429
  24.5 7.9 %collective-permute-start.6 = (f32[8,256]{1,0:T(8,128)S(1)}, f32[8,256]{1,0:T(8,128)S(1)}, u32[]{:S(2)}, u32[]{:S(2)}) collective-permute-start(f32[8,256]{1,0:T(8,128)S(1)} %get-tuple-element.47), channel_id=1, source_target_pairs={{0,97},{1,98},{2,99},{3,100},{4,101},{5,102},{6,103},{7,104},{8,10... | collective-permute-start | bytes 24584 | tf_op jit(solution)/shard_map/ppermute | solution.py:444
  24.9 7.5 %collective-permute-start.7 = (f32[8,256]{1,0:T(8,128)S(1)}, f32[8,256]{1,0:T(8,128)S(1)}, u32[]{:S(2)}, u32[]{:S(2)}) collective-permute-start(f32[8,256]{1,0:T(8,128)S(1)} %get-tuple-element.48), channel_id=1, source_target_pairs={{0,111},{1,96},{2,97},{3,98},{4,99},{5,100},{6,101},{7,102},{8,103... | collective-permute-start | bytes 24584 | tf_op jit(solution)/shard_map/ppermute | solution.py:444
  32.5 5.2 %collective-permute-start.10 = (f32[8,128]{1,0:T(8,128)S(1)}, f32[8,128]{1,0:T(8,128)S(1)}, u32[]{:S(2)}, u32[]{:S(2)}) collective-permute-start(f32[8,128]{1,0:T(8,128)S(1)} %mix.1), channel_id=1, source_target_pairs={{0,64},{16,80},{32,96},{48,112},{64,0},{80,16},{96,32},{112,48},{1... | collective-permute-start | bytes 12296 | tf_op jit(solution)/shard_map/ppermute | solution.py:434
  32.7 4.9 %collective-permute-start.9 = (f32[8,128]{1,0:T(8,128)S(1)}, f32[8,128]{1,0:T(8,128)S(1)}, u32[]{:S(2)}, u32[]{:S(2)}) collective-permute-start(f32[8,128]{1,0:T(8,128)S(1)} %mix.1), channel_id=1, source_target_pairs={{0,96},{16,112},{32,64},{48,80},{64,32},{80,48},{96,0},{112,16},{1... | collective-permute-start | bytes 12296 | tf_op jit(solution)/shard_map/ppermute | solution.py:434
  34.6 3.6 %collective-permute-start.8 = (f32[8,128]{1,0:T(8,128)S(1)}, f32[8,128]{1,0:T(8,128)S(1)}, u32[]{:S(2)}, u32[]{:S(2)}) collective-permute-start(f32[8,128]{1,0:T(8,128)S(1)} %mix.1), channel_id=1, source_target_pairs={{0,32},{16,48},{32,0},{48,16},{64,96},{80,112},{96,64},{112,80},{1... | collective-permute-start | bytes 12296 | tf_op jit(solution)/shard_map/ppermute | solution.py:434
  38.2 8.4 %collective-permute-start.11 = (f32[8,128]{1,0:T(8,128)S(1)}, f32[8,128]{1,0:T(8,128)S(1)}, u32[]{:S(2)}, u32[]{:S(2)}) collective-permute-start(f32[8,128]{1,0:T(8,128)S(1)} %add_add_fusion.here_ref), channel_id=1, source_target_pairs={{0,112},{16,96},{32,80},{48,64},{64,48},{80,32},{96,16},{112,0},{1... | collective-permute-start | bytes 12296 | tf_op jit(solution)/shard_map/ppermute | solution.py:434
  53.6 45.8 %collective-permute-start.12 = (f32[2048,256]{1,0:T(8,128)S(1)}, f32[2048,256]{1,0:T(8,128)S(1)}, u32[]{:S(2)}, u32[]{:S(2)}) collective-permute-start(f32[2048,256]{1,0:T(8,128)S(1)} %get-tuple-element.52.up), channel_id=1, source_target_pairs={{0,1},{1,2},{2,3},{3,4},{4,5},{5,6},{6,7},{7,8},{8,9},{9,10},{10,1... | collective-permute-start | bytes 6291464 | tf_op jit(solution)/shard_map/ppermute | solution.py:429
  55.1 44.4 %collective-permute-start.13 = (f32[2048,256]{1,0:T(8,128)S(1)}, f32[2048,256]{1,0:T(8,128)S(1)}, u32[]{:S(2)}, u32[]{:S(2)}) collective-permute-start(f32[2048,256]{1,0:T(8,128)S(1)} %get-tuple-element.53.down), channel_id=1, source_target_pairs={{0,15},{1,0},{2,1},{3,2},{4,3},{5,4},{6,5},{7,6},{8,7},{9,8},{10,9... | collective-permute-start | bytes 6291464 | tf_op jit(solution)/shard_map/ppermute | solution.py:429
  55.5 15.1 %collective-permute-start.16 = (f32[2,128,512]{2,1,0:T(8,128)S(1)}, f32[2,128,512]{2,1,0:T(8,128)S(1)}, u32[]{:S(2)}, u32[]{:S(2)}) collective-permute-start(f32[2,128,512]{2,1,0:T(8,128)S(1)} %get-tuple-element.61), channel_id=1, source_target_pairs={{0,96},{16,112},{32,64},{48,80},{64,32},{80,48},{96,0},{112,16},{1... | collective-permute-start | bytes 1572872 | tf_op jit(solution)/shard_map/ppermute | solution.py:434
  57.4 15.6 %collective-permute-start.14 = (f32[2,128,512]{2,1,0:T(8,128)S(1)}, f32[2,128,512]{2,1,0:T(8,128)S(1)}, u32[]{:S(2)}, u32[]{:S(2)}) collective-permute-start(f32[2,128,512]{2,1,0:T(8,128)S(1)} %get-tuple-element.56), channel_id=1, source_target_pairs={{0,32},{16,48},{32,0},{48,16},{64,96},{80,112},{96,64},{112,80},{1... | collective-permute-start | bytes 1572872 | tf_op jit(solution)/shard_map/ppermute | solution.py:434
  67.8 15.5 %collective-permute-start.19 = (f32[2,128,512]{2,1,0:T(8,128)S(1)}, f32[2,128,512]{2,1,0:T(8,128)S(1)}, u32[]{:S(2)}, u32[]{:S(2)}) collective-permute-start(f32[2,128,512]{2,1,0:T(8,128)S(1)} %get-tuple-element.66), channel_id=1, source_target_pairs={{0,32},{16,48},{32,0},{48,16},{64,96},{80,112},{96,64},{112,80},{1... | collective-permute-start | bytes 1572872 | tf_op jit(solution)/shard_map/ppermute | solution.py:434
  70.6 15.7 %collective-permute-start.21 = (f32[2,128,512]{2,1,0:T(8,128)S(1)}, f32[2,128,512]{2,1,0:T(8,128)S(1)}, u32[]{:S(2)}, u32[]{:S(2)}) collective-permute-start(f32[2,128,512]{2,1,0:T(8,128)S(1)} %get-tuple-element.70), channel_id=1, source_target_pairs={{0,96},{16,112},{32,64},{48,80},{64,32},{80,48},{96,0},{112,16},{1... | collective-permute-start | bytes 1572872 | tf_op jit(solution)/shard_map/ppermute | solution.py:434
  73.1 15.8 %collective-permute-start.17 = (f32[128,512]{1,0:T(8,128)S(1)}, f32[128,512]{1,0:T(8,128)S(1)}, u32[]{:S(2)}, u32[]{:S(2)}) collective-permute-start(f32[128,512]{1,0:T(8,128)S(1)} %get-tuple-element.63), channel_id=1, source_target_pairs={{0,32},{16,48},{32,0},{48,16},{64,96},{80,112},{96,64},{112,80},{1... | collective-permute-start | bytes 786440 | tf_op jit(solution)/shard_map/ppermute | solution.py:434
  83.3 10.3 %collective-permute-start.15 = (f32[128,512]{1,0:T(8,128)S(1)}, f32[128,512]{1,0:T(8,128)S(1)}, u32[]{:S(2)}, u32[]{:S(2)}) collective-permute-start(f32[128,512]{1,0:T(8,128)S(1)} %get-tuple-element.59), channel_id=1, source_target_pairs={{0,96},{16,112},{32,64},{48,80},{64,32},{80,48},{96,0},{112,16},{1... | collective-permute-start | bytes 786440 | tf_op jit(solution)/shard_map/ppermute | solution.py:434
  86.4 12.5 %collective-permute-start.20 = (f32[128,512]{1,0:T(8,128)S(1)}, f32[128,512]{1,0:T(8,128)S(1)}, u32[]{:S(2)}, u32[]{:S(2)}) collective-permute-start(f32[128,512]{1,0:T(8,128)S(1)} %get-tuple-element.68), channel_id=1, source_target_pairs={{0,96},{16,112},{32,64},{48,80},{64,32},{80,48},{96,0},{112,16},{1... | collective-permute-start | bytes 786440 | tf_op jit(solution)/shard_map/ppermute | solution.py:434
  88.9 10.0 %collective-permute-start.22 = (f32[128,512]{1,0:T(8,128)S(1)}, f32[128,512]{1,0:T(8,128)S(1)}, u32[]{:S(2)}, u32[]{:S(2)}) collective-permute-start(f32[128,512]{1,0:T(8,128)S(1)} %get-tuple-element.72), channel_id=1, source_target_pairs={{0,32},{16,48},{32,0},{48,16},{64,96},{80,112},{96,64},{112,80},{1... | collective-permute-start | bytes 786440 | tf_op jit(solution)/shard_map/ppermute | solution.py:434
  93.6 9.3 %collective-permute-start.18 = (f32[2,64,512]{2,1,0:T(8,128)S(1)}, f32[2,64,512]{2,1,0:T(8,128)S(1)}, u32[]{:S(2)}, u32[]{:S(2)}) collective-permute-start(f32[2,64,512]{2,1,0:T(8,128)S(1)} %get-tuple-element.65), channel_id=1, source_target_pairs={{0,16},{16,0},{32,48},{48,32},{64,80},{80,64},{96,112},{112,96},{1... | collective-permute-start | bytes 786440 | tf_op jit(solution)/shard_map/ppermute | solution.py:434
  98.9 9.6 %collective-permute-start.23 = (f32[2,64,512]{2,1,0:T(8,128)S(1)}, f32[2,64,512]{2,1,0:T(8,128)S(1)}, u32[]{:S(2)}, u32[]{:S(2)}) collective-permute-start(f32[2,64,512]{2,1,0:T(8,128)S(1)} %get-tuple-element.74), channel_id=1, source_target_pairs={{0,16},{16,0},{32,48},{48,32},{64,80},{80,64},{96,112},{112,96},{1... | collective-permute-start | bytes 786440 | tf_op jit(solution)/shard_map/ppermute | solution.py:434

commit v4 on v3

--- a/solution.py
+++ b/solution.py
@@ -11,6 +11,7 @@
 STEPS = 2
 READ = 256
 CHUNK = 512
+LONG = 512
 VMEM = 16 * 1024 * 1024
 
 epsilon = 1e-06
@@ -123,8 +124,8 @@
     )(plan, *sums, rotations, *after)
 
 
-def pieces(rows):
-    count = -(-rows // CHUNK)
+def pieces(rows, longest=CHUNK):
+    count = -(-rows // longest)
     return [(k * (rows // count), rows // count) for k in range(count)]
 
 
@@ -273,7 +274,7 @@
 def stay_again_kernel(total_rows, plan_ref, high_ref, low_ref, rot_ref, up, down, result, *refs):
     outs, (gram_acc, kept_ref, sem) = refs[:4], refs[4:]
     copies = []
-    for k, (r, count) in enumerate(pieces(up.shape[0])):
+    for k, (r, count) in enumerate(pieces(up.shape[0], LONG)):
         here = slice(r, r + count)
         for pair, sent in enumerate((up, down)):
             x = stacked(high_ref, low_ref, plan_ref, 1, pair, r, count)
@@ -309,7 +310,7 @@
         scratch_shapes=[
             pltpu.VMEM((2, 2 * BW, 2 * BW), jnp.float32),
             pltpu.VMEM((rows, 2 * BW), jnp.float32),
-            pltpu.SemaphoreType.DMA((len(pieces(rows)),)),
+            pltpu.SemaphoreType.DMA((len(pieces(rows, LONG)),)),
         ],
         compiler_params=params(),
         cost_estimate=cost(1 << 10, 1 << 10),
@@ -375,6 +376,44 @@
         cost_estimate=cost(1 << 10, 1 << 10),
         name="halve",
     )(mine0, got0, mine1, got1)
+
+
+def halve_early_kernel(mine0, got0, mine1, got1, _, keep_ref, send_ref):
+    bit = lax.axis_index("frame") % 2
+    for pair, (mine, got) in enumerate(((mine0, got0), (mine1, got1))):
+        for ref, chosen in ((keep_ref, bit), (send_ref, 1 - bit)):
+            rows = pl.ds(pl.multiple_of(64 * chosen, 64), 64)
+            ref[pair] = mine[:, rows, :] + got[:, rows, :]
+
+
+def halve_early(args, after):
+    return pl.pallas_call(
+        halve_early_kernel,
+        in_specs=[in_vmem] * 4 + [anywhere],
+        out_specs=[in_vmem] * 2,
+        out_shape=[f32(2, 2, 64, 2 * BW)] * 2,
+        compiler_params=params(),
+        cost_estimate=cost(1 << 10, 1 << 10),
+        name="halve_early",
+    )(*args, after)
+
+
+def pass_on_kernel(mine, got, keep_ref, send0, send1):
+    for pair, sent in enumerate((send0, send1)):
+        keep_ref[pair] = mine[pair, 0] + got[pair, 0]
+        sent[...] = mine[pair, 1] + got[pair, 1]
+
+
+def pass_on(mine, got):
+    return pl.pallas_call(
+        pass_on_kernel,
+        in_specs=[in_vmem] * 2,
+        out_specs=[in_vmem] * 3,
+        out_shape=[f32(2, 64, 2 * BW), f32(64, 2 * BW), f32(64, 2 * BW)],
+        compiler_params=params(),
+        cost_estimate=cost(1 << 10, 1 << 10),
+        name="pass_on",
+    )(mine, got)
 
 
 def fill_kernel(_, up, down, out, done, sem):
@@ -403,25 +442,22 @@
     )(out, up, down)
 
 
-def finish_kernel(*refs):
-    out = refs[-1]
-    for step in range(STEPS):
-        mine, got = refs[2 * step], refs[2 * step + 1]
-        for pair in range(2):
-            out[step, :, pair, :] = mine[pair] + got[pair]
-
-
-def finish(pieces, after):
-    args = [array for piece in pieces for array in piece]
+def finish_kernel(first_mine, first_got0, first_got1, last_mine, last_got, _, out):
+    for pair, got in enumerate((first_got0, first_got1)):
+        out[0, :, pair, :] = first_mine[pair] + got[...]
+        out[1, :, pair, :] = last_mine[pair] + last_got[pair]
+
+
+def finish(first_grams, last_grams, after):
     return pl.pallas_call(
         finish_kernel,
-        in_specs=[in_vmem] * len(args) + [anywhere],
+        in_specs=[in_vmem] * 5 + [anywhere],
         out_specs=in_vmem,
         out_shape=f32(STEPS, 64, 2, 2 * BW),
         compiler_params=params(),
         cost_estimate=cost(1 << 10, 1 << 10),
         name="finish",
-    )(*args, after)
+    )(*first_grams, *last_grams, after)
 
 
 def shift(x, by):
@@ -452,17 +488,22 @@
 NEAR = ((2, 6), (6, 2))
 
 
-def begin_sum(halves, after=()):
-    return [
-        add_first(mine, swap(other, NEAR[pair][0]), after)
-        for pair, (mine, other) in enumerate(halves)
-    ]
-
-
-def end_sum(begun):
-    args = [(kept, swap(sent, NEAR[pair][1])) for pair, (kept, sent) in enumerate(begun)]
-    mine, other = halve(*args[0], *args[1])
+def last_sum(halves):
+    args = []
+    for (mine, other), (here, there) in zip(halves, NEAR):
+        kept, sent = add_first(mine, swap(other, here), ())
+        args += [kept, swap(sent, there)]
+    mine, other = halve(*args)
     return mine, swap(other, 1)
+
+
+def first_sum(halves, after):
+    args = []
+    for (mine, other), (here, _) in zip(halves, NEAR):
+        args += [mine, swap(other, here)]
+    mine, other = halve_early(args, after)
+    mine, *sent = pass_on(mine, swap(other, 1))
+    return mine, swap(sent[0], NEAR[0][1]), swap(sent[1], NEAR[1][1])
 
 
 def local(columns, rotations, plan):
@@ -478,10 +519,10 @@
     up, down, high, low = send_again(plan, kept, *moved, rot, halves[0][0])
     moved = shift(up, 1), shift(down, -1)
     result, halves_again = stay_again(total_rows, plan, high, low, rot, up, down)
-    first_grams = end_sum(begin_sum(halves, (halves_again[0][0],)))
-    last_grams = end_sum(begin_sum(halves_again))
+    first_grams = first_sum(halves, halves_again[0][0])
+    last_grams = last_sum(halves_again)
     result, done = fill(result, *moved)
-    return result, finish((first_grams, last_grams), done)
+    return result, finish(first_grams, last_grams, done)
 
 
 def solution(mesh):

time: 110 us -> 109 us (level)
  the two profiles are of different devices: /device:TPU:104 before, /device:TPU:0 now
where the time goes in v4:
time: 109 us
  starting transfers between devices  41.9 us (38%)
  Pallas kernels  37.9 us (35%)
  waiting for transfers between devices  28.5 us (26%)
    ppermute x18, waiting for transfers between devices, swap(): return lax.ppermute(x, 'frame', [(i, i ^ bit) for i in range(size)])  28.5 us
    ppermute x18, starting transfers between devices, swap(): return lax.ppermute(x, 'frame', [(i, i ^ bit) for i in range(size)])  28.1 us
    pallas_call x1, Pallas kernels, stay_again(): pl.pallas_call(functools.partial(stay_again_kernel, total_rows), in_specs...  10.3 us
    ppermute x4, starting transfers between devices, shift(): return lax.ppermute(x, 'pair', [(i, (i + by) % size) for i in range(size)])  7.83 us
    ppermute x2, starting transfers between devices, shift_aside(): return lax.ppermute(x, ('frame', 'pair'), pairs)  5.96 us
    pallas_call x1, Pallas kernels, send_again(): pl.pallas_call(send_again_kernel, in_specs=[in_smem] + [in_vmem] * 5 + [a...  5.34 us
    pallas_call x1, Pallas kernels, gram(): pl.pallas_call(functools.partial(gram_kernel, total_rows), in_specs=[in_v...  4.94 us
    pallas_call x1, Pallas kernels, stay(): pl.pallas_call(stay_kernel, in_specs=[in_smem] + [in_vmem] * 3, out_specs...  4.06 us
  transfers between devices with their start and end apart: 24, of which 12 were waited for; matrix products, arithmetic and copies ran while one was open for 0% of the time, Pallas kernels for 21%

profile of v4, /device:TPU:0, one launch (start us, length us, event | category | flops | bytes accessed | tf_op | source)
XLA Modules:
  0.0 109.1 jit_solution(12895344109764662572)
XLA Ops:
  0.6 0.0 copy-start.1
  0.6 3.8 %first.1 = (bf16[4,2048,256]{2,1,0:T(8,128)(2,1)S(1)}, bf16[4,2048,256]{2,1,0:T(8,128)(2,1)S(1)}, f32[8,128]{1,0:T(8,128)S(1)}) custom-call(f32[2048,1024]{1,0:T(8,128)} %x_ref.1), custom_call_target="tpu_custom_call" | custom-call | flops 1024 | bytes 1024 | tf_op jit(solution)/shard_map/first/pallas_call | solution.py:80
  4.5 3.2 %collective-permute-start.2 = (f32[8,128]{1,0:T(8,128)S(1)}, f32[8,128]{1,0:T(8,128)S(1)}, u32[]{:S(2)}, u32[]{:S(2)}) collective-permute-start(f32[8,128]{1,0:T(8,128)S(1)} %get-tuple-element.40), channel_id=1, source_target_pairs={{0,64},{16,80},{32,96},{48,112},{64,0},{80,16},{96,32},{112,48},{1... | collective-permute-start | bytes 12296 | tf_op jit(solution)/shard_map/ppermute | solution.py:470
  7.7 1.1 %collective-permute-start.1 = (f32[8,128]{1,0:T(8,128)S(1)}, f32[8,128]{1,0:T(8,128)S(1)}, u32[]{:S(2)}, u32[]{:S(2)}) collective-permute-start(f32[8,128]{1,0:T(8,128)S(1)} %get-tuple-element.40), channel_id=1, source_target_pairs={{0,96},{16,112},{32,64},{48,80},{64,32},{80,48},{96,0},{112,16},{1... | collective-permute-start | bytes 12296 | tf_op jit(solution)/shard_map/ppermute | solution.py:470
  8.8 0.0 collective-permute-start
  8.8 0.9 collective-permute-done.2
  9.7 2.8 %collective-permute-done.1 = f32[8,128]{1,0:T(8,128)S(1)} collective-permute-done((f32[8,128]{1,0:T(8,128)S(1)}, f32[8,128]{1,0:T(8,128)S(1)}, u32[]{:S(2)}, u32[]{:S(2)}) %collective-permute-start.1) | collective-permute-done | bytes 4128 | tf_op jit(solution)/shard_map/ppermute | solution.py:470
  12.5 0.0 collective-permute-done
  12.5 3.3 %collective-permute-start.3 = (f32[8,128]{1,0:T(8,128)S(1)}, f32[8,128]{1,0:T(8,128)S(1)}, u32[]{:S(2)}, u32[]{:S(2)}) collective-permute-start(f32[8,128]{1,0:T(8,128)S(1)} %add_add_fusion.1.here_ref), channel_id=1, source_target_pairs={{0,16},{16,0},{32,48},{48,32},{64,80},{80,64},{96,112},{112,96},{1... | collective-permute-start | bytes 12296 | tf_op jit(solution)/shard_map/ppermute | solution.py:470
  15.8 1.9 %collective-permute-done.3.there_ref = f32[8,128]{1,0:T(8,128)S(1)} collective-permute-done((f32[8,128]{1,0:T(8,128)S(1)}, f32[8,128]{1,0:T(8,128)S(1)}, u32[]{:S(2)}, u32[]{:S(2)}) %collective-permute-start.3) | collective-permute-done | bytes 4128 | tf_op jit(solution)/shard_map/ppermute | solution.py:470
  17.7 1.1 scale.2.rot_ref
  18.8 4.0 %send.1 = (f32[2048,256]{1,0:T(8,128)S(1)}, f32[2048,256]{1,0:T(8,128)S(1)}, f32[8,256]{1,0:T(8,128)S(1)}, f32[8,256]{1,0:T(8,128)S(1)}) custom-call(s32[2,1,4]{2,1,0:T(1,128)S(1)} %copy-done.1, bf16[4,2048,256]{2,1,0:T(8,128)(2,1)S(1)} %get-tuple-element.38.high_ref, bf16[4,2048,256]{2,1,0:T(8,128)(2,1)S(1)} %get-tuple-element.39.low_ref, ...), custom_call_target="tpu_custom_call" | custom-call | flops 1024 | bytes 1024 | tf_op jit(solution)/shard_map/send/pallas_call | solution.py:175
  22.8 0.1 collective-permute-start.4
  22.8 3.8 %collective-permute-start.5 = (f32[2048,256]{1,0:T(8,128)S(1)}, f32[2048,256]{1,0:T(8,128)S(1)}, u32[]{:S(2)}, u32[]{:S(2)}) collective-permute-start(f32[2048,256]{1,0:T(8,128)S(1)} %get-tuple-element.44.down), channel_id=1, source_target_pairs={{0,15},{1,0},{2,1},{3,2},{4,3},{5,4},{6,5},{7,6},{8,7},{9,8},{10,9... | collective-permute-start | bytes 6291464 | tf_op jit(solution)/shard_map/ppermute | solution.py:465
  26.7 0.0 collective-permute-start.6
  26.7 6.0 %collective-permute-start.7 = (f32[8,256]{1,0:T(8,128)S(1)}, f32[8,256]{1,0:T(8,128)S(1)}, u32[]{:S(2)}, u32[]{:S(2)}) collective-permute-start(f32[8,256]{1,0:T(8,128)S(1)} %get-tuple-element.47), channel_id=1, source_target_pairs={{0,111},{1,96},{2,97},{3,98},{4,99},{5,100},{6,101},{7,102},{8,103... | collective-permute-start | bytes 24584 | tf_op jit(solution)/shard_map/ppermute | solution.py:480
  32.7 4.1 %stay.1 = (bf16[2,2048,256]{2,1,0:T(8,128)(2,1)S(1)}, bf16[2,2048,256]{2,1,0:T(8,128)(2,1)S(1)}, f32[8,128]{1,0:T(8,128)S(1)}) custom-call(s32[2,1,4]{2,1,0:T(1,128)S(1)} %copy-done.1, bf16[4,2048,256]{2,1,0:T(8,128)(2,1)S(1)} %get-tuple-element.38.high_ref, bf16[4,2048,256]{2,1,0:T(8,128)(2,1)S(1)} %get-tuple-element.39.low_ref, ...), custom_call_target="tpu_custom_call" | custom-call | flops 1024 | bytes 1024 | tf_op jit(solution)/shard_map/stay/pallas_call | solution.py:204
  36.7 0.0 collective-permute-done.6.before
  36.7 0.0 collective-permute-done.7.after
  36.8 0.2 collective-permute-start.10
  37.0 1.9 %collective-permute-start.9 = (f32[8,128]{1,0:T(8,128)S(1)}, f32[8,128]{1,0:T(8,128)S(1)}, u32[]{:S(2)}, u32[]{:S(2)}) collective-permute-start(f32[8,128]{1,0:T(8,128)S(1)} %mix.1), channel_id=1, source_target_pairs={{0,96},{16,112},{32,64},{48,80},{64,32},{80,48},{96,0},{112,16},{1... | collective-permute-start | bytes 12296 | tf_op jit(solution)/shard_map/ppermute | solution.py:470
  38.9 1.5 %collective-permute-start.8 = (f32[8,128]{1,0:T(8,128)S(1)}, f32[8,128]{1,0:T(8,128)S(1)}, u32[]{:S(2)}, u32[]{:S(2)}) collective-permute-start(f32[8,128]{1,0:T(8,128)S(1)} %mix.1), channel_id=1, source_target_pairs={{0,32},{16,48},{32,0},{48,16},{64,96},{80,112},{96,64},{112,80},{1... | collective-permute-start | bytes 12296 | tf_op jit(solution)/shard_map/ppermute | solution.py:470
  40.3 1.6 %collective-permute-done.10 = f32[8,128]{1,0:T(8,128)S(1)} collective-permute-done((f32[8,128]{1,0:T(8,128)S(1)}, f32[8,128]{1,0:T(8,128)S(1)}, u32[]{:S(2)}, u32[]{:S(2)}) %collective-permute-start.10) | collective-permute-done | bytes 4128 | tf_op jit(solution)/shard_map/ppermute | solution.py:470
  42.0 0.0 collective-permute-done.9
  42.0 0.5 collective-permute-done.8
  42.5 4.3 %collective-permute-start.11 = (f32[8,128]{1,0:T(8,128)S(1)}, f32[8,128]{1,0:T(8,128)S(1)}, u32[]{:S(2)}, u32[]{:S(2)}) collective-permute-start(f32[8,128]{1,0:T(8,128)S(1)} %add_add_fusion.here_ref), channel_id=1, source_target_pairs={{0,112},{16,96},{32,80},{48,64},{64,48},{80,32},{96,16},{112,0},{1... | collective-permute-start | bytes 12296 | tf_op jit(solution)/shard_map/ppermute | solution.py:470
  46.8 4.9 %gram.1 = (f32[2,128,512]{2,1,0:T(8,128)S(1)}, f32[2,128,512]{2,1,0:T(8,128)S(1)}, f32[2,128,512]{2,1,0:T(8,128)S(1)}, f32[2,128,512]{2,1,0:T(8,128)S(1)}) custom-call(bf16[2,2048,256]{2,1,0:T(8,128)(2,1)S(1)} %get-tuple-element.41.kept_high, bf16[2,2048,256]{2,1,0:T(8,128)(2,1)S(1)} %get-tuple-element.42.kept_low, f32[2048,256]{1,0:T(8,128)S(1)} %get-tuple-element.43.up, ...), custom_call_target="tpu_custom_call" | custom-call | flops 1024 | bytes 1024 | tf_op jit(solution)/shard_map/gram/pallas_call | solution.py:233
  51.8 0.0 collective-permute-done.11.there_ref
  51.8 1.1 scale.3.rot_ref
  52.8 0.0 collective-permute-done.4.up_in
  52.9 0.0 collective-permute-done.5.down_in
  52.9 5.3 %send_again.1 = (f32[2048,256]{1,0:T(8,128)S(1)}, f32[2048,256]{1,0:T(8,128)S(1)}, bf16[4,2048,256]{2,1,0:T(8,128)(2,1)S(1)}, bf16[4,2048,256]{2,1,0:T(8,128)(2,1)S(1)}) custom-call(s32[2,1,4]{2,1,0:T(1,128)S(1)} %copy-done.1, bf16[2,2048,256]{2,1,0:T(8,128)(2,1)S(1)} %get-tuple-element.41.kept_high, bf16[2,2048,256]{2,1,0:T(8,128)(2,1)S(1)} %get-tuple-element.42.kept_low, ...), custom_call_target="tpu_custom_call" | custom-call | flops 1024 | bytes 1024 | tf_op jit(solution)/shard_map/send_again/pallas_call | solution.py:263
  58.2 0.1 collective-permute-start.12
  58.3 3.8 %collective-permute-start.13 = (f32[2048,256]{1,0:T(8,128)S(1)}, f32[2048,256]{1,0:T(8,128)S(1)}, u32[]{:S(2)}, u32[]{:S(2)}) collective-permute-start(f32[2048,256]{1,0:T(8,128)S(1)} %get-tuple-element.52.down), channel_id=1, source_target_pairs={{0,15},{1,0},{2,1},{3,2},{4,3},{5,4},{6,5},{7,6},{8,7},{9,8},{10,9... | collective-permute-start | bytes 6291464 | tf_op jit(solution)/shard_map/ppermute | solution.py:465
  62.1 1.1 %collective-permute-start.14 = (f32[2,128,512]{2,1,0:T(8,128)S(1)}, f32[2,128,512]{2,1,0:T(8,128)S(1)}, u32[]{:S(2)}, u32[]{:S(2)}) collective-permute-start(f32[2,128,512]{2,1,0:T(8,128)S(1)} %get-tuple-element.55), channel_id=1, source_target_pairs={{0,32},{16,48},{32,0},{48,16},{64,96},{80,112},{96,64},{112,80},{1... | collective-permute-start | bytes 1572872 | tf_op jit(solution)/shard_map/ppermute | solution.py:470
  63.2 1.3 %collective-permute-start.15 = (f32[2,128,512]{2,1,0:T(8,128)S(1)}, f32[2,128,512]{2,1,0:T(8,128)S(1)}, u32[]{:S(2)}, u32[]{:S(2)}) collective-permute-start(f32[2,128,512]{2,1,0:T(8,128)S(1)} %get-tuple-element.57), channel_id=1, source_target_pairs={{0,96},{16,112},{32,64},{48,80},{64,32},{80,48},{96,0},{112,16},{1... | collective-permute-start | bytes 1572872 | tf_op jit(solution)/shard_map/ppermute | solution.py:470
  64.5 10.3 %stay_again.1 = (f32[2048,1024]{1,0:T(8,128)}, f32[2,128,512]{2,1,0:T(8,128)S(1)}, f32[2,128,512]{2,1,0:T(8,128)S(1)}, f32[2,128,512]{2,1,0:T(8,128)S(1)}, f32[2,128,512]{2,1,0:T(8,128)S(1)}) custom-call(s32[2,1,4]{2,1,0:T(1,128)S(1)} %copy-done.1, bf16[4,2048,256]{2,1,0:T(8,128)(2,1)S(1)} %get-tuple-element.49.high_ref, ...), custom_call_target="tpu_custom_call" | custom-call | flops 1024 | bytes 1024 | tf_op jit(solution)/shard_map/stay_again/pallas_call | solution.py:305
  74.9 0.7 collective-permute-start.19
  75.5 0.0 collective-permute-done.14.got0
  75.5 1.7 %collective-permute-start.21 = (f32[2,128,512]{2,1,0:T(8,128)S(1)}, f32[2,128,512]{2,1,0:T(8,128)S(1)}, u32[]{:S(2)}, u32[]{:S(2)}) collective-permute-start(f32[2,128,512]{2,1,0:T(8,128)S(1)} %get-tuple-element.68), channel_id=1, source_target_pairs={{0,96},{16,112},{32,64},{48,80},{64,32},{80,48},{96,0},{112,16},{1... | collective-permute-start | bytes 1572872 | tf_op jit(solution)/shard_map/ppermute | solution.py:470
  77.2 0.0 collective-permute-done.15.got1
  77.2 0.1 halve_early.1
  77.3 1.3 %collective-permute-start.16 = (f32[2,2,64,512]{3,2,1,0:T(8,128)S(1)}, f32[2,2,64,512]{3,2,1,0:T(8,128)S(1)}, u32[]{:S(2)}, u32[]{:S(2)}) collective-permute-start(f32[2,2,64,512]{3,2,1,0:T(8,128)S(1)} %get-tuple-element.60), channel_id=1, source_target_pairs={{0,16},{16,0},{32,48},{48,32},{64,80},{80,64},{96,112},{112,96},{1... | collective-permute-start | bytes 1572872 | tf_op jit(solution)/shard_map/ppermute | solution.py:470
  78.6 6.5 %collective-permute-done.19.got = f32[2,128,512]{2,1,0:T(8,128)S(1)} collective-permute-done((f32[2,128,512]{2,1,0:T(8,128)S(1)}, f32[2,128,512]{2,1,0:T(8,128)S(1)}, u32[]{:S(2)}, u32[]{:S(2)}) %collective-permute-start.19) | collective-permute-done | bytes 524320 | tf_op jit(solution)/shard_map/ppermute | solution.py:470
  85.1 0.1 add.32
  85.2 2.7 %collective-permute-start.20 = (f32[128,512]{1,0:T(8,128)S(1)}, f32[128,512]{1,0:T(8,128)S(1)}, u32[]{:S(2)}, u32[]{:S(2)}) collective-permute-start(f32[128,512]{1,0:T(8,128)S(1)} %get-tuple-element.66), channel_id=1, source_target_pairs={{0,96},{16,112},{32,64},{48,80},{64,32},{80,48},{96,0},{112,16},{1... | collective-permute-start | bytes 786440 | tf_op jit(solution)/shard_map/ppermute | solution.py:470
  87.8 0.9 collective-permute-done.21.got
  88.7 0.1 add.33
  88.8 0.9 collective-permute-start.22
  89.7 3.2 %collective-permute-done.20.got0 = f32[128,512]{1,0:T(8,128)S(1)} collective-permute-done((f32[128,512]{1,0:T(8,128)S(1)}, f32[128,512]{1,0:T(8,128)S(1)}, u32[]{:S(2)}, u32[]{:S(2)}) %collective-permute-start.20) | collective-permute-done | bytes 262176 | tf_op jit(solution)/shard_map/ppermute | solution.py:470
  92.8 2.9 %collective-permute-done.22.got1 = f32[128,512]{1,0:T(8,128)S(1)} collective-permute-done((f32[128,512]{1,0:T(8,128)S(1)}, f32[128,512]{1,0:T(8,128)S(1)}, u32[]{:S(2)}, u32[]{:S(2)}) %collective-permute-start.22) | collective-permute-done | bytes 262176 | tf_op jit(solution)/shard_map/ppermute | solution.py:470
  95.8 0.1 halve.1
  95.8 1.3 %collective-permute-start.23 = (f32[2,64,512]{2,1,0:T(8,128)S(1)}, f32[2,64,512]{2,1,0:T(8,128)S(1)}, u32[]{:S(2)}, u32[]{:S(2)}) collective-permute-start(f32[2,64,512]{2,1,0:T(8,128)S(1)} %get-tuple-element.72), channel_id=1, source_target_pairs={{0,16},{16,0},{32,48},{48,32},{64,80},{80,64},{96,112},{112,96},{1... | collective-permute-start | bytes 786440 | tf_op jit(solution)/shard_map/ppermute | solution.py:470
  97.1 4.4 %collective-permute-done.16.got = f32[2,2,64,512]{3,2,1,0:T(8,128)S(1)} collective-permute-done((f32[2,2,64,512]{3,2,1,0:T(8,128)S(1)}, f32[2,2,64,512]{3,2,1,0:T(8,128)S(1)}, u32[]{:S(2)}, u32[]{:S(2)}) %collective-permute-start.16) | collective-permute-done | bytes 524320 | tf_op jit(solution)/shard_map/ppermute | solution.py:470
  101.4 0.1 pass_on.1
  101.5 1.8 %collective-permute-start.17 = (f32[64,512]{1,0:T(8,128)S(1)}, f32[64,512]{1,0:T(8,128)S(1)}, u32[]{:S(2)}, u32[]{:S(2)}) collective-permute-start(f32[64,512]{1,0:T(8,128)S(1)} %get-tuple-element.62), channel_id=1, source_target_pairs={{0,96},{16,112},{32,64},{48,80},{64,32},{80,48},{96,0},{112,16},{1... | collective-permute-start | bytes 393224 | tf_op jit(solution)/shard_map/ppermute | solution.py:470
  103.3 0.0 collective-permute-start.18
  103.3 0.0 collective-permute-done.12.up
  103.3 0.0 collective-permute-done.13.down
  103.3 2.0 %fill.1 = (f32[2048,1024]{1,0:T(8,128)}, f32[8,128]{1,0:T(8,128)S(1)}) custom-call(f32[2048,1024]{1,0:T(8,128)} %get-tuple-element.53._, f32[2048,256]{1,0:T(8,128)S(1)} %collective-permute-done.12.up, f32[2048,256]{1,0:T(8,128)S(1)} %collective-permute-done.13.down), custom_call_target="tpu_custom_call", output_to_operand_aliasing={{0}: (0, {})} | custom-call | flops 1024 | bytes 1024 | tf_op jit(solution)/shard_map/fill/pallas_call | solution.py:432
  105.3 2.4 %collective-permute-done.17.first_got0 = f32[64,512]{1,0:T(8,128)S(1)} collective-permute-done((f32[64,512]{1,0:T(8,128)S(1)}, f32[64,512]{1,0:T(8,128)S(1)}, u32[]{:S(2)}, u32[]{:S(2)}) %collective-permute-start.17) | collective-permute-done | bytes 131104 | tf_op jit(solution)/shard_map/ppermute | solution.py:470
  107.7 0.5 collective-permute-done.18.first_got1
  108.2 0.0 collective-permute-done.23.last_got
  108.2 0.9 finish.1
  (6 shorter events, 0.0 us)
Async XLA Ops:
  0.6 17.1 %copy-start.1 = (s32[2,1,4]{2,1,0:T(1,128)S(1)}, s32[2,1,4]{2,1,0:T(1,128)}, u32[]{:S(2)}) copy-start(s32[2,1,4]{2,1,0:T(1,128)} %plan_ref.11) | copy-start | bytes 100
  0.6 17.1 %copy-start = (f32[2,2,512,512]{3,2,1,0:T(8,128)S(1)}, f32[2,2,512,512]{3,2,1,0:T(8,128)}, u32[]{:S(2)}) copy-start(f32[2,2,512,512]{3,2,1,0:T(8,128)} %rot_ref.3) | copy-start | bytes 12582916
  4.5 5.2 %collective-permute-start.2 = (f32[8,128]{1,0:T(8,128)S(1)}, f32[8,128]{1,0:T(8,128)S(1)}, u32[]{:S(2)}, u32[]{:S(2)}) collective-permute-start(f32[8,128]{1,0:T(8,128)S(1)} %get-tuple-element.40), channel_id=1, source_target_pairs={{0,64},{16,80},{32,96},{48,112},{64,0},{80,16},{96,32},{112,48},{1... | collective-permute-start | bytes 12296 | tf_op jit(solution)/shard_map/ppermute | solution.py:470
  7.7 4.8 %collective-permute-start.1 = (f32[8,128]{1,0:T(8,128)S(1)}, f32[8,128]{1,0:T(8,128)S(1)}, u32[]{:S(2)}, u32[]{:S(2)}) collective-permute-start(f32[8,128]{1,0:T(8,128)S(1)} %get-tuple-element.40), channel_id=1, source_target_pairs={{0,96},{16,112},{32,64},{48,80},{64,32},{80,48},{96,0},{112,16},{1... | collective-permute-start | bytes 12296 | tf_op jit(solution)/shard_map/ppermute | solution.py:470
  8.8 3.7 %collective-permute-start = (f32[8,128]{1,0:T(8,128)S(1)}, f32[8,128]{1,0:T(8,128)S(1)}, u32[]{:S(2)}, u32[]{:S(2)}) collective-permute-start(f32[8,128]{1,0:T(8,128)S(1)} %get-tuple-element.40), channel_id=1, source_target_pairs={{0,32},{16,48},{32,0},{48,16},{64,96},{80,112},{96,64},{112,80},{1... | collective-permute-start | bytes 12296 | tf_op jit(solution)/shard_map/ppermute | solution.py:470
  12.5 5.2 %collective-permute-start.3 = (f32[8,128]{1,0:T(8,128)S(1)}, f32[8,128]{1,0:T(8,128)S(1)}, u32[]{:S(2)}, u32[]{:S(2)}) collective-permute-start(f32[8,128]{1,0:T(8,128)S(1)} %add_add_fusion.1.here_ref), channel_id=1, source_target_pairs={{0,16},{16,0},{32,48},{48,32},{64,80},{80,64},{96,112},{112,96},{1... | collective-permute-start | bytes 12296 | tf_op jit(solution)/shard_map/ppermute | solution.py:470
  22.8 30.1 %collective-permute-start.4 = (f32[2048,256]{1,0:T(8,128)S(1)}, f32[2048,256]{1,0:T(8,128)S(1)}, u32[]{:S(2)}, u32[]{:S(2)}) collective-permute-start(f32[2048,256]{1,0:T(8,128)S(1)} %get-tuple-element.43.up), channel_id=1, source_target_pairs={{0,1},{1,2},{2,3},{3,4},{4,5},{5,6},{6,7},{7,8},{8,9},{9,10},{10,1... | collective-permute-start | bytes 6291464 | tf_op jit(solution)/shard_map/ppermute | solution.py:465
  22.8 30.0 %collective-permute-start.5 = (f32[2048,256]{1,0:T(8,128)S(1)}, f32[2048,256]{1,0:T(8,128)S(1)}, u32[]{:S(2)}, u32[]{:S(2)}) collective-permute-start(f32[2048,256]{1,0:T(8,128)S(1)} %get-tuple-element.44.down), channel_id=1, source_target_pairs={{0,15},{1,0},{2,1},{3,2},{4,3},{5,4},{6,5},{7,6},{8,7},{9,8},{10,9... | collective-permute-start | bytes 6291464 | tf_op jit(solution)/shard_map/ppermute | solution.py:465
  26.7 10.0 %collective-permute-start.6 = (f32[8,256]{1,0:T(8,128)S(1)}, f32[8,256]{1,0:T(8,128)S(1)}, u32[]{:S(2)}, u32[]{:S(2)}) collective-permute-start(f32[8,256]{1,0:T(8,128)S(1)} %get-tuple-element.46), channel_id=1, source_target_pairs={{0,97},{1,98},{2,99},{3,100},{4,101},{5,102},{6,103},{7,104},{8,10... | collective-permute-start | bytes 24584 | tf_op jit(solution)/shard_map/ppermute | solution.py:480
  26.7 10.0 %collective-permute-start.7 = (f32[8,256]{1,0:T(8,128)S(1)}, f32[8,256]{1,0:T(8,128)S(1)}, u32[]{:S(2)}, u32[]{:S(2)}) collective-permute-start(f32[8,256]{1,0:T(8,128)S(1)} %get-tuple-element.47), channel_id=1, source_target_pairs={{0,111},{1,96},{2,97},{3,98},{4,99},{5,100},{6,101},{7,102},{8,103... | collective-permute-start | bytes 24584 | tf_op jit(solution)/shard_map/ppermute | solution.py:480
  36.8 5.2 %collective-permute-start.10 = (f32[8,128]{1,0:T(8,128)S(1)}, f32[8,128]{1,0:T(8,128)S(1)}, u32[]{:S(2)}, u32[]{:S(2)}) collective-permute-start(f32[8,128]{1,0:T(8,128)S(1)} %mix.1), channel_id=1, source_target_pairs={{0,64},{16,80},{32,96},{48,112},{64,0},{80,16},{96,32},{112,48},{1... | collective-permute-start | bytes 12296 | tf_op jit(solution)/shard_map/ppermute | solution.py:470
  37.0 4.9 %collective-permute-start.9 = (f32[8,128]{1,0:T(8,128)S(1)}, f32[8,128]{1,0:T(8,128)S(1)}, u32[]{:S(2)}, u32[]{:S(2)}) collective-permute-start(f32[8,128]{1,0:T(8,128)S(1)} %mix.1), channel_id=1, source_target_pairs={{0,96},{16,112},{32,64},{48,80},{64,32},{80,48},{96,0},{112,16},{1... | collective-permute-start | bytes 12296 | tf_op jit(solution)/shard_map/ppermute | solution.py:470
  38.9 3.6 %collective-permute-start.8 = (f32[8,128]{1,0:T(8,128)S(1)}, f32[8,128]{1,0:T(8,128)S(1)}, u32[]{:S(2)}, u32[]{:S(2)}) collective-permute-start(f32[8,128]{1,0:T(8,128)S(1)} %mix.1), channel_id=1, source_target_pairs={{0,32},{16,48},{32,0},{48,16},{64,96},{80,112},{96,64},{112,80},{1... | collective-permute-start | bytes 12296 | tf_op jit(solution)/shard_map/ppermute | solution.py:470
  42.5 9.3 %collective-permute-start.11 = (f32[8,128]{1,0:T(8,128)S(1)}, f32[8,128]{1,0:T(8,128)S(1)}, u32[]{:S(2)}, u32[]{:S(2)}) collective-permute-start(f32[8,128]{1,0:T(8,128)S(1)} %add_add_fusion.here_ref), channel_id=1, source_target_pairs={{0,112},{16,96},{32,80},{48,64},{64,48},{80,32},{96,16},{112,0},{1... | collective-permute-start | bytes 12296 | tf_op jit(solution)/shard_map/ppermute | solution.py:470
  58.2 45.0 %collective-permute-start.12 = (f32[2048,256]{1,0:T(8,128)S(1)}, f32[2048,256]{1,0:T(8,128)S(1)}, u32[]{:S(2)}, u32[]{:S(2)}) collective-permute-start(f32[2048,256]{1,0:T(8,128)S(1)} %get-tuple-element.51.up), channel_id=1, source_target_pairs={{0,1},{1,2},{2,3},{3,4},{4,5},{5,6},{6,7},{7,8},{8,9},{9,10},{10,1... | collective-permute-start | bytes 6291464 | tf_op jit(solution)/shard_map/ppermute | solution.py:465
  58.3 45.0 %collective-permute-start.13 = (f32[2048,256]{1,0:T(8,128)S(1)}, f32[2048,256]{1,0:T(8,128)S(1)}, u32[]{:S(2)}, u32[]{:S(2)}) collective-permute-start(f32[2048,256]{1,0:T(8,128)S(1)} %get-tuple-element.52.down), channel_id=1, source_target_pairs={{0,15},{1,0},{2,1},{3,2},{4,3},{5,4},{6,5},{7,6},{8,7},{9,8},{10,9... | collective-permute-start | bytes 6291464 | tf_op jit(solution)/shard_map/ppermute | solution.py:465
  62.1 13.4 %collective-permute-start.14 = (f32[2,128,512]{2,1,0:T(8,128)S(1)}, f32[2,128,512]{2,1,0:T(8,128)S(1)}, u32[]{:S(2)}, u32[]{:S(2)}) collective-permute-start(f32[2,128,512]{2,1,0:T(8,128)S(1)} %get-tuple-element.55), channel_id=1, source_target_pairs={{0,32},{16,48},{32,0},{48,16},{64,96},{80,112},{96,64},{112,80},{1... | collective-permute-start | bytes 1572872 | tf_op jit(solution)/shard_map/ppermute | solution.py:470
  63.2 14.0 %collective-permute-start.15 = (f32[2,128,512]{2,1,0:T(8,128)S(1)}, f32[2,128,512]{2,1,0:T(8,128)S(1)}, u32[]{:S(2)}, u32[]{:S(2)}) collective-permute-start(f32[2,128,512]{2,1,0:T(8,128)S(1)} %get-tuple-element.57), channel_id=1, source_target_pairs={{0,96},{16,112},{32,64},{48,80},{64,32},{80,48},{96,0},{112,16},{1... | collective-permute-start | bytes 1572872 | tf_op jit(solution)/shard_map/ppermute | solution.py:470
  74.9 10.2 %collective-permute-start.19 = (f32[2,128,512]{2,1,0:T(8,128)S(1)}, f32[2,128,512]{2,1,0:T(8,128)S(1)}, u32[]{:S(2)}, u32[]{:S(2)}) collective-permute-start(f32[2,128,512]{2,1,0:T(8,128)S(1)} %get-tuple-element.64), channel_id=1, source_target_pairs={{0,32},{16,48},{32,0},{48,16},{64,96},{80,112},{96,64},{112,80},{1... | collective-permute-start | bytes 1572872 | tf_op jit(solution)/shard_map/ppermute | solution.py:470
  75.5 13.2 %collective-permute-start.21 = (f32[2,128,512]{2,1,0:T(8,128)S(1)}, f32[2,128,512]{2,1,0:T(8,128)S(1)}, u32[]{:S(2)}, u32[]{:S(2)}) collective-permute-start(f32[2,128,512]{2,1,0:T(8,128)S(1)} %get-tuple-element.68), channel_id=1, source_target_pairs={{0,96},{16,112},{32,64},{48,80},{64,32},{80,48},{96,0},{112,16},{1... | collective-permute-start | bytes 1572872 | tf_op jit(solution)/shard_map/ppermute | solution.py:470
  77.3 24.1 %collective-permute-start.16 = (f32[2,2,64,512]{3,2,1,0:T(8,128)S(1)}, f32[2,2,64,512]{3,2,1,0:T(8,128)S(1)}, u32[]{:S(2)}, u32[]{:S(2)}) collective-permute-start(f32[2,2,64,512]{3,2,1,0:T(8,128)S(1)} %get-tuple-element.60), channel_id=1, source_target_pairs={{0,16},{16,0},{32,48},{48,32},{64,80},{80,64},{96,112},{112,96},{1... | collective-permute-start | bytes 1572872 | tf_op jit(solution)/shard_map/ppermute | solution.py:470
  85.2 7.7 %collective-permute-start.20 = (f32[128,512]{1,0:T(8,128)S(1)}, f32[128,512]{1,0:T(8,128)S(1)}, u32[]{:S(2)}, u32[]{:S(2)}) collective-permute-start(f32[128,512]{1,0:T(8,128)S(1)} %get-tuple-element.66), channel_id=1, source_target_pairs={{0,96},{16,112},{32,64},{48,80},{64,32},{80,48},{96,0},{112,16},{1... | collective-permute-start | bytes 786440 | tf_op jit(solution)/shard_map/ppermute | solution.py:470
  88.8 7.0 %collective-permute-start.22 = (f32[128,512]{1,0:T(8,128)S(1)}, f32[128,512]{1,0:T(8,128)S(1)}, u32[]{:S(2)}, u32[]{:S(2)}) collective-permute-start(f32[128,512]{1,0:T(8,128)S(1)} %get-tuple-element.70), channel_id=1, source_target_pairs={{0,32},{16,48},{32,0},{48,16},{64,96},{80,112},{96,64},{112,80},{1... | collective-permute-start | bytes 786440 | tf_op jit(solution)/shard_map/ppermute | solution.py:470
  95.8 12.4 %collective-permute-start.23 = (f32[2,64,512]{2,1,0:T(8,128)S(1)}, f32[2,64,512]{2,1,0:T(8,128)S(1)}, u32[]{:S(2)}, u32[]{:S(2)}) collective-permute-start(f32[2,64,512]{2,1,0:T(8,128)S(1)} %get-tuple-element.72), channel_id=1, source_target_pairs={{0,16},{16,0},{32,48},{48,32},{64,80},{80,64},{96,112},{112,96},{1... | collective-permute-start | bytes 786440 | tf_op jit(solution)/shard_map/ppermute | solution.py:470
  101.5 6.3 %collective-permute-start.17 = (f32[64,512]{1,0:T(8,128)S(1)}, f32[64,512]{1,0:T(8,128)S(1)}, u32[]{:S(2)}, u32[]{:S(2)}) collective-permute-start(f32[64,512]{1,0:T(8,128)S(1)} %get-tuple-element.62), channel_id=1, source_target_pairs={{0,96},{16,112},{32,64},{48,80},{64,32},{80,48},{96,0},{112,16},{1... | collective-permute-start | bytes 393224 | tf_op jit(solution)/shard_map/ppermute | solution.py:470
  103.3 5.0 %collective-permute-start.18 = (f32[64,512]{1,0:T(8,128)S(1)}, f32[64,512]{1,0:T(8,128)S(1)}, u32[]{:S(2)}, u32[]{:S(2)}) collective-permute-start(f32[64,512]{1,0:T(8,128)S(1)} %get-tuple-element.63), channel_id=1, source_target_pairs={{0,32},{16,48},{32,0},{48,16},{64,96},{80,112},{96,64},{112,80},{1... | collective-permute-start | bytes 393224 | tf_op jit(solution)/shard_map/ppermute | solution.py:470

commit v5 on v3

--- a/solution.py
+++ b/solution.py
@@ -11,6 +11,7 @@
 STEPS = 2
 READ = 256
 CHUNK = 512
+LONG = 512
 VMEM = 16 * 1024 * 1024
 
 epsilon = 1e-06
@@ -123,8 +124,8 @@
     )(plan, *sums, rotations, *after)
 
 
-def pieces(rows):
-    count = -(-rows // CHUNK)
+def pieces(rows, longest=CHUNK):
+    count = -(-rows // longest)
     return [(k * (rows // count), rows // count) for k in range(count)]
 
 
@@ -213,33 +214,29 @@
     return kept, sums
 
 
-def gram_kernel(total_rows, kept_high, kept_low, up, down, *refs):
-    outs, gram_acc = refs[:4], refs[4]
-    for r, count in pieces(up.shape[0]):
+def gram_kernel(total_rows, pair, kept_high, kept_low, sent_ref, mine, other, gram_acc):
+    for r, count in pieces(sent_ref.shape[0]):
         here = slice(r, r + count)
-        for pair, sent in enumerate((up, down)):
-            h, l = split(sent[here, :])
-            gram = half_gram(
-                jnp.concatenate([kept_high[pair, here, :], h], axis=1),
-                jnp.concatenate([kept_low[pair, here, :], l], axis=1),
-            )
-            gram_acc[pair] = gram + gram_acc[pair] if r else gram
-    for pair in range(2):
-        cut_gram(total_rows, pair, gram_acc, *outs[2 * pair : 2 * pair + 2])
-
-
-def gram(total_rows, kept, up, down):
-    outs = pl.pallas_call(
-        functools.partial(gram_kernel, total_rows),
-        in_specs=[in_vmem] * 4,
-        out_specs=[in_vmem] * 4,
-        out_shape=[f32(2, 128, 2 * BW)] * 4,
+        h, l = split(sent_ref[here, :])
+        gram = half_gram(
+            jnp.concatenate([kept_high[pair, here, :], h], axis=1),
+            jnp.concatenate([kept_low[pair, here, :], l], axis=1),
+        )
+        gram_acc[pair] = gram + gram_acc[pair] if r else gram
+    cut_gram(total_rows, pair, gram_acc, mine, other)
+
+
+def gram(total_rows, pair, kept, sent):
+    return pl.pallas_call(
+        functools.partial(gram_kernel, total_rows, pair),
+        in_specs=[in_vmem] * 3,
+        out_specs=[in_vmem] * 2,
+        out_shape=[f32(2, 128, 2 * BW)] * 2,
         scratch_shapes=[pltpu.VMEM((2, 2 * BW, 2 * BW), jnp.float32)],
         compiler_params=params(),
         cost_estimate=cost(1 << 10, 1 << 10),
         name="gram",
-    )(*kept, up, down)
-    return outs[:2], outs[2:]
+    )(*kept, sent)
 
 
 def send_again_kernel(plan_ref, kept_high, kept_low, up_in, down_in, rot_ref, _,
@@ -273,7 +270,7 @@
 def stay_again_kernel(total_rows, plan_ref, high_ref, low_ref, rot_ref, up, down, result, *refs):
     outs, (gram_acc, kept_ref, sem) = refs[:4], refs[4:]
     copies = []
-    for k, (r, count) in enumerate(pieces(up.shape[0])):
+    for k, (r, count) in enumerate(pieces(up.shape[0], LONG)):
         here = slice(r, r + count)
         for pair, sent in enumerate((up, down)):
             x = stacked(high_ref, low_ref, plan_ref, 1, pair, r, count)
@@ -309,7 +306,7 @@
         scratch_shapes=[
             pltpu.VMEM((2, 2 * BW, 2 * BW), jnp.float32),
             pltpu.VMEM((rows, 2 * BW), jnp.float32),
-            pltpu.SemaphoreType.DMA((len(pieces(rows)),)),
+            pltpu.SemaphoreType.DMA((len(pieces(rows, LONG)),)),
         ],
         compiler_params=params(),
         cost_estimate=cost(1 << 10, 1 << 10),
@@ -350,31 +347,55 @@
         add_kernel,
         in_specs=[in_vmem] * 2 + [anywhere] * len(after),
         out_specs=[in_vmem] * 2,
-        out_shape=[f32(128, 2 * BW)] * 2,
+        out_shape=[f32(mine.shape[1], 2 * BW)] * 2,
         compiler_params=params(),
         cost_estimate=cost(1 << 10, 1 << 10),
         name="add",
     )(mine, got, *after)
 
 
-def halve_kernel(mine0, got0, mine1, got1, keep_ref, send_ref):
+def halve_kernel(*refs):
+    keep_ref, send_ref = refs[-2:]
     bit = lax.axis_index("frame") % 2
-    for pair, (mine, got) in enumerate(((mine0, got0), (mine1, got1))):
+    for k in range(keep_ref.shape[0]):
+        mine, got = refs[2 * k], refs[2 * k + 1]
         for ref, chosen in ((keep_ref, bit), (send_ref, 1 - bit)):
             rows = pl.ds(pl.multiple_of(64 * chosen, 64), 64)
-            ref[pair] = mine[rows, :] + got[rows, :]
-
-
-def halve(mine0, got0, mine1, got1):
+            ref[k] = mine[rows, :] + got[rows, :]
+
+
+def halve(terms):
+    args = [array for term in terms for array in term]
     return pl.pallas_call(
         halve_kernel,
-        in_specs=[in_vmem] * 4,
+        in_specs=[in_vmem] * len(args),
         out_specs=[in_vmem] * 2,
-        out_shape=[f32(2, 64, 2 * BW)] * 2,
+        out_shape=[f32(len(terms), 64, 2 * BW)] * 2,
         compiler_params=params(),
         cost_estimate=cost(1 << 10, 1 << 10),
         name="halve",
-    )(mine0, got0, mine1, got1)
+    )(*args)
+
+
+def begin_kernel(mine0, got0, mine1, got1, _, keep0, send0, keep1, send1):
+    bit = lax.axis_index("frame") % 2
+    for ref, chosen in ((keep0, bit), (send0, 1 - bit)):
+        rows = pl.ds(pl.multiple_of(64 * chosen, 64), 64)
+        ref[...] = mine0[:, rows, :] + got0[:, rows, :]
+    keep1[...] = mine1[0] + got1[0]
+    send1[...] = mine1[1] + got1[1]
+
+
+def begin(args, after):
+    return pl.pallas_call(
+        begin_kernel,
+        in_specs=[in_vmem] * 4 + [anywhere],
+        out_specs=[in_vmem] * 4,
+        out_shape=[f32(2, 64, 2 * BW)] * 2 + [f32(128, 2 * BW)] * 2,
+        compiler_params=params(),
+        cost_estimate=cost(1 << 10, 1 << 10),
+        name="begin",
+    )(*args, after)
 
 
 def fill_kernel(_, up, down, out, done, sem):
@@ -403,25 +424,23 @@
     )(out, up, down)
 
 
-def finish_kernel(*refs):
-    out = refs[-1]
-    for step in range(STEPS):
-        mine, got = refs[2 * step], refs[2 * step + 1]
-        for pair in range(2):
-            out[step, :, pair, :] = mine[pair] + got[pair]
-
-
-def finish(pieces, after):
-    args = [array for piece in pieces for array in piece]
+def finish_kernel(early_mine, early_got, mine, got, _, out):
+    out[0, :, 0, :] = early_mine[...] + early_got[...]
+    out[0, :, 1, :] = mine[2] + got[2]
+    for pair in range(2):
+        out[1, :, pair, :] = mine[pair] + got[pair]
+
+
+def finish(early, late, after):
     return pl.pallas_call(
         finish_kernel,
-        in_specs=[in_vmem] * len(args) + [anywhere],
+        in_specs=[in_vmem] * 4 + [anywhere],
         out_specs=in_vmem,
         out_shape=f32(STEPS, 64, 2, 2 * BW),
         compiler_params=params(),
         cost_estimate=cost(1 << 10, 1 << 10),
         name="finish",
-    )(*args, after)
+    )(*early, *late, after)
 
 
 def shift(x, by):
@@ -444,25 +463,40 @@
     return lax.ppermute(x, ("frame", "pair"), pairs)
 
 
-def all_sum(x, across):
-    x = (x + swap(x, 2)) + (swap(x, 6) + swap(x, 4))
+def add_kernel_of_four(a, b, c, d, *refs):
+    refs[-1][...] = (a[...] + b[...]) + (c[...] + d[...])
+
+
+def all_sum(x, across, after=()):
+    x = pl.pallas_call(
+        add_kernel_of_four,
+        in_specs=[in_vmem] * 4 + [anywhere] * len(after),
+        out_specs=in_vmem,
+        out_shape=f32(8, 128),
+        compiler_params=params(),
+        cost_estimate=cost(1 << 10, 1 << 10),
+        name="add_four",
+    )(x, swap(x, 2), swap(x, 6), swap(x, 4), *after)
     return x, swap(x, across)
 
 
 NEAR = ((2, 6), (6, 2))
 
 
-def begin_sum(halves, after=()):
-    return [
-        add_first(mine, swap(other, NEAR[pair][0]), after)
-        for pair, (mine, other) in enumerate(halves)
-    ]
-
-
-def end_sum(begun):
-    args = [(kept, swap(sent, NEAR[pair][1])) for pair, (kept, sent) in enumerate(begun)]
-    mine, other = halve(*args[0], *args[1])
-    return mine, swap(other, 1)
+def gram_sums(first_halves, last_halves):
+    args = []
+    for (mine, other), (here, _) in zip(first_halves, NEAR):
+        args += [mine, swap(other, here)]
+    mine, other, kept1, sent1 = begin(args, last_halves[0][0])
+    kept, sent = add_first(mine, swap(other, 1), ())
+    early = kept, swap(sent, NEAR[0][1])
+    terms = []
+    for (mine, other), (here, there) in zip(last_halves, NEAR):
+        kept, sent = add_first(mine, swap(other, here), ())
+        terms.append((kept, swap(sent, there)))
+    terms.append((kept1, swap(sent1, NEAR[1][1])))
+    mine, other = halve(terms)
+    return early, (mine, swap(other, 1))
 
 
 def local(columns, rotations, plan):
@@ -473,15 +507,15 @@
     moved = shift(up, 1), shift(down, -1)
     kept, own = stay(plan, high, low, rot)
     mixed = mix(own, shift_aside(up_sums, 1), shift_aside(down_sums, -1))
-    halves = gram(total_rows, kept, up, down)
-    rot = scaled(total_rows, 1, all_sum(mixed, 7), rotations, plan, (halves[0][0],))
+    halves = [gram(total_rows, pair, kept, sent) for pair, sent in enumerate((up, down))]
+    tiles = all_sum(mixed, 7, (halves[0][0],))
+    rot = scaled(total_rows, 1, tiles, rotations, plan, (halves[1][0],))
     up, down, high, low = send_again(plan, kept, *moved, rot, halves[0][0])
     moved = shift(up, 1), shift(down, -1)
     result, halves_again = stay_again(total_rows, plan, high, low, rot, up, down)
-    first_grams = end_sum(begin_sum(halves, (halves_again[0][0],)))
-    last_grams = end_sum(begin_sum(halves_again))
+    early, late = gram_sums(halves, halves_again)
     result, done = fill(result, *moved)
-    return result, finish((first_grams, last_grams), done)
+    return result, finish(early, late, done)
 
 
 def solution(mesh):

time: 110 us -> 109 us (level)
  the two profiles are of different devices: /device:TPU:104 before, /device:TPU:0 now
where the time goes in v5:
time: 109 us
  starting transfers between devices  44.7 us (41%)
  Pallas kernels  38.3 us (35%)
  waiting for transfers between devices  24.9 us (23%)
    ppermute x18, starting transfers between devices, swap(): return lax.ppermute(x, 'frame', [(i, i ^ bit) for i in range(size)])  30.9 us
    ppermute x18, waiting for transfers between devices, swap(): return lax.ppermute(x, 'frame', [(i, i ^ bit) for i in range(size)])  24.9 us
    pallas_call x1, Pallas kernels, stay_again(): pl.pallas_call(functools.partial(stay_again_kernel, total_rows), in_specs...  10.3 us
    ppermute x4, starting transfers between devices, shift(): return lax.ppermute(x, 'pair', [(i, (i + by) % size) for i in range(size)])  7.83 us
    ppermute x2, starting transfers between devices, shift_aside(): return lax.ppermute(x, ('frame', 'pair'), pairs)  5.96 us
    pallas_call x2, Pallas kernels, gram(): pl.pallas_call(functools.partial(gram_kernel, total_rows, pair), in_specs...  5.31 us
    pallas_call x1, Pallas kernels, send_again(): pl.pallas_call(send_again_kernel, in_specs=[in_smem] + [in_vmem] * 5 + [a...  5.31 us
    pallas_call x1, Pallas kernels, stay(): pl.pallas_call(stay_kernel, in_specs=[in_smem] + [in_vmem] * 3, out_specs...  4.08 us
  transfers between devices with their start and end apart: 24, of which 10 were waited for; matrix products, arithmetic and copies ran while one was open for 0% of the time, Pallas kernels for 21%

profile of v5, /device:TPU:0, one launch (start us, length us, event | category | flops | bytes accessed | tf_op | source)
XLA Modules:
  0.0 108.7 jit_solution(1541330717990906210)
XLA Ops:
  0.6 0.0 copy-start.1
  0.6 3.8 %first.1 = (bf16[4,2048,256]{2,1,0:T(8,128)(2,1)S(1)}, bf16[4,2048,256]{2,1,0:T(8,128)(2,1)S(1)}, f32[8,128]{1,0:T(8,128)S(1)}) custom-call(f32[2048,1024]{1,0:T(8,128)} %x_ref.1), custom_call_target="tpu_custom_call" | custom-call | flops 1024 | bytes 1024 | tf_op jit(solution)/shard_map/first/pallas_call | solution.py:80
  4.5 3.2 %collective-permute-start.2 = (f32[8,128]{1,0:T(8,128)S(1)}, f32[8,128]{1,0:T(8,128)S(1)}, u32[]{:S(2)}, u32[]{:S(2)}) collective-permute-start(f32[8,128]{1,0:T(8,128)S(1)} %get-tuple-element.41.a), channel_id=1, source_target_pairs={{0,64},{16,80},{32,96},{48,112},{64,0},{80,16},{96,32},{112,48},{1... | collective-permute-start | bytes 12296 | tf_op jit(solution)/shard_map/ppermute | solution.py:453
  7.7 1.1 %collective-permute-start.1 = (f32[8,128]{1,0:T(8,128)S(1)}, f32[8,128]{1,0:T(8,128)S(1)}, u32[]{:S(2)}, u32[]{:S(2)}) collective-permute-start(f32[8,128]{1,0:T(8,128)S(1)} %get-tuple-element.41.a), channel_id=1, source_target_pairs={{0,96},{16,112},{32,64},{48,80},{64,32},{80,48},{96,0},{112,16},{1... | collective-permute-start | bytes 12296 | tf_op jit(solution)/shard_map/ppermute | solution.py:453
  8.8 0.0 collective-permute-start
  8.8 0.9 collective-permute-done.2.d
  9.7 2.8 %collective-permute-done.1.c = f32[8,128]{1,0:T(8,128)S(1)} collective-permute-done((f32[8,128]{1,0:T(8,128)S(1)}, f32[8,128]{1,0:T(8,128)S(1)}, u32[]{:S(2)}, u32[]{:S(2)}) %collective-permute-start.1) | collective-permute-done | bytes 4128 | tf_op jit(solution)/shard_map/ppermute | solution.py:453
  12.5 0.0 collective-permute-done.b
  12.5 3.3 %collective-permute-start.3 = (f32[8,128]{1,0:T(8,128)S(1)}, f32[8,128]{1,0:T(8,128)S(1)}, u32[]{:S(2)}, u32[]{:S(2)}) collective-permute-start(f32[8,128]{1,0:T(8,128)S(1)} %add_four.2.here_ref), channel_id=1, source_target_pairs={{0,16},{16,0},{32,48},{48,32},{64,80},{80,64},{96,112},{112,96},{1... | collective-permute-start | bytes 12296 | tf_op jit(solution)/shard_map/ppermute | solution.py:453
  15.8 1.9 %collective-permute-done.3.there_ref = f32[8,128]{1,0:T(8,128)S(1)} collective-permute-done((f32[8,128]{1,0:T(8,128)S(1)}, f32[8,128]{1,0:T(8,128)S(1)}, u32[]{:S(2)}, u32[]{:S(2)}) %collective-permute-start.3) | collective-permute-done | bytes 4128 | tf_op jit(solution)/shard_map/ppermute | solution.py:453
  17.7 1.1 scale.2.rot_ref
  18.8 4.0 %send.1 = (f32[2048,256]{1,0:T(8,128)S(1)}, f32[2048,256]{1,0:T(8,128)S(1)}, f32[8,256]{1,0:T(8,128)S(1)}, f32[8,256]{1,0:T(8,128)S(1)}) custom-call(s32[2,1,4]{2,1,0:T(1,128)S(1)} %copy-done.1, bf16[4,2048,256]{2,1,0:T(8,128)(2,1)S(1)} %get-tuple-element.39.high_ref, bf16[4,2048,256]{2,1,0:T(8,128)(2,1)S(1)} %get-tuple-element.40.low_ref, ...), custom_call_target="tpu_custom_call" | custom-call | flops 1024 | bytes 1024 | tf_op jit(solution)/shard_map/send/pallas_call | solution.py:175
  22.8 0.1 collective-permute-start.4
  22.8 3.8 %collective-permute-start.5 = (f32[2048,256]{1,0:T(8,128)S(1)}, f32[2048,256]{1,0:T(8,128)S(1)}, u32[]{:S(2)}, u32[]{:S(2)}) collective-permute-start(f32[2048,256]{1,0:T(8,128)S(1)} %get-tuple-element.45.sent_ref), channel_id=1, source_target_pairs={{0,15},{1,0},{2,1},{3,2},{4,3},{5,4},{6,5},{7,6},{8,7},{9,8},{10,9... | collective-permute-start | bytes 6291464 | tf_op jit(solution)/shard_map/ppermute | solution.py:448
  26.7 0.0 collective-permute-start.6
  26.7 6.0 %collective-permute-start.7 = (f32[8,256]{1,0:T(8,128)S(1)}, f32[8,256]{1,0:T(8,128)S(1)}, u32[]{:S(2)}, u32[]{:S(2)}) collective-permute-start(f32[8,256]{1,0:T(8,128)S(1)} %get-tuple-element.48), channel_id=1, source_target_pairs={{0,111},{1,96},{2,97},{3,98},{4,99},{5,100},{6,101},{7,102},{8,103... | collective-permute-start | bytes 24584 | tf_op jit(solution)/shard_map/ppermute | solution.py:463
  32.7 4.1 %stay.1 = (bf16[2,2048,256]{2,1,0:T(8,128)(2,1)S(1)}, bf16[2,2048,256]{2,1,0:T(8,128)(2,1)S(1)}, f32[8,128]{1,0:T(8,128)S(1)}) custom-call(s32[2,1,4]{2,1,0:T(1,128)S(1)} %copy-done.1, bf16[4,2048,256]{2,1,0:T(8,128)(2,1)S(1)} %get-tuple-element.39.high_ref, bf16[4,2048,256]{2,1,0:T(8,128)(2,1)S(1)} %get-tuple-element.40.low_ref, ...), custom_call_target="tpu_custom_call" | custom-call | flops 1024 | bytes 1024 | tf_op jit(solution)/shard_map/stay/pallas_call | solution.py:204
  36.7 0.0 collective-permute-done.6.before
  36.8 0.0 collective-permute-done.7.after
  36.8 0.2 collective-permute-start.10
  37.0 1.9 %collective-permute-start.9 = (f32[8,128]{1,0:T(8,128)S(1)}, f32[8,128]{1,0:T(8,128)S(1)}, u32[]{:S(2)}, u32[]{:S(2)}) collective-permute-start(f32[8,128]{1,0:T(8,128)S(1)} %mix.1.a), channel_id=1, source_target_pairs={{0,96},{16,112},{32,64},{48,80},{64,32},{80,48},{96,0},{112,16},{1... | collective-permute-start | bytes 12296 | tf_op jit(solution)/shard_map/ppermute | solution.py:453
  38.9 1.5 %collective-permute-start.8 = (f32[8,128]{1,0:T(8,128)S(1)}, f32[8,128]{1,0:T(8,128)S(1)}, u32[]{:S(2)}, u32[]{:S(2)}) collective-permute-start(f32[8,128]{1,0:T(8,128)S(1)} %mix.1.a), channel_id=1, source_target_pairs={{0,32},{16,48},{32,0},{48,16},{64,96},{80,112},{96,64},{112,80},{1... | collective-permute-start | bytes 12296 | tf_op jit(solution)/shard_map/ppermute | solution.py:453
  40.4 2.7 %gram.2 = (f32[2,128,512]{2,1,0:T(8,128)S(1)}, f32[2,128,512]{2,1,0:T(8,128)S(1)}) custom-call(bf16[2,2048,256]{2,1,0:T(8,128)(2,1)S(1)} %get-tuple-element.42.kept_high, bf16[2,2048,256]{2,1,0:T(8,128)(2,1)S(1)} %get-tuple-element.43.kept_low, f32[2048,256]{1,0:T(8,128)S(1)} %get-tuple-element.44.sent_ref), custom_call_target="tpu_custom_call" | custom-call | flops 1024 | bytes 1024 | tf_op jit(solution)/shard_map/gram/pallas_call | solution.py:230
  43.0 0.0 collective-permute-done.10.d
  43.0 0.0 collective-permute-done.9.c
  43.0 0.0 collective-permute-done.8.b
  43.1 4.7 %collective-permute-start.11 = (f32[8,128]{1,0:T(8,128)S(1)}, f32[8,128]{1,0:T(8,128)S(1)}, u32[]{:S(2)}, u32[]{:S(2)}) collective-permute-start(f32[8,128]{1,0:T(8,128)S(1)} %add_four.3.here_ref), channel_id=1, source_target_pairs={{0,112},{16,96},{32,80},{48,64},{64,48},{80,32},{96,16},{112,0},{1... | collective-permute-start | bytes 12296 | tf_op jit(solution)/shard_map/ppermute | solution.py:453
  47.7 2.7 %gram.3 = (f32[2,128,512]{2,1,0:T(8,128)S(1)}, f32[2,128,512]{2,1,0:T(8,128)S(1)}) custom-call(bf16[2,2048,256]{2,1,0:T(8,128)(2,1)S(1)} %get-tuple-element.42.kept_high, bf16[2,2048,256]{2,1,0:T(8,128)(2,1)S(1)} %get-tuple-element.43.kept_low, f32[2048,256]{1,0:T(8,128)S(1)} %get-tuple-element.45.sent_ref), custom_call_target="tpu_custom_call" | custom-call | flops 1024 | bytes 1024 | tf_op jit(solution)/shard_map/gram/pallas_call | solution.py:230
  50.4 0.1 collective-permute-done.11.there_ref
  50.5 1.1 scale.3.rot_ref
  51.5 0.0 collective-permute-done.4.up_in
  51.6 0.0 collective-permute-done.5.down_in
  51.6 5.3 %send_again.1 = (f32[2048,256]{1,0:T(8,128)S(1)}, f32[2048,256]{1,0:T(8,128)S(1)}, bf16[4,2048,256]{2,1,0:T(8,128)(2,1)S(1)}, bf16[4,2048,256]{2,1,0:T(8,128)(2,1)S(1)}) custom-call(s32[2,1,4]{2,1,0:T(1,128)S(1)} %copy-done.1, bf16[2,2048,256]{2,1,0:T(8,128)(2,1)S(1)} %get-tuple-element.42.kept_high, bf16[2,2048,256]{2,1,0:T(8,128)(2,1)S(1)} %get-tuple-element.43.kept_low, ...), custom_call_target="tpu_custom_call" | custom-call | flops 1024 | bytes 1024 | tf_op jit(solution)/shard_map/send_again/pallas_call | solution.py:259
  56.9 0.1 collective-permute-start.12
  57.0 3.8 %collective-permute-start.13 = (f32[2048,256]{1,0:T(8,128)S(1)}, f32[2048,256]{1,0:T(8,128)S(1)}, u32[]{:S(2)}, u32[]{:S(2)}) collective-permute-start(f32[2048,256]{1,0:T(8,128)S(1)} %get-tuple-element.54.down), channel_id=1, source_target_pairs={{0,15},{1,0},{2,1},{3,2},{4,3},{5,4},{6,5},{7,6},{8,7},{9,8},{10,9... | collective-permute-start | bytes 6291464 | tf_op jit(solution)/shard_map/ppermute | solution.py:448
  60.8 0.1 collective-permute-start.14
  60.9 1.8 %collective-permute-start.15 = (f32[2,128,512]{2,1,0:T(8,128)S(1)}, f32[2,128,512]{2,1,0:T(8,128)S(1)}, u32[]{:S(2)}, u32[]{:S(2)}) collective-permute-start(f32[2,128,512]{2,1,0:T(8,128)S(1)} %get-tuple-element.58), channel_id=1, source_target_pairs={{0,96},{16,112},{32,64},{48,80},{64,32},{80,48},{96,0},{112,16},{1... | collective-permute-start | bytes 1572872 | tf_op jit(solution)/shard_map/ppermute | solution.py:453
  62.7 10.3 %stay_again.1 = (f32[2048,1024]{1,0:T(8,128)}, f32[2,128,512]{2,1,0:T(8,128)S(1)}, f32[2,128,512]{2,1,0:T(8,128)S(1)}, f32[2,128,512]{2,1,0:T(8,128)S(1)}, f32[2,128,512]{2,1,0:T(8,128)S(1)}) custom-call(s32[2,1,4]{2,1,0:T(1,128)S(1)} %copy-done.1, bf16[4,2048,256]{2,1,0:T(8,128)(2,1)S(1)} %get-tuple-element.51.high_ref, ...), custom_call_target="tpu_custom_call" | custom-call | flops 1024 | bytes 1024 | tf_op jit(solution)/shard_map/stay_again/pallas_call | solution.py:301
  73.1 1.5 %collective-permute-start.18 = (f32[2,128,512]{2,1,0:T(8,128)S(1)}, f32[2,128,512]{2,1,0:T(8,128)S(1)}, u32[]{:S(2)}, u32[]{:S(2)}) collective-permute-start(f32[2,128,512]{2,1,0:T(8,128)S(1)} %get-tuple-element.64), channel_id=1, source_target_pairs={{0,32},{16,48},{32,0},{48,16},{64,96},{80,112},{96,64},{112,80},{1... | collective-permute-start | bytes 1572872 | tf_op jit(solution)/shard_map/ppermute | solution.py:453
  74.6 0.0 collective-permute-done.14.got0
  74.6 1.3 %collective-permute-start.20 = (f32[2,128,512]{2,1,0:T(8,128)S(1)}, f32[2,128,512]{2,1,0:T(8,128)S(1)}, u32[]{:S(2)}, u32[]{:S(2)}) collective-permute-start(f32[2,128,512]{2,1,0:T(8,128)S(1)} %get-tuple-element.68), channel_id=1, source_target_pairs={{0,96},{16,112},{32,64},{48,80},{64,32},{80,48},{96,0},{112,16},{1... | collective-permute-start | bytes 1572872 | tf_op jit(solution)/shard_map/ppermute | solution.py:453
  75.9 0.0 collective-permute-done.15.got1
  75.9 0.1 begin.1
  76.0 0.2 collective-permute-start.22
  76.2 11.8 %collective-permute-done.18.got = f32[2,128,512]{2,1,0:T(8,128)S(1)} collective-permute-done((f32[2,128,512]{2,1,0:T(8,128)S(1)}, f32[2,128,512]{2,1,0:T(8,128)S(1)}, u32[]{:S(2)}, u32[]{:S(2)}) %collective-permute-start.18) | collective-permute-done | bytes 524320 | tf_op jit(solution)/shard_map/ppermute | solution.py:453
  88.0 0.1 add.4
  88.1 1.5 %collective-permute-start.19 = (f32[128,512]{1,0:T(8,128)S(1)}, f32[128,512]{1,0:T(8,128)S(1)}, u32[]{:S(2)}, u32[]{:S(2)}) collective-permute-start(f32[128,512]{1,0:T(8,128)S(1)} %get-tuple-element.66), channel_id=1, source_target_pairs={{0,96},{16,112},{32,64},{48,80},{64,32},{80,48},{96,0},{112,16},{1... | collective-permute-start | bytes 786440 | tf_op jit(solution)/shard_map/ppermute | solution.py:453
  89.6 0.0 collective-permute-done.20.got
  89.6 0.1 add.5
  89.7 0.8 collective-permute-start.21
  90.4 1.5 %collective-permute-done.22.refs_5_ = f32[128,512]{1,0:T(8,128)S(1)} collective-permute-done((f32[128,512]{1,0:T(8,128)S(1)}, f32[128,512]{1,0:T(8,128)S(1)}, u32[]{:S(2)}, u32[]{:S(2)}) %collective-permute-start.22) | collective-permute-done | bytes 262176 | tf_op jit(solution)/shard_map/ppermute | solution.py:453
  91.9 3.2 %collective-permute-start.16 = (f32[2,64,512]{2,1,0:T(8,128)S(1)}, f32[2,64,512]{2,1,0:T(8,128)S(1)}, u32[]{:S(2)}, u32[]{:S(2)}) collective-permute-start(f32[2,64,512]{2,1,0:T(8,128)S(1)} %get-tuple-element.61), channel_id=1, source_target_pairs={{0,16},{16,0},{32,48},{48,32},{64,80},{80,64},{96,112},{112,96},{1... | collective-permute-start | bytes 786440 | tf_op jit(solution)/shard_map/ppermute | solution.py:453
  95.1 0.7 collective-permute-done.19.refs_1_
  95.7 0.4 collective-permute-done.21.refs_3_
  96.1 0.1 halve.1
  96.2 3.3 %collective-permute-start.23 = (f32[3,64,512]{2,1,0:T(8,128)S(1)}, f32[3,64,512]{2,1,0:T(8,128)S(1)}, u32[]{:S(2)}, u32[]{:S(2)}) collective-permute-start(f32[3,64,512]{2,1,0:T(8,128)S(1)} %get-tuple-element.74), channel_id=1, source_target_pairs={{0,16},{16,0},{32,48},{48,32},{64,80},{80,64},{96,112},{112,96},{1... | collective-permute-start | bytes 1179656 | tf_op jit(solution)/shard_map/ppermute | solution.py:453
  99.5 2.0 %collective-permute-done.16.got = f32[2,64,512]{2,1,0:T(8,128)S(1)} collective-permute-done((f32[2,64,512]{2,1,0:T(8,128)S(1)}, f32[2,64,512]{2,1,0:T(8,128)S(1)}, u32[]{:S(2)}, u32[]{:S(2)}) %collective-permute-start.16) | collective-permute-done | bytes 262176 | tf_op jit(solution)/shard_map/ppermute | solution.py:453
  101.5 1.3 %collective-permute-start.17 = (f32[64,512]{1,0:T(8,128)S(1)}, f32[64,512]{1,0:T(8,128)S(1)}, u32[]{:S(2)}, u32[]{:S(2)}) collective-permute-start(f32[64,512]{1,0:T(8,128)S(1)} %get-tuple-element.63), channel_id=1, source_target_pairs={{0,96},{16,112},{32,64},{48,80},{64,32},{80,48},{96,0},{112,16},{1... | collective-permute-start | bytes 393224 | tf_op jit(solution)/shard_map/ppermute | solution.py:453
  102.9 0.0 collective-permute-done.12.up
  102.9 0.0 collective-permute-done.13.down
  102.9 2.0 %fill.1 = (f32[2048,1024]{1,0:T(8,128)}, f32[8,128]{1,0:T(8,128)S(1)}) custom-call(f32[2048,1024]{1,0:T(8,128)} %get-tuple-element.55._, f32[2048,256]{1,0:T(8,128)S(1)} %collective-permute-done.12.up, f32[2048,256]{1,0:T(8,128)S(1)} %collective-permute-done.13.down), custom_call_target="tpu_custom_call", output_to_operand_aliasing={{0}: (0, {})} | custom-call | flops 1024 | bytes 1024 | tf_op jit(solution)/shard_map/fill/pallas_call | solution.py:414
  104.9 2.9 %collective-permute-done.17.early_got = f32[64,512]{1,0:T(8,128)S(1)} collective-permute-done((f32[64,512]{1,0:T(8,128)S(1)}, f32[64,512]{1,0:T(8,128)S(1)}, u32[]{:S(2)}, u32[]{:S(2)}) %collective-permute-start.17) | collective-permute-done | bytes 131104 | tf_op jit(solution)/shard_map/ppermute | solution.py:453
  107.8 0.0 collective-permute-done.23.got
  107.8 0.9 finish.1
  (7 shorter events, 0.1 us)
Async XLA Ops:
  0.6 17.1 %copy-start.1 = (s32[2,1,4]{2,1,0:T(1,128)S(1)}, s32[2,1,4]{2,1,0:T(1,128)}, u32[]{:S(2)}) copy-start(s32[2,1,4]{2,1,0:T(1,128)} %plan_ref.11) | copy-start | bytes 100
  0.6 17.1 %copy-start = (f32[2,2,512,512]{3,2,1,0:T(8,128)S(1)}, f32[2,2,512,512]{3,2,1,0:T(8,128)}, u32[]{:S(2)}) copy-start(f32[2,2,512,512]{3,2,1,0:T(8,128)} %rot_ref.3) | copy-start | bytes 12582916
  4.5 5.2 %collective-permute-start.2 = (f32[8,128]{1,0:T(8,128)S(1)}, f32[8,128]{1,0:T(8,128)S(1)}, u32[]{:S(2)}, u32[]{:S(2)}) collective-permute-start(f32[8,128]{1,0:T(8,128)S(1)} %get-tuple-element.41.a), channel_id=1, source_target_pairs={{0,64},{16,80},{32,96},{48,112},{64,0},{80,16},{96,32},{112,48},{1... | collective-permute-start | bytes 12296 | tf_op jit(solution)/shard_map/ppermute | solution.py:453
  7.7 4.8 %collective-permute-start.1 = (f32[8,128]{1,0:T(8,128)S(1)}, f32[8,128]{1,0:T(8,128)S(1)}, u32[]{:S(2)}, u32[]{:S(2)}) collective-permute-start(f32[8,128]{1,0:T(8,128)S(1)} %get-tuple-element.41.a), channel_id=1, source_target_pairs={{0,96},{16,112},{32,64},{48,80},{64,32},{80,48},{96,0},{112,16},{1... | collective-permute-start | bytes 12296 | tf_op jit(solution)/shard_map/ppermute | solution.py:453
  8.8 3.7 %collective-permute-start = (f32[8,128]{1,0:T(8,128)S(1)}, f32[8,128]{1,0:T(8,128)S(1)}, u32[]{:S(2)}, u32[]{:S(2)}) collective-permute-start(f32[8,128]{1,0:T(8,128)S(1)} %get-tuple-element.41.a), channel_id=1, source_target_pairs={{0,32},{16,48},{32,0},{48,16},{64,96},{80,112},{96,64},{112,80},{1... | collective-permute-start | bytes 12296 | tf_op jit(solution)/shard_map/ppermute | solution.py:453
  12.5 5.2 %collective-permute-start.3 = (f32[8,128]{1,0:T(8,128)S(1)}, f32[8,128]{1,0:T(8,128)S(1)}, u32[]{:S(2)}, u32[]{:S(2)}) collective-permute-start(f32[8,128]{1,0:T(8,128)S(1)} %add_four.2.here_ref), channel_id=1, source_target_pairs={{0,16},{16,0},{32,48},{48,32},{64,80},{80,64},{96,112},{112,96},{1... | collective-permute-start | bytes 12296 | tf_op jit(solution)/shard_map/ppermute | solution.py:453
  22.8 28.8 %collective-permute-start.4 = (f32[2048,256]{1,0:T(8,128)S(1)}, f32[2048,256]{1,0:T(8,128)S(1)}, u32[]{:S(2)}, u32[]{:S(2)}) collective-permute-start(f32[2048,256]{1,0:T(8,128)S(1)} %get-tuple-element.44.sent_ref), channel_id=1, source_target_pairs={{0,1},{1,2},{2,3},{3,4},{4,5},{5,6},{6,7},{7,8},{8,9},{9,10},{10,1... | collective-permute-start | bytes 6291464 | tf_op jit(solution)/shard_map/ppermute | solution.py:448
  22.8 28.7 %collective-permute-start.5 = (f32[2048,256]{1,0:T(8,128)S(1)}, f32[2048,256]{1,0:T(8,128)S(1)}, u32[]{:S(2)}, u32[]{:S(2)}) collective-permute-start(f32[2048,256]{1,0:T(8,128)S(1)} %get-tuple-element.45.sent_ref), channel_id=1, source_target_pairs={{0,15},{1,0},{2,1},{3,2},{4,3},{5,4},{6,5},{7,6},{8,7},{9,8},{10,9... | collective-permute-start | bytes 6291464 | tf_op jit(solution)/shard_map/ppermute | solution.py:448
  26.7 10.1 %collective-permute-start.6 = (f32[8,256]{1,0:T(8,128)S(1)}, f32[8,256]{1,0:T(8,128)S(1)}, u32[]{:S(2)}, u32[]{:S(2)}) collective-permute-start(f32[8,256]{1,0:T(8,128)S(1)} %get-tuple-element.47), channel_id=1, source_target_pairs={{0,97},{1,98},{2,99},{3,100},{4,101},{5,102},{6,103},{7,104},{8,10... | collective-permute-start | bytes 24584 | tf_op jit(solution)/shard_map/ppermute | solution.py:463
  26.7 10.1 %collective-permute-start.7 = (f32[8,256]{1,0:T(8,128)S(1)}, f32[8,256]{1,0:T(8,128)S(1)}, u32[]{:S(2)}, u32[]{:S(2)}) collective-permute-start(f32[8,256]{1,0:T(8,128)S(1)} %get-tuple-element.48), channel_id=1, source_target_pairs={{0,111},{1,96},{2,97},{3,98},{4,99},{5,100},{6,101},{7,102},{8,103... | collective-permute-start | bytes 24584 | tf_op jit(solution)/shard_map/ppermute | solution.py:463
  36.8 6.2 %collective-permute-start.10 = (f32[8,128]{1,0:T(8,128)S(1)}, f32[8,128]{1,0:T(8,128)S(1)}, u32[]{:S(2)}, u32[]{:S(2)}) collective-permute-start(f32[8,128]{1,0:T(8,128)S(1)} %mix.1.a), channel_id=1, source_target_pairs={{0,64},{16,80},{32,96},{48,112},{64,0},{80,16},{96,32},{112,48},{1... | collective-permute-start | bytes 12296 | tf_op jit(solution)/shard_map/ppermute | solution.py:453
  37.0 6.0 %collective-permute-start.9 = (f32[8,128]{1,0:T(8,128)S(1)}, f32[8,128]{1,0:T(8,128)S(1)}, u32[]{:S(2)}, u32[]{:S(2)}) collective-permute-start(f32[8,128]{1,0:T(8,128)S(1)} %mix.1.a), channel_id=1, source_target_pairs={{0,96},{16,112},{32,64},{48,80},{64,32},{80,48},{96,0},{112,16},{1... | collective-permute-start | bytes 12296 | tf_op jit(solution)/shard_map/ppermute | solution.py:453
  38.9 4.1 %collective-permute-start.8 = (f32[8,128]{1,0:T(8,128)S(1)}, f32[8,128]{1,0:T(8,128)S(1)}, u32[]{:S(2)}, u32[]{:S(2)}) collective-permute-start(f32[8,128]{1,0:T(8,128)S(1)} %mix.1.a), channel_id=1, source_target_pairs={{0,32},{16,48},{32,0},{48,16},{64,96},{80,112},{96,64},{112,80},{1... | collective-permute-start | bytes 12296 | tf_op jit(solution)/shard_map/ppermute | solution.py:453
  43.1 7.4 %collective-permute-start.11 = (f32[8,128]{1,0:T(8,128)S(1)}, f32[8,128]{1,0:T(8,128)S(1)}, u32[]{:S(2)}, u32[]{:S(2)}) collective-permute-start(f32[8,128]{1,0:T(8,128)S(1)} %add_four.3.here_ref), channel_id=1, source_target_pairs={{0,112},{16,96},{32,80},{48,64},{64,48},{80,32},{96,16},{112,0},{1... | collective-permute-start | bytes 12296 | tf_op jit(solution)/shard_map/ppermute | solution.py:453
  56.9 46.0 %collective-permute-start.12 = (f32[2048,256]{1,0:T(8,128)S(1)}, f32[2048,256]{1,0:T(8,128)S(1)}, u32[]{:S(2)}, u32[]{:S(2)}) collective-permute-start(f32[2048,256]{1,0:T(8,128)S(1)} %get-tuple-element.53.up), channel_id=1, source_target_pairs={{0,1},{1,2},{2,3},{3,4},{4,5},{5,6},{6,7},{7,8},{8,9},{9,10},{10,1... | collective-permute-start | bytes 6291464 | tf_op jit(solution)/shard_map/ppermute | solution.py:448
  57.0 45.9 %collective-permute-start.13 = (f32[2048,256]{1,0:T(8,128)S(1)}, f32[2048,256]{1,0:T(8,128)S(1)}, u32[]{:S(2)}, u32[]{:S(2)}) collective-permute-start(f32[2048,256]{1,0:T(8,128)S(1)} %get-tuple-element.54.down), channel_id=1, source_target_pairs={{0,15},{1,0},{2,1},{3,2},{4,3},{5,4},{6,5},{7,6},{8,7},{9,8},{10,9... | collective-permute-start | bytes 6291464 | tf_op jit(solution)/shard_map/ppermute | solution.py:448
  60.8 13.8 %collective-permute-start.14 = (f32[2,128,512]{2,1,0:T(8,128)S(1)}, f32[2,128,512]{2,1,0:T(8,128)S(1)}, u32[]{:S(2)}, u32[]{:S(2)}) collective-permute-start(f32[2,128,512]{2,1,0:T(8,128)S(1)} %get-tuple-element.57), channel_id=1, source_target_pairs={{0,32},{16,48},{32,0},{48,16},{64,96},{80,112},{96,64},{112,80},{1... | collective-permute-start | bytes 1572872 | tf_op jit(solution)/shard_map/ppermute | solution.py:453
  60.9 14.9 %collective-permute-start.15 = (f32[2,128,512]{2,1,0:T(8,128)S(1)}, f32[2,128,512]{2,1,0:T(8,128)S(1)}, u32[]{:S(2)}, u32[]{:S(2)}) collective-permute-start(f32[2,128,512]{2,1,0:T(8,128)S(1)} %get-tuple-element.58), channel_id=1, source_target_pairs={{0,96},{16,112},{32,64},{48,80},{64,32},{80,48},{96,0},{112,16},{1... | collective-permute-start | bytes 1572872 | tf_op jit(solution)/shard_map/ppermute | solution.py:453
  73.1 14.9 %collective-permute-start.18 = (f32[2,128,512]{2,1,0:T(8,128)S(1)}, f32[2,128,512]{2,1,0:T(8,128)S(1)}, u32[]{:S(2)}, u32[]{:S(2)}) collective-permute-start(f32[2,128,512]{2,1,0:T(8,128)S(1)} %get-tuple-element.64), channel_id=1, source_target_pairs={{0,32},{16,48},{32,0},{48,16},{64,96},{80,112},{96,64},{112,80},{1... | collective-permute-start | bytes 1572872 | tf_op jit(solution)/shard_map/ppermute | solution.py:453
  74.6 15.0 %collective-permute-start.20 = (f32[2,128,512]{2,1,0:T(8,128)S(1)}, f32[2,128,512]{2,1,0:T(8,128)S(1)}, u32[]{:S(2)}, u32[]{:S(2)}) collective-permute-start(f32[2,128,512]{2,1,0:T(8,128)S(1)} %get-tuple-element.68), channel_id=1, source_target_pairs={{0,96},{16,112},{32,64},{48,80},{64,32},{80,48},{96,0},{112,16},{1... | collective-permute-start | bytes 1572872 | tf_op jit(solution)/shard_map/ppermute | solution.py:453
  76.0 15.9 %collective-permute-start.22 = (f32[128,512]{1,0:T(8,128)S(1)}, f32[128,512]{1,0:T(8,128)S(1)}, u32[]{:S(2)}, u32[]{:S(2)}) collective-permute-start(f32[128,512]{1,0:T(8,128)S(1)} %get-tuple-element.72), channel_id=1, source_target_pairs={{0,32},{16,48},{32,0},{48,16},{64,96},{80,112},{96,64},{112,80},{1... | collective-permute-start | bytes 786440 | tf_op jit(solution)/shard_map/ppermute | solution.py:453
  88.1 7.7 %collective-permute-start.19 = (f32[128,512]{1,0:T(8,128)S(1)}, f32[128,512]{1,0:T(8,128)S(1)}, u32[]{:S(2)}, u32[]{:S(2)}) collective-permute-start(f32[128,512]{1,0:T(8,128)S(1)} %get-tuple-element.66), channel_id=1, source_target_pairs={{0,96},{16,112},{32,64},{48,80},{64,32},{80,48},{96,0},{112,16},{1... | collective-permute-start | bytes 786440 | tf_op jit(solution)/shard_map/ppermute | solution.py:453
  89.7 6.5 %collective-permute-start.21 = (f32[128,512]{1,0:T(8,128)S(1)}, f32[128,512]{1,0:T(8,128)S(1)}, u32[]{:S(2)}, u32[]{:S(2)}) collective-permute-start(f32[128,512]{1,0:T(8,128)S(1)} %get-tuple-element.70), channel_id=1, source_target_pairs={{0,32},{16,48},{32,0},{48,16},{64,96},{80,112},{96,64},{112,80},{1... | collective-permute-start | bytes 786440 | tf_op jit(solution)/shard_map/ppermute | solution.py:453
  91.9 9.6 %collective-permute-start.16 = (f32[2,64,512]{2,1,0:T(8,128)S(1)}, f32[2,64,512]{2,1,0:T(8,128)S(1)}, u32[]{:S(2)}, u32[]{:S(2)}) collective-permute-start(f32[2,64,512]{2,1,0:T(8,128)S(1)} %get-tuple-element.61), channel_id=1, source_target_pairs={{0,16},{16,0},{32,48},{48,32},{64,80},{80,64},{96,112},{112,96},{1... | collective-permute-start | bytes 786440 | tf_op jit(solution)/shard_map/ppermute | solution.py:453
  96.2 11.6 %collective-permute-start.23 = (f32[3,64,512]{2,1,0:T(8,128)S(1)}, f32[3,64,512]{2,1,0:T(8,128)S(1)}, u32[]{:S(2)}, u32[]{:S(2)}) collective-permute-start(f32[3,64,512]{2,1,0:T(8,128)S(1)} %get-tuple-element.74), channel_id=1, source_target_pairs={{0,16},{16,0},{32,48},{48,32},{64,80},{80,64},{96,112},{112,96},{1... | collective-permute-start | bytes 1179656 | tf_op jit(solution)/shard_map/ppermute | solution.py:453
  101.5 6.3 %collective-permute-start.17 = (f32[64,512]{1,0:T(8,128)S(1)}, f32[64,512]{1,0:T(8,128)S(1)}, u32[]{:S(2)}, u32[]{:S(2)}) collective-permute-start(f32[64,512]{1,0:T(8,128)S(1)} %get-tuple-element.63), channel_id=1, source_target_pairs={{0,96},{16,112},{32,64},{48,80},{64,32},{80,48},{96,0},{112,16},{1... | collective-permute-start | bytes 393224 | tf_op jit(solution)/shard_map/ppermute | solution.py:453

commit v6 on v5

--- a/solution.py
+++ b/solution.py
@@ -138,11 +138,24 @@
 
 def half_gram(nh, nl):
     turned = nh.T
-    return jnp.dot(
-        jnp.concatenate([turned, turned], axis=1),
-        jnp.concatenate([nh * jnp.bfloat16(0.5), nl], axis=0),
-        preferred_element_type=jnp.float32,
+    half = nh * jnp.bfloat16(0.5)
+    top, bottom = turned[:BW], turned[BW:]
+    dot = functools.partial(jnp.dot, preferred_element_type=jnp.float32)
+    upper = jnp.concatenate([half[:, :BW], nh[:, BW:]], axis=1)
+    above = dot(
+        jnp.concatenate([top, top], axis=1), jnp.concatenate([upper, nl], axis=0)
     )
+    below = jnp.concatenate(
+        [
+            dot(bottom, nl[:, :BW]),
+            dot(
+                jnp.concatenate([bottom, bottom], axis=1),
+                jnp.concatenate([half[:, BW:], nl[:, BW:]], axis=0),
+            ),
+        ],
+        axis=1,
+    )
+    return jnp.concatenate([above, below], axis=0)
 
 
 def cut_gram(total_rows, pair, gram_acc, mine, other):
@@ -456,7 +469,7 @@
 def shift_aside(x, by):
     frames, holders = lax.axis_size("frame"), lax.axis_size("pair")
     pairs = [
-        (f * holders + h, (f ^ 6) * holders + (h + by) % holders)
+        (f * holders + h, (f ^ 2) * holders + (h + by) % holders)
         for f in range(frames)
         for h in range(holders)
     ]
@@ -508,7 +521,7 @@
     kept, own = stay(plan, high, low, rot)
     mixed = mix(own, shift_aside(up_sums, 1), shift_aside(down_sums, -1))
     halves = [gram(total_rows, pair, kept, sent) for pair, sent in enumerate((up, down))]
-    tiles = all_sum(mixed, 7, (halves[0][0],))
+    tiles = all_sum(mixed, 3, (halves[0][0],))
     rot = scaled(total_rows, 1, tiles, rotations, plan, (halves[1][0],))
     up, down, high, low = send_again(plan, kept, *moved, rot, halves[0][0])
     moved = shift(up, 1), shift(down, -1)

time: 109 us -> 108 us (level)
  starting transfers between devices: 44.7 us -> 42.6 us
  waiting for transfers between devices: 24.9 us -> 26.5 us
    ppermute x4, waiting for transfers between devices: 0.01 us -> 1.46 us  [shift(): return lax.ppermute(x, 'pair', [(i, (i + by) % size) for i in range(size)])]
    ppermute x2, starting transfers between devices: 5.96 us -> 4.75 us  [shift_aside(): return lax.ppermute(x, ('frame', 'pair'), pairs)]
  transfers between devices with their start and end apart: 24 -> 24, of which waited for: 10 -> 12; matrix products, arithmetic and copies ran while one was open for 0% -> 0% of each run, Pallas kernels for 21% -> 21%
where the time goes in v6:
time: 108 us
  starting transfers between devices  42.6 us (39%)
  Pallas kernels  37.6 us (35%)
  waiting for transfers between devices  26.5 us (25%)
    ppermute x18, starting transfers between devices, swap(): return lax.ppermute(x, 'frame', [(i, i ^ bit) for i in range(size)])  29.9 us
    ppermute x18, waiting for transfers between devices, swap(): return lax.ppermute(x, 'frame', [(i, i ^ bit) for i in range(size)])  25 us
    pallas_call x1, Pallas kernels, stay_again(): pl.pallas_call(functools.partial(stay_again_kernel, total_rows), in_specs...  10.2 us
    ppermute x4, starting transfers between devices, shift(): return lax.ppermute(x, 'pair', [(i, (i + by) % size) for i in range(size)])  7.92 us
    pallas_call x1, Pallas kernels, send_again(): pl.pallas_call(send_again_kernel, in_specs=[in_smem] + [in_vmem] * 5 + [a...  5.3 us
    pallas_call x2, Pallas kernels, gram(): pl.pallas_call(functools.partial(gram_kernel, total_rows, pair), in_specs...  4.82 us
    ppermute x2, starting transfers between devices, shift_aside(): return lax.ppermute(x, ('frame', 'pair'), pairs)  4.75 us
    pallas_call x1, Pallas kernels, stay(): pl.pallas_call(stay_kernel, in_specs=[in_smem] + [in_vmem] * 3, out_specs...  4.08 us
  transfers between devices with their start and end apart: 24, of which 12 were waited for; matrix products, arithmetic and copies ran while one was open for 0% of the time, Pallas kernels for 21%

profile of v6, /device:TPU:0, one launch (start us, length us, event | category | flops | bytes accessed | tf_op | source)
XLA Modules:
  0.0 107.5 jit_solution(8045365771388559752)
XLA Ops:
  0.6 0.0 copy-start.1
  0.6 3.8 %first.1 = (bf16[4,2048,256]{2,1,0:T(8,128)(2,1)S(1)}, bf16[4,2048,256]{2,1,0:T(8,128)(2,1)S(1)}, f32[8,128]{1,0:T(8,128)S(1)}) custom-call(f32[2048,1024]{1,0:T(8,128)} %x_ref.1), custom_call_target="tpu_custom_call" | custom-call | flops 1024 | bytes 1024 | tf_op jit(solution)/shard_map/first/pallas_call | solution.py:80
  4.5 3.2 %collective-permute-start.2 = (f32[8,128]{1,0:T(8,128)S(1)}, f32[8,128]{1,0:T(8,128)S(1)}, u32[]{:S(2)}, u32[]{:S(2)}) collective-permute-start(f32[8,128]{1,0:T(8,128)S(1)} %get-tuple-element.41.a), channel_id=1, source_target_pairs={{0,64},{16,80},{32,96},{48,112},{64,0},{80,16},{96,32},{112,48},{1... | collective-permute-start | bytes 12296 | tf_op jit(solution)/shard_map/ppermute | solution.py:466
  7.7 1.1 %collective-permute-start.1 = (f32[8,128]{1,0:T(8,128)S(1)}, f32[8,128]{1,0:T(8,128)S(1)}, u32[]{:S(2)}, u32[]{:S(2)}) collective-permute-start(f32[8,128]{1,0:T(8,128)S(1)} %get-tuple-element.41.a), channel_id=1, source_target_pairs={{0,96},{16,112},{32,64},{48,80},{64,32},{80,48},{96,0},{112,16},{1... | collective-permute-start | bytes 12296 | tf_op jit(solution)/shard_map/ppermute | solution.py:466
  8.8 0.0 collective-permute-start
  8.8 0.9 collective-permute-done.2.d
  9.7 2.8 %collective-permute-done.1.c = f32[8,128]{1,0:T(8,128)S(1)} collective-permute-done((f32[8,128]{1,0:T(8,128)S(1)}, f32[8,128]{1,0:T(8,128)S(1)}, u32[]{:S(2)}, u32[]{:S(2)}) %collective-permute-start.1) | collective-permute-done | bytes 4128 | tf_op jit(solution)/shard_map/ppermute | solution.py:466
  12.5 0.0 collective-permute-done.b
  12.5 3.3 %collective-permute-start.3 = (f32[8,128]{1,0:T(8,128)S(1)}, f32[8,128]{1,0:T(8,128)S(1)}, u32[]{:S(2)}, u32[]{:S(2)}) collective-permute-start(f32[8,128]{1,0:T(8,128)S(1)} %add_four.2.here_ref), channel_id=1, source_target_pairs={{0,16},{16,0},{32,48},{48,32},{64,80},{80,64},{96,112},{112,96},{1... | collective-permute-start | bytes 12296 | tf_op jit(solution)/shard_map/ppermute | solution.py:466
  15.8 1.9 %collective-permute-done.3.there_ref = f32[8,128]{1,0:T(8,128)S(1)} collective-permute-done((f32[8,128]{1,0:T(8,128)S(1)}, f32[8,128]{1,0:T(8,128)S(1)}, u32[]{:S(2)}, u32[]{:S(2)}) %collective-permute-start.3) | collective-permute-done | bytes 4128 | tf_op jit(solution)/shard_map/ppermute | solution.py:466
  17.7 1.1 scale.2.rot_ref
  18.8 4.0 %send.1 = (f32[2048,256]{1,0:T(8,128)S(1)}, f32[2048,256]{1,0:T(8,128)S(1)}, f32[8,256]{1,0:T(8,128)S(1)}, f32[8,256]{1,0:T(8,128)S(1)}) custom-call(s32[2,1,4]{2,1,0:T(1,128)S(1)} %copy-done.1, bf16[4,2048,256]{2,1,0:T(8,128)(2,1)S(1)} %get-tuple-element.39.high_ref, bf16[4,2048,256]{2,1,0:T(8,128)(2,1)S(1)} %get-tuple-element.40.low_ref, ...), custom_call_target="tpu_custom_call" | custom-call | flops 1024 | bytes 1024 | tf_op jit(solution)/shard_map/send/pallas_call | solution.py:188
  22.8 0.1 collective-permute-start.4
  22.8 3.8 %collective-permute-start.5 = (f32[2048,256]{1,0:T(8,128)S(1)}, f32[2048,256]{1,0:T(8,128)S(1)}, u32[]{:S(2)}, u32[]{:S(2)}) collective-permute-start(f32[2048,256]{1,0:T(8,128)S(1)} %get-tuple-element.45.sent_ref), channel_id=1, source_target_pairs={{0,15},{1,0},{2,1},{3,2},{4,3},{5,4},{6,5},{7,6},{8,7},{9,8},{10,9... | collective-permute-start | bytes 6291464 | tf_op jit(solution)/shard_map/ppermute | solution.py:461
  26.7 0.0 collective-permute-start.6
  26.7 4.8 %collective-permute-start.7 = (f32[8,256]{1,0:T(8,128)S(1)}, f32[8,256]{1,0:T(8,128)S(1)}, u32[]{:S(2)}, u32[]{:S(2)}) collective-permute-start(f32[8,256]{1,0:T(8,128)S(1)} %get-tuple-element.48), channel_id=1, source_target_pairs={{0,47},{1,32},{2,33},{3,34},{4,35},{5,36},{6,37},{7,38},{8,39},{9,... | collective-permute-start | bytes 24584 | tf_op jit(solution)/shard_map/ppermute | solution.py:476
  31.4 4.1 %stay.1 = (bf16[2,2048,256]{2,1,0:T(8,128)(2,1)S(1)}, bf16[2,2048,256]{2,1,0:T(8,128)(2,1)S(1)}, f32[8,128]{1,0:T(8,128)S(1)}) custom-call(s32[2,1,4]{2,1,0:T(1,128)S(1)} %copy-done.1, bf16[4,2048,256]{2,1,0:T(8,128)(2,1)S(1)} %get-tuple-element.39.high_ref, bf16[4,2048,256]{2,1,0:T(8,128)(2,1)S(1)} %get-tuple-element.40.low_ref, ...), custom_call_target="tpu_custom_call" | custom-call | flops 1024 | bytes 1024 | tf_op jit(solution)/shard_map/stay/pallas_call | solution.py:217
  35.5 0.0 collective-permute-done.6.before
  35.5 0.0 collective-permute-done.7.after
  35.6 1.5 %collective-permute-start.10 = (f32[8,128]{1,0:T(8,128)S(1)}, f32[8,128]{1,0:T(8,128)S(1)}, u32[]{:S(2)}, u32[]{:S(2)}) collective-permute-start(f32[8,128]{1,0:T(8,128)S(1)} %mix.1.a), channel_id=1, source_target_pairs={{0,64},{16,80},{32,96},{48,112},{64,0},{80,16},{96,32},{112,48},{1... | collective-permute-start | bytes 12296 | tf_op jit(solution)/shard_map/ppermute | solution.py:466
  37.0 1.1 %collective-permute-start.9 = (f32[8,128]{1,0:T(8,128)S(1)}, f32[8,128]{1,0:T(8,128)S(1)}, u32[]{:S(2)}, u32[]{:S(2)}) collective-permute-start(f32[8,128]{1,0:T(8,128)S(1)} %mix.1.a), channel_id=1, source_target_pairs={{0,96},{16,112},{32,64},{48,80},{64,32},{80,48},{96,0},{112,16},{1... | collective-permute-start | bytes 12296 | tf_op jit(solution)/shard_map/ppermute | solution.py:466
  38.2 1.0 collective-permute-start.8
  39.1 2.4 %gram.2 = (f32[2,128,512]{2,1,0:T(8,128)S(1)}, f32[2,128,512]{2,1,0:T(8,128)S(1)}) custom-call(bf16[2,2048,256]{2,1,0:T(8,128)(2,1)S(1)} %get-tuple-element.42.kept_high, bf16[2,2048,256]{2,1,0:T(8,128)(2,1)S(1)} %get-tuple-element.43.kept_low, f32[2048,256]{1,0:T(8,128)S(1)} %get-tuple-element.44.sent_ref), custom_call_target="tpu_custom_call" | custom-call | flops 1024 | bytes 1024 | tf_op jit(solution)/shard_map/gram/pallas_call | solution.py:243
  41.6 0.0 collective-permute-done.10.d
  41.6 0.3 collective-permute-done.9.c
  41.8 0.0 collective-permute-done.8.b
  41.9 3.5 %collective-permute-start.11 = (f32[8,128]{1,0:T(8,128)S(1)}, f32[8,128]{1,0:T(8,128)S(1)}, u32[]{:S(2)}, u32[]{:S(2)}) collective-permute-start(f32[8,128]{1,0:T(8,128)S(1)} %add_four.3.here_ref), channel_id=1, source_target_pairs={{0,48},{16,32},{32,16},{48,0},{64,112},{80,96},{96,80},{112,64},{1... | collective-permute-start | bytes 12296 | tf_op jit(solution)/shard_map/ppermute | solution.py:466
  45.4 2.4 %gram.3 = (f32[2,128,512]{2,1,0:T(8,128)S(1)}, f32[2,128,512]{2,1,0:T(8,128)S(1)}) custom-call(bf16[2,2048,256]{2,1,0:T(8,128)(2,1)S(1)} %get-tuple-element.42.kept_high, bf16[2,2048,256]{2,1,0:T(8,128)(2,1)S(1)} %get-tuple-element.43.kept_low, f32[2048,256]{1,0:T(8,128)S(1)} %get-tuple-element.45.sent_ref), custom_call_target="tpu_custom_call" | custom-call | flops 1024 | bytes 1024 | tf_op jit(solution)/shard_map/gram/pallas_call | solution.py:243
  47.8 0.3 collective-permute-done.11.there_ref
  48.0 1.1 scale.3.rot_ref
  49.1 1.4 %collective-permute-done.4.up_in = f32[2048,256]{1,0:T(8,128)S(1)} collective-permute-done((f32[2048,256]{1,0:T(8,128)S(1)}, f32[2048,256]{1,0:T(8,128)S(1)}, u32[]{:S(2)}, u32[]{:S(2)}) %collective-permute-start.4) | collective-permute-done | bytes 2097184 | tf_op jit(solution)/shard_map/ppermute | solution.py:461
  50.6 0.0 collective-permute-done.5.down_in
  50.6 5.3 %send_again.1 = (f32[2048,256]{1,0:T(8,128)S(1)}, f32[2048,256]{1,0:T(8,128)S(1)}, bf16[4,2048,256]{2,1,0:T(8,128)(2,1)S(1)}, bf16[4,2048,256]{2,1,0:T(8,128)(2,1)S(1)}) custom-call(s32[2,1,4]{2,1,0:T(1,128)S(1)} %copy-done.1, bf16[2,2048,256]{2,1,0:T(8,128)(2,1)S(1)} %get-tuple-element.42.kept_high, bf16[2,2048,256]{2,1,0:T(8,128)(2,1)S(1)} %get-tuple-element.43.kept_low, ...), custom_call_target="tpu_custom_call" | custom-call | flops 1024 | bytes 1024 | tf_op jit(solution)/shard_map/send_again/pallas_call | solution.py:272
  55.9 0.2 collective-permute-start.12
  56.1 3.8 %collective-permute-start.13 = (f32[2048,256]{1,0:T(8,128)S(1)}, f32[2048,256]{1,0:T(8,128)S(1)}, u32[]{:S(2)}, u32[]{:S(2)}) collective-permute-start(f32[2048,256]{1,0:T(8,128)S(1)} %get-tuple-element.54.down), channel_id=1, source_target_pairs={{0,15},{1,0},{2,1},{3,2},{4,3},{5,4},{6,5},{7,6},{8,7},{9,8},{10,9... | collective-permute-start | bytes 6291464 | tf_op jit(solution)/shard_map/ppermute | solution.py:461
  59.9 0.0 collective-permute-start.14
  59.9 1.9 %collective-permute-start.15 = (f32[2,128,512]{2,1,0:T(8,128)S(1)}, f32[2,128,512]{2,1,0:T(8,128)S(1)}, u32[]{:S(2)}, u32[]{:S(2)}) collective-permute-start(f32[2,128,512]{2,1,0:T(8,128)S(1)} %get-tuple-element.58), channel_id=1, source_target_pairs={{0,96},{16,112},{32,64},{48,80},{64,32},{80,48},{96,0},{112,16},{1... | collective-permute-start | bytes 1572872 | tf_op jit(solution)/shard_map/ppermute | solution.py:466
  61.8 10.2 %stay_again.1 = (f32[2048,1024]{1,0:T(8,128)}, f32[2,128,512]{2,1,0:T(8,128)S(1)}, f32[2,128,512]{2,1,0:T(8,128)S(1)}, f32[2,128,512]{2,1,0:T(8,128)S(1)}, f32[2,128,512]{2,1,0:T(8,128)S(1)}) custom-call(s32[2,1,4]{2,1,0:T(1,128)S(1)} %copy-done.1, bf16[4,2048,256]{2,1,0:T(8,128)(2,1)S(1)} %get-tuple-element.51.high_ref, ...), custom_call_target="tpu_custom_call" | custom-call | flops 1024 | bytes 1024 | tf_op jit(solution)/shard_map/stay_again/pallas_call | solution.py:314
  72.0 1.5 %collective-permute-start.18 = (f32[2,128,512]{2,1,0:T(8,128)S(1)}, f32[2,128,512]{2,1,0:T(8,128)S(1)}, u32[]{:S(2)}, u32[]{:S(2)}) collective-permute-start(f32[2,128,512]{2,1,0:T(8,128)S(1)} %get-tuple-element.64), channel_id=1, source_target_pairs={{0,32},{16,48},{32,0},{48,16},{64,96},{80,112},{96,64},{112,80},{1... | collective-permute-start | bytes 1572872 | tf_op jit(solution)/shard_map/ppermute | solution.py:466
  73.5 0.0 collective-permute-done.14.got0
  73.5 1.3 %collective-permute-start.20 = (f32[2,128,512]{2,1,0:T(8,128)S(1)}, f32[2,128,512]{2,1,0:T(8,128)S(1)}, u32[]{:S(2)}, u32[]{:S(2)}) collective-permute-start(f32[2,128,512]{2,1,0:T(8,128)S(1)} %get-tuple-element.68), channel_id=1, source_target_pairs={{0,96},{16,112},{32,64},{48,80},{64,32},{80,48},{96,0},{112,16},{1... | collective-permute-start | bytes 1572872 | tf_op jit(solution)/shard_map/ppermute | solution.py:466
  74.8 0.0 collective-permute-done.15.got1
  74.8 0.1 begin.1
  74.9 0.1 collective-permute-start.22
  75.0 11.9 %collective-permute-done.18.got = f32[2,128,512]{2,1,0:T(8,128)S(1)} collective-permute-done((f32[2,128,512]{2,1,0:T(8,128)S(1)}, f32[2,128,512]{2,1,0:T(8,128)S(1)}, u32[]{:S(2)}, u32[]{:S(2)}) %collective-permute-start.18) | collective-permute-done | bytes 524320 | tf_op jit(solution)/shard_map/ppermute | solution.py:466
  86.9 0.1 add.4
  87.0 1.4 %collective-permute-start.19 = (f32[128,512]{1,0:T(8,128)S(1)}, f32[128,512]{1,0:T(8,128)S(1)}, u32[]{:S(2)}, u32[]{:S(2)}) collective-permute-start(f32[128,512]{1,0:T(8,128)S(1)} %get-tuple-element.66), channel_id=1, source_target_pairs={{0,96},{16,112},{32,64},{48,80},{64,32},{80,48},{96,0},{112,16},{1... | collective-permute-start | bytes 786440 | tf_op jit(solution)/shard_map/ppermute | solution.py:466
  88.4 0.0 collective-permute-done.20.got
  88.4 0.1 add.5
  88.4 0.9 collective-permute-start.21
  89.3 1.4 %collective-permute-done.22.refs_5_ = f32[128,512]{1,0:T(8,128)S(1)} collective-permute-done((f32[128,512]{1,0:T(8,128)S(1)}, f32[128,512]{1,0:T(8,128)S(1)}, u32[]{:S(2)}, u32[]{:S(2)}) %collective-permute-start.22) | collective-permute-done | bytes 262176 | tf_op jit(solution)/shard_map/ppermute | solution.py:466
  90.8 3.2 %collective-permute-start.16 = (f32[2,64,512]{2,1,0:T(8,128)S(1)}, f32[2,64,512]{2,1,0:T(8,128)S(1)}, u32[]{:S(2)}, u32[]{:S(2)}) collective-permute-start(f32[2,64,512]{2,1,0:T(8,128)S(1)} %get-tuple-element.61), channel_id=1, source_target_pairs={{0,16},{16,0},{32,48},{48,32},{64,80},{80,64},{96,112},{112,96},{1... | collective-permute-start | bytes 786440 | tf_op jit(solution)/shard_map/ppermute | solution.py:466
  93.9 0.7 collective-permute-done.19.refs_1_
  94.7 0.2 collective-permute-done.21.refs_3_
  94.9 0.1 halve.1
  95.0 3.6 %collective-permute-start.23 = (f32[3,64,512]{2,1,0:T(8,128)S(1)}, f32[3,64,512]{2,1,0:T(8,128)S(1)}, u32[]{:S(2)}, u32[]{:S(2)}) collective-permute-start(f32[3,64,512]{2,1,0:T(8,128)S(1)} %get-tuple-element.74), channel_id=1, source_target_pairs={{0,16},{16,0},{32,48},{48,32},{64,80},{80,64},{96,112},{112,96},{1... | collective-permute-start | bytes 1179656 | tf_op jit(solution)/shard_map/ppermute | solution.py:466
  98.6 1.8 %collective-permute-done.16.got = f32[2,64,512]{2,1,0:T(8,128)S(1)} collective-permute-done((f32[2,64,512]{2,1,0:T(8,128)S(1)}, f32[2,64,512]{2,1,0:T(8,128)S(1)}, u32[]{:S(2)}, u32[]{:S(2)}) %collective-permute-start.16) | collective-permute-done | bytes 262176 | tf_op jit(solution)/shard_map/ppermute | solution.py:466
  100.4 1.4 %collective-permute-start.17 = (f32[64,512]{1,0:T(8,128)S(1)}, f32[64,512]{1,0:T(8,128)S(1)}, u32[]{:S(2)}, u32[]{:S(2)}) collective-permute-start(f32[64,512]{1,0:T(8,128)S(1)} %get-tuple-element.63), channel_id=1, source_target_pairs={{0,96},{16,112},{32,64},{48,80},{64,32},{80,48},{96,0},{112,16},{1... | collective-permute-start | bytes 393224 | tf_op jit(solution)/shard_map/ppermute | solution.py:466
  101.7 0.0 collective-permute-done.12.up
  101.7 0.0 collective-permute-done.13.down
  101.7 2.0 %fill.1 = (f32[2048,1024]{1,0:T(8,128)}, f32[8,128]{1,0:T(8,128)S(1)}) custom-call(f32[2048,1024]{1,0:T(8,128)} %get-tuple-element.55._, f32[2048,256]{1,0:T(8,128)S(1)} %collective-permute-done.12.up, f32[2048,256]{1,0:T(8,128)S(1)} %collective-permute-done.13.down), custom_call_target="tpu_custom_call", output_to_operand_aliasing={{0}: (0, {})} | custom-call | flops 1024 | bytes 1024 | tf_op jit(solution)/shard_map/fill/pallas_call | solution.py:427
  103.8 2.8 %collective-permute-done.17.early_got = f32[64,512]{1,0:T(8,128)S(1)} collective-permute-done((f32[64,512]{1,0:T(8,128)S(1)}, f32[64,512]{1,0:T(8,128)S(1)}, u32[]{:S(2)}, u32[]{:S(2)}) %collective-permute-start.17) | collective-permute-done | bytes 131104 | tf_op jit(solution)/shard_map/ppermute | solution.py:466
  106.6 0.0 collective-permute-done.23.got
  106.6 0.9 finish.1
  (7 shorter events, 0.1 us)
Async XLA Ops:
  0.6 17.1 %copy-start.1 = (s32[2,1,4]{2,1,0:T(1,128)S(1)}, s32[2,1,4]{2,1,0:T(1,128)}, u32[]{:S(2)}) copy-start(s32[2,1,4]{2,1,0:T(1,128)} %plan_ref.11) | copy-start | bytes 100
  0.6 17.1 %copy-start = (f32[2,2,512,512]{3,2,1,0:T(8,128)S(1)}, f32[2,2,512,512]{3,2,1,0:T(8,128)}, u32[]{:S(2)}) copy-start(f32[2,2,512,512]{3,2,1,0:T(8,128)} %rot_ref.3) | copy-start | bytes 12582916
  4.5 5.2 %collective-permute-start.2 = (f32[8,128]{1,0:T(8,128)S(1)}, f32[8,128]{1,0:T(8,128)S(1)}, u32[]{:S(2)}, u32[]{:S(2)}) collective-permute-start(f32[8,128]{1,0:T(8,128)S(1)} %get-tuple-element.41.a), channel_id=1, source_target_pairs={{0,64},{16,80},{32,96},{48,112},{64,0},{80,16},{96,32},{112,48},{1... | collective-permute-start | bytes 12296 | tf_op jit(solution)/shard_map/ppermute | solution.py:466
  7.7 4.8 %collective-permute-start.1 = (f32[8,128]{1,0:T(8,128)S(1)}, f32[8,128]{1,0:T(8,128)S(1)}, u32[]{:S(2)}, u32[]{:S(2)}) collective-permute-start(f32[8,128]{1,0:T(8,128)S(1)} %get-tuple-element.41.a), channel_id=1, source_target_pairs={{0,96},{16,112},{32,64},{48,80},{64,32},{80,48},{96,0},{112,16},{1... | collective-permute-start | bytes 12296 | tf_op jit(solution)/shard_map/ppermute | solution.py:466
  8.8 3.7 %collective-permute-start = (f32[8,128]{1,0:T(8,128)S(1)}, f32[8,128]{1,0:T(8,128)S(1)}, u32[]{:S(2)}, u32[]{:S(2)}) collective-permute-start(f32[8,128]{1,0:T(8,128)S(1)} %get-tuple-element.41.a), channel_id=1, source_target_pairs={{0,32},{16,48},{32,0},{48,16},{64,96},{80,112},{96,64},{112,80},{1... | collective-permute-start | bytes 12296 | tf_op jit(solution)/shard_map/ppermute | solution.py:466
  12.5 5.2 %collective-permute-start.3 = (f32[8,128]{1,0:T(8,128)S(1)}, f32[8,128]{1,0:T(8,128)S(1)}, u32[]{:S(2)}, u32[]{:S(2)}) collective-permute-start(f32[8,128]{1,0:T(8,128)S(1)} %add_four.2.here_ref), channel_id=1, source_target_pairs={{0,16},{16,0},{32,48},{48,32},{64,80},{80,64},{96,112},{112,96},{1... | collective-permute-start | bytes 12296 | tf_op jit(solution)/shard_map/ppermute | solution.py:466
  22.8 27.8 %collective-permute-start.4 = (f32[2048,256]{1,0:T(8,128)S(1)}, f32[2048,256]{1,0:T(8,128)S(1)}, u32[]{:S(2)}, u32[]{:S(2)}) collective-permute-start(f32[2048,256]{1,0:T(8,128)S(1)} %get-tuple-element.44.sent_ref), channel_id=1, source_target_pairs={{0,1},{1,2},{2,3},{3,4},{4,5},{5,6},{6,7},{7,8},{8,9},{9,10},{10,1... | collective-permute-start | bytes 6291464 | tf_op jit(solution)/shard_map/ppermute | solution.py:461
  22.8 27.7 %collective-permute-start.5 = (f32[2048,256]{1,0:T(8,128)S(1)}, f32[2048,256]{1,0:T(8,128)S(1)}, u32[]{:S(2)}, u32[]{:S(2)}) collective-permute-start(f32[2048,256]{1,0:T(8,128)S(1)} %get-tuple-element.45.sent_ref), channel_id=1, source_target_pairs={{0,15},{1,0},{2,1},{3,2},{4,3},{5,4},{6,5},{7,6},{8,7},{9,8},{10,9... | collective-permute-start | bytes 6291464 | tf_op jit(solution)/shard_map/ppermute | solution.py:461
  26.7 8.8 %collective-permute-start.6 = (f32[8,256]{1,0:T(8,128)S(1)}, f32[8,256]{1,0:T(8,128)S(1)}, u32[]{:S(2)}, u32[]{:S(2)}) collective-permute-start(f32[8,256]{1,0:T(8,128)S(1)} %get-tuple-element.47), channel_id=1, source_target_pairs={{0,33},{1,34},{2,35},{3,36},{4,37},{5,38},{6,39},{7,40},{8,41},{9,... | collective-permute-start | bytes 24584 | tf_op jit(solution)/shard_map/ppermute | solution.py:476
  26.7 8.8 %collective-permute-start.7 = (f32[8,256]{1,0:T(8,128)S(1)}, f32[8,256]{1,0:T(8,128)S(1)}, u32[]{:S(2)}, u32[]{:S(2)}) collective-permute-start(f32[8,256]{1,0:T(8,128)S(1)} %get-tuple-element.48), channel_id=1, source_target_pairs={{0,47},{1,32},{2,33},{3,34},{4,35},{5,36},{6,37},{7,38},{8,39},{9,... | collective-permute-start | bytes 24584 | tf_op jit(solution)/shard_map/ppermute | solution.py:476
  35.6 6.0 %collective-permute-start.10 = (f32[8,128]{1,0:T(8,128)S(1)}, f32[8,128]{1,0:T(8,128)S(1)}, u32[]{:S(2)}, u32[]{:S(2)}) collective-permute-start(f32[8,128]{1,0:T(8,128)S(1)} %mix.1.a), channel_id=1, source_target_pairs={{0,64},{16,80},{32,96},{48,112},{64,0},{80,16},{96,32},{112,48},{1... | collective-permute-start | bytes 12296 | tf_op jit(solution)/shard_map/ppermute | solution.py:466
  37.0 4.8 %collective-permute-start.9 = (f32[8,128]{1,0:T(8,128)S(1)}, f32[8,128]{1,0:T(8,128)S(1)}, u32[]{:S(2)}, u32[]{:S(2)}) collective-permute-start(f32[8,128]{1,0:T(8,128)S(1)} %mix.1.a), channel_id=1, source_target_pairs={{0,96},{16,112},{32,64},{48,80},{64,32},{80,48},{96,0},{112,16},{1... | collective-permute-start | bytes 12296 | tf_op jit(solution)/shard_map/ppermute | solution.py:466
  38.2 3.7 %collective-permute-start.8 = (f32[8,128]{1,0:T(8,128)S(1)}, f32[8,128]{1,0:T(8,128)S(1)}, u32[]{:S(2)}, u32[]{:S(2)}) collective-permute-start(f32[8,128]{1,0:T(8,128)S(1)} %mix.1.a), channel_id=1, source_target_pairs={{0,32},{16,48},{32,0},{48,16},{64,96},{80,112},{96,64},{112,80},{1... | collective-permute-start | bytes 12296 | tf_op jit(solution)/shard_map/ppermute | solution.py:466
  41.9 6.2 %collective-permute-start.11 = (f32[8,128]{1,0:T(8,128)S(1)}, f32[8,128]{1,0:T(8,128)S(1)}, u32[]{:S(2)}, u32[]{:S(2)}) collective-permute-start(f32[8,128]{1,0:T(8,128)S(1)} %add_four.3.here_ref), channel_id=1, source_target_pairs={{0,48},{16,32},{32,16},{48,0},{64,112},{80,96},{96,80},{112,64},{1... | collective-permute-start | bytes 12296 | tf_op jit(solution)/shard_map/ppermute | solution.py:466
  55.9 45.8 %collective-permute-start.12 = (f32[2048,256]{1,0:T(8,128)S(1)}, f32[2048,256]{1,0:T(8,128)S(1)}, u32[]{:S(2)}, u32[]{:S(2)}) collective-permute-start(f32[2048,256]{1,0:T(8,128)S(1)} %get-tuple-element.53.up), channel_id=1, source_target_pairs={{0,1},{1,2},{2,3},{3,4},{4,5},{5,6},{6,7},{7,8},{8,9},{9,10},{10,1... | collective-permute-start | bytes 6291464 | tf_op jit(solution)/shard_map/ppermute | solution.py:461
  56.1 45.7 %collective-permute-start.13 = (f32[2048,256]{1,0:T(8,128)S(1)}, f32[2048,256]{1,0:T(8,128)S(1)}, u32[]{:S(2)}, u32[]{:S(2)}) collective-permute-start(f32[2048,256]{1,0:T(8,128)S(1)} %get-tuple-element.54.down), channel_id=1, source_target_pairs={{0,15},{1,0},{2,1},{3,2},{4,3},{5,4},{6,5},{7,6},{8,7},{9,8},{10,9... | collective-permute-start | bytes 6291464 | tf_op jit(solution)/shard_map/ppermute | solution.py:461
  59.9 13.6 %collective-permute-start.14 = (f32[2,128,512]{2,1,0:T(8,128)S(1)}, f32[2,128,512]{2,1,0:T(8,128)S(1)}, u32[]{:S(2)}, u32[]{:S(2)}) collective-permute-start(f32[2,128,512]{2,1,0:T(8,128)S(1)} %get-tuple-element.57), channel_id=1, source_target_pairs={{0,32},{16,48},{32,0},{48,16},{64,96},{80,112},{96,64},{112,80},{1... | collective-permute-start | bytes 1572872 | tf_op jit(solution)/shard_map/ppermute | solution.py:466
  59.9 14.9 %collective-permute-start.15 = (f32[2,128,512]{2,1,0:T(8,128)S(1)}, f32[2,128,512]{2,1,0:T(8,128)S(1)}, u32[]{:S(2)}, u32[]{:S(2)}) collective-permute-start(f32[2,128,512]{2,1,0:T(8,128)S(1)} %get-tuple-element.58), channel_id=1, source_target_pairs={{0,96},{16,112},{32,64},{48,80},{64,32},{80,48},{96,0},{112,16},{1... | collective-permute-start | bytes 1572872 | tf_op jit(solution)/shard_map/ppermute | solution.py:466
  72.0 14.9 %collective-permute-start.18 = (f32[2,128,512]{2,1,0:T(8,128)S(1)}, f32[2,128,512]{2,1,0:T(8,128)S(1)}, u32[]{:S(2)}, u32[]{:S(2)}) collective-permute-start(f32[2,128,512]{2,1,0:T(8,128)S(1)} %get-tuple-element.64), channel_id=1, source_target_pairs={{0,32},{16,48},{32,0},{48,16},{64,96},{80,112},{96,64},{112,80},{1... | collective-permute-start | bytes 1572872 | tf_op jit(solution)/shard_map/ppermute | solution.py:466
  73.5 14.9 %collective-permute-start.20 = (f32[2,128,512]{2,1,0:T(8,128)S(1)}, f32[2,128,512]{2,1,0:T(8,128)S(1)}, u32[]{:S(2)}, u32[]{:S(2)}) collective-permute-start(f32[2,128,512]{2,1,0:T(8,128)S(1)} %get-tuple-element.68), channel_id=1, source_target_pairs={{0,96},{16,112},{32,64},{48,80},{64,32},{80,48},{96,0},{112,16},{1... | collective-permute-start | bytes 1572872 | tf_op jit(solution)/shard_map/ppermute | solution.py:466
  74.9 15.8 %collective-permute-start.22 = (f32[128,512]{1,0:T(8,128)S(1)}, f32[128,512]{1,0:T(8,128)S(1)}, u32[]{:S(2)}, u32[]{:S(2)}) collective-permute-start(f32[128,512]{1,0:T(8,128)S(1)} %get-tuple-element.72), channel_id=1, source_target_pairs={{0,32},{16,48},{32,0},{48,16},{64,96},{80,112},{96,64},{112,80},{1... | collective-permute-start | bytes 786440 | tf_op jit(solution)/shard_map/ppermute | solution.py:466
  87.0 7.7 %collective-permute-start.19 = (f32[128,512]{1,0:T(8,128)S(1)}, f32[128,512]{1,0:T(8,128)S(1)}, u32[]{:S(2)}, u32[]{:S(2)}) collective-permute-start(f32[128,512]{1,0:T(8,128)S(1)} %get-tuple-element.66), channel_id=1, source_target_pairs={{0,96},{16,112},{32,64},{48,80},{64,32},{80,48},{96,0},{112,16},{1... | collective-permute-start | bytes 786440 | tf_op jit(solution)/shard_map/ppermute | solution.py:466
  88.4 6.5 %collective-permute-start.21 = (f32[128,512]{1,0:T(8,128)S(1)}, f32[128,512]{1,0:T(8,128)S(1)}, u32[]{:S(2)}, u32[]{:S(2)}) collective-permute-start(f32[128,512]{1,0:T(8,128)S(1)} %get-tuple-element.70), channel_id=1, source_target_pairs={{0,32},{16,48},{32,0},{48,16},{64,96},{80,112},{96,64},{112,80},{1... | collective-permute-start | bytes 786440 | tf_op jit(solution)/shard_map/ppermute | solution.py:466
  90.8 9.6 %collective-permute-start.16 = (f32[2,64,512]{2,1,0:T(8,128)S(1)}, f32[2,64,512]{2,1,0:T(8,128)S(1)}, u32[]{:S(2)}, u32[]{:S(2)}) collective-permute-start(f32[2,64,512]{2,1,0:T(8,128)S(1)} %get-tuple-element.61), channel_id=1, source_target_pairs={{0,16},{16,0},{32,48},{48,32},{64,80},{80,64},{96,112},{112,96},{1... | collective-permute-start | bytes 786440 | tf_op jit(solution)/shard_map/ppermute | solution.py:466
  95.0 11.6 %collective-permute-start.23 = (f32[3,64,512]{2,1,0:T(8,128)S(1)}, f32[3,64,512]{2,1,0:T(8,128)S(1)}, u32[]{:S(2)}, u32[]{:S(2)}) collective-permute-start(f32[3,64,512]{2,1,0:T(8,128)S(1)} %get-tuple-element.74), channel_id=1, source_target_pairs={{0,16},{16,0},{32,48},{48,32},{64,80},{80,64},{96,112},{112,96},{1... | collective-permute-start | bytes 1179656 | tf_op jit(solution)/shard_map/ppermute | solution.py:466
  100.4 6.3 %collective-permute-start.17 = (f32[64,512]{1,0:T(8,128)S(1)}, f32[64,512]{1,0:T(8,128)S(1)}, u32[]{:S(2)}, u32[]{:S(2)}) collective-permute-start(f32[64,512]{1,0:T(8,128)S(1)} %get-tuple-element.63), channel_id=1, source_target_pairs={{0,96},{16,112},{32,64},{48,80},{64,32},{80,48},{96,0},{112,16},{1... | collective-permute-start | bytes 393224 | tf_op jit(solution)/shard_map/ppermute | solution.py:466

commit v7 on v6

--- a/solution.py
+++ b/solution.py
@@ -163,7 +163,7 @@
     gram_acc[pair] = (half + half.T) * jnp.float32(1.0 / total_rows)
     x = lax.axis_index("frame") // 2
     near = x + 1 - 2 * (x % 2)
-    blocks = (((x, 3 - x), (near, 3 - near)), ((x, near), (3 - x, 3 - near)))[pair]
+    blocks = (((x, near), (3 - x, 3 - near)), ((x, 3 - x), (near, 3 - near)))[pair]
     for ref, rows in zip((mine, other), blocks):
         for k in range(2):
             row = pl.multiple_of(128 * rows[k], 128)
@@ -493,7 +493,7 @@
     return x, swap(x, across)
 
 
-NEAR = ((2, 6), (6, 2))
+NEAR = ((6, 2), (2, 6))
 
 
 def gram_sums(first_halves, last_halves):

time: 108 us -> 108 us (level)
  transfers between devices with their start and end apart: 24 -> 24, of which waited for: 12 -> 11; matrix products, arithmetic and copies ran while one was open for 0% -> 0% of each run, Pallas kernels for 21% -> 21%
where the time goes in v7:
time: 108 us
  starting transfers between devices  43.2 us (40%)
  Pallas kernels  37.6 us (35%)
  waiting for transfers between devices  26 us (24%)
    ppermute x18, starting transfers between devices, swap(): return lax.ppermute(x, 'frame', [(i, i ^ bit) for i in range(size)])  30.5 us
    ppermute x18, waiting for transfers between devices, swap(): return lax.ppermute(x, 'frame', [(i, i ^ bit) for i in range(size)])  24.5 us
    pallas_call x1, Pallas kernels, stay_again(): pl.pallas_call(functools.partial(stay_again_kernel, total_rows), in_specs...  10.2 us
    ppermute x4, starting transfers between devices, shift(): return lax.ppermute(x, 'pair', [(i, (i + by) % size) for i in range(size)])  7.92 us
    pallas_call x1, Pallas kernels, send_again(): pl.pallas_call(send_again_kernel, in_specs=[in_smem] + [in_vmem] * 5 + [a...  5.3 us
    pallas_call x2, Pallas kernels, gram(): pl.pallas_call(functools.partial(gram_kernel, total_rows, pair), in_specs...  4.82 us
    ppermute x2, starting transfers between devices, shift_aside(): return lax.ppermute(x, ('frame', 'pair'), pairs)  4.75 us
    pallas_call x1, Pallas kernels, stay(): pl.pallas_call(stay_kernel, in_specs=[in_smem] + [in_vmem] * 3, out_specs...  4.08 us
  transfers between devices with their start and end apart: 24, of which 11 were waited for; matrix products, arithmetic and copies ran while one was open for 0% of the time, Pallas kernels for 21%

profile of v7, /device:TPU:0, one launch (start us, length us, event | category | flops | bytes accessed | tf_op | source)
XLA Modules:
  0.0 107.5 jit_solution(7878410834507028066)
XLA Ops:
  0.6 3.8 %first.1 = (bf16[4,2048,256]{2,1,0:T(8,128)(2,1)S(1)}, bf16[4,2048,256]{2,1,0:T(8,128)(2,1)S(1)}, f32[8,128]{1,0:T(8,128)S(1)}) custom-call(f32[2048,1024]{1,0:T(8,128)} %x_ref.1), custom_call_target="tpu_custom_call" | custom-call | flops 1024 | bytes 1024 | tf_op jit(solution)/shard_map/first/pallas_call | solution.py:80
  4.5 3.2 %collective-permute-start.2 = (f32[8,128]{1,0:T(8,128)S(1)}, f32[8,128]{1,0:T(8,128)S(1)}, u32[]{:S(2)}, u32[]{:S(2)}) collective-permute-start(f32[8,128]{1,0:T(8,128)S(1)} %get-tuple-element.41.a), channel_id=1, source_target_pairs={{0,64},{16,80},{32,96},{48,112},{64,0},{80,16},{96,32},{112,48},{1... | collective-permute-start | bytes 12296 | tf_op jit(solution)/shard_map/ppermute | solution.py:466
  7.7 1.1 %collective-permute-start.1 = (f32[8,128]{1,0:T(8,128)S(1)}, f32[8,128]{1,0:T(8,128)S(1)}, u32[]{:S(2)}, u32[]{:S(2)}) collective-permute-start(f32[8,128]{1,0:T(8,128)S(1)} %get-tuple-element.41.a), channel_id=1, source_target_pairs={{0,96},{16,112},{32,64},{48,80},{64,32},{80,48},{96,0},{112,16},{1... | collective-permute-start | bytes 12296 | tf_op jit(solution)/shard_map/ppermute | solution.py:466
  8.8 0.0 collective-permute-start
  8.8 0.9 collective-permute-done.2.d
  9.7 2.8 %collective-permute-done.1.c = f32[8,128]{1,0:T(8,128)S(1)} collective-permute-done((f32[8,128]{1,0:T(8,128)S(1)}, f32[8,128]{1,0:T(8,128)S(1)}, u32[]{:S(2)}, u32[]{:S(2)}) %collective-permute-start.1) | collective-permute-done | bytes 4128 | tf_op jit(solution)/shard_map/ppermute | solution.py:466
  12.5 0.0 collective-permute-done.b
  12.5 3.3 %collective-permute-start.3 = (f32[8,128]{1,0:T(8,128)S(1)}, f32[8,128]{1,0:T(8,128)S(1)}, u32[]{:S(2)}, u32[]{:S(2)}) collective-permute-start(f32[8,128]{1,0:T(8,128)S(1)} %add_four.2.here_ref), channel_id=1, source_target_pairs={{0,16},{16,0},{32,48},{48,32},{64,80},{80,64},{96,112},{112,96},{1... | collective-permute-start | bytes 12296 | tf_op jit(solution)/shard_map/ppermute | solution.py:466
  15.8 1.9 %collective-permute-done.3.there_ref = f32[8,128]{1,0:T(8,128)S(1)} collective-permute-done((f32[8,128]{1,0:T(8,128)S(1)}, f32[8,128]{1,0:T(8,128)S(1)}, u32[]{:S(2)}, u32[]{:S(2)}) %collective-permute-start.3) | collective-permute-done | bytes 4128 | tf_op jit(solution)/shard_map/ppermute | solution.py:466
  17.7 0.0 copy-done.1
  17.7 1.1 scale.2.rot_ref
  18.8 4.0 %send.1 = (f32[2048,256]{1,0:T(8,128)S(1)}, f32[2048,256]{1,0:T(8,128)S(1)}, f32[8,256]{1,0:T(8,128)S(1)}, f32[8,256]{1,0:T(8,128)S(1)}) custom-call(s32[2,1,4]{2,1,0:T(1,128)S(1)} %copy-done.1, bf16[4,2048,256]{2,1,0:T(8,128)(2,1)S(1)} %get-tuple-element.39.high_ref, bf16[4,2048,256]{2,1,0:T(8,128)(2,1)S(1)} %get-tuple-element.40.low_ref, ...), custom_call_target="tpu_custom_call" | custom-call | flops 1024 | bytes 1024 | tf_op jit(solution)/shard_map/send/pallas_call | solution.py:188
  22.8 0.1 collective-permute-start.4
  22.8 3.8 %collective-permute-start.5 = (f32[2048,256]{1,0:T(8,128)S(1)}, f32[2048,256]{1,0:T(8,128)S(1)}, u32[]{:S(2)}, u32[]{:S(2)}) collective-permute-start(f32[2048,256]{1,0:T(8,128)S(1)} %get-tuple-element.45.sent_ref), channel_id=1, source_target_pairs={{0,15},{1,0},{2,1},{3,2},{4,3},{5,4},{6,5},{7,6},{8,7},{9,8},{10,9... | collective-permute-start | bytes 6291464 | tf_op jit(solution)/shard_map/ppermute | solution.py:461
  26.7 0.0 collective-permute-start.6
  26.7 4.8 %collective-permute-start.7 = (f32[8,256]{1,0:T(8,128)S(1)}, f32[8,256]{1,0:T(8,128)S(1)}, u32[]{:S(2)}, u32[]{:S(2)}) collective-permute-start(f32[8,256]{1,0:T(8,128)S(1)} %get-tuple-element.48), channel_id=1, source_target_pairs={{0,47},{1,32},{2,33},{3,34},{4,35},{5,36},{6,37},{7,38},{8,39},{9,... | collective-permute-start | bytes 24584 | tf_op jit(solution)/shard_map/ppermute | solution.py:476
  31.4 4.1 %stay.1 = (bf16[2,2048,256]{2,1,0:T(8,128)(2,1)S(1)}, bf16[2,2048,256]{2,1,0:T(8,128)(2,1)S(1)}, f32[8,128]{1,0:T(8,128)S(1)}) custom-call(s32[2,1,4]{2,1,0:T(1,128)S(1)} %copy-done.1, bf16[4,2048,256]{2,1,0:T(8,128)(2,1)S(1)} %get-tuple-element.39.high_ref, bf16[4,2048,256]{2,1,0:T(8,128)(2,1)S(1)} %get-tuple-element.40.low_ref, ...), custom_call_target="tpu_custom_call" | custom-call | flops 1024 | bytes 1024 | tf_op jit(solution)/shard_map/stay/pallas_call | solution.py:217
  35.5 0.0 collective-permute-done.6.before
  35.5 0.0 collective-permute-done.7.after
  35.6 1.5 %collective-permute-start.10 = (f32[8,128]{1,0:T(8,128)S(1)}, f32[8,128]{1,0:T(8,128)S(1)}, u32[]{:S(2)}, u32[]{:S(2)}) collective-permute-start(f32[8,128]{1,0:T(8,128)S(1)} %mix.1.a), channel_id=1, source_target_pairs={{0,64},{16,80},{32,96},{48,112},{64,0},{80,16},{96,32},{112,48},{1... | collective-permute-start | bytes 12296 | tf_op jit(solution)/shard_map/ppermute | solution.py:466
  37.0 1.1 %collective-permute-start.9 = (f32[8,128]{1,0:T(8,128)S(1)}, f32[8,128]{1,0:T(8,128)S(1)}, u32[]{:S(2)}, u32[]{:S(2)}) collective-permute-start(f32[8,128]{1,0:T(8,128)S(1)} %mix.1.a), channel_id=1, source_target_pairs={{0,96},{16,112},{32,64},{48,80},{64,32},{80,48},{96,0},{112,16},{1... | collective-permute-start | bytes 12296 | tf_op jit(solution)/shard_map/ppermute | solution.py:466
  38.2 1.0 collective-permute-start.8
  39.1 2.4 %gram.2 = (f32[2,128,512]{2,1,0:T(8,128)S(1)}, f32[2,128,512]{2,1,0:T(8,128)S(1)}) custom-call(bf16[2,2048,256]{2,1,0:T(8,128)(2,1)S(1)} %get-tuple-element.42.kept_high, bf16[2,2048,256]{2,1,0:T(8,128)(2,1)S(1)} %get-tuple-element.43.kept_low, f32[2048,256]{1,0:T(8,128)S(1)} %get-tuple-element.44.sent_ref), custom_call_target="tpu_custom_call" | custom-call | flops 1024 | bytes 1024 | tf_op jit(solution)/shard_map/gram/pallas_call | solution.py:243
  41.6 0.0 collective-permute-done.10.d
  41.6 0.3 collective-permute-done.9.c
  41.8 0.0 collective-permute-done.8.b
  41.9 3.5 %collective-permute-start.11 = (f32[8,128]{1,0:T(8,128)S(1)}, f32[8,128]{1,0:T(8,128)S(1)}, u32[]{:S(2)}, u32[]{:S(2)}) collective-permute-start(f32[8,128]{1,0:T(8,128)S(1)} %add_four.3.here_ref), channel_id=1, source_target_pairs={{0,48},{16,32},{32,16},{48,0},{64,112},{80,96},{96,80},{112,64},{1... | collective-permute-start | bytes 12296 | tf_op jit(solution)/shard_map/ppermute | solution.py:466
  45.4 2.4 %gram.3 = (f32[2,128,512]{2,1,0:T(8,128)S(1)}, f32[2,128,512]{2,1,0:T(8,128)S(1)}) custom-call(bf16[2,2048,256]{2,1,0:T(8,128)(2,1)S(1)} %get-tuple-element.42.kept_high, bf16[2,2048,256]{2,1,0:T(8,128)(2,1)S(1)} %get-tuple-element.43.kept_low, f32[2048,256]{1,0:T(8,128)S(1)} %get-tuple-element.45.sent_ref), custom_call_target="tpu_custom_call" | custom-call | flops 1024 | bytes 1024 | tf_op jit(solution)/shard_map/gram/pallas_call | solution.py:243
  47.8 0.3 collective-permute-done.11.there_ref
  48.0 1.1 scale.3.rot_ref
  49.1 1.4 %collective-permute-done.4.up_in = f32[2048,256]{1,0:T(8,128)S(1)} collective-permute-done((f32[2048,256]{1,0:T(8,128)S(1)}, f32[2048,256]{1,0:T(8,128)S(1)}, u32[]{:S(2)}, u32[]{:S(2)}) %collective-permute-start.4) | collective-permute-done | bytes 2097184 | tf_op jit(solution)/shard_map/ppermute | solution.py:461
  50.6 0.0 collective-permute-done.5.down_in
  50.6 5.3 %send_again.1 = (f32[2048,256]{1,0:T(8,128)S(1)}, f32[2048,256]{1,0:T(8,128)S(1)}, bf16[4,2048,256]{2,1,0:T(8,128)(2,1)S(1)}, bf16[4,2048,256]{2,1,0:T(8,128)(2,1)S(1)}) custom-call(s32[2,1,4]{2,1,0:T(1,128)S(1)} %copy-done.1, bf16[2,2048,256]{2,1,0:T(8,128)(2,1)S(1)} %get-tuple-element.42.kept_high, bf16[2,2048,256]{2,1,0:T(8,128)(2,1)S(1)} %get-tuple-element.43.kept_low, ...), custom_call_target="tpu_custom_call" | custom-call | flops 1024 | bytes 1024 | tf_op jit(solution)/shard_map/send_again/pallas_call | solution.py:272
  55.9 0.2 collective-permute-start.12
  56.1 3.8 %collective-permute-start.13 = (f32[2048,256]{1,0:T(8,128)S(1)}, f32[2048,256]{1,0:T(8,128)S(1)}, u32[]{:S(2)}, u32[]{:S(2)}) collective-permute-start(f32[2048,256]{1,0:T(8,128)S(1)} %get-tuple-element.54.down), channel_id=1, source_target_pairs={{0,15},{1,0},{2,1},{3,2},{4,3},{5,4},{6,5},{7,6},{8,7},{9,8},{10,9... | collective-permute-start | bytes 6291464 | tf_op jit(solution)/shard_map/ppermute | solution.py:461
  59.9 1.9 %collective-permute-start.14 = (f32[2,128,512]{2,1,0:T(8,128)S(1)}, f32[2,128,512]{2,1,0:T(8,128)S(1)}, u32[]{:S(2)}, u32[]{:S(2)}) collective-permute-start(f32[2,128,512]{2,1,0:T(8,128)S(1)} %get-tuple-element.57), channel_id=1, source_target_pairs={{0,96},{16,112},{32,64},{48,80},{64,32},{80,48},{96,0},{112,16},{1... | collective-permute-start | bytes 1572872 | tf_op jit(solution)/shard_map/ppermute | solution.py:466
  61.8 0.0 collective-permute-start.15
  61.8 10.2 %stay_again.1 = (f32[2048,1024]{1,0:T(8,128)}, f32[2,128,512]{2,1,0:T(8,128)S(1)}, f32[2,128,512]{2,1,0:T(8,128)S(1)}, f32[2,128,512]{2,1,0:T(8,128)S(1)}, f32[2,128,512]{2,1,0:T(8,128)S(1)}) custom-call(s32[2,1,4]{2,1,0:T(1,128)S(1)} %copy-done.1, bf16[4,2048,256]{2,1,0:T(8,128)(2,1)S(1)} %get-tuple-element.51.high_ref, ...), custom_call_target="tpu_custom_call" | custom-call | flops 1024 | bytes 1024 | tf_op jit(solution)/shard_map/stay_again/pallas_call | solution.py:314
  72.0 1.4 %collective-permute-start.18 = (f32[2,128,512]{2,1,0:T(8,128)S(1)}, f32[2,128,512]{2,1,0:T(8,128)S(1)}, u32[]{:S(2)}, u32[]{:S(2)}) collective-permute-start(f32[2,128,512]{2,1,0:T(8,128)S(1)} %get-tuple-element.64), channel_id=1, source_target_pairs={{0,96},{16,112},{32,64},{48,80},{64,32},{80,48},{96,0},{112,16},{1... | collective-permute-start | bytes 1572872 | tf_op jit(solution)/shard_map/ppermute | solution.py:466
  73.4 0.0 collective-permute-done.14.got0
  73.4 1.4 %collective-permute-start.20 = (f32[2,128,512]{2,1,0:T(8,128)S(1)}, f32[2,128,512]{2,1,0:T(8,128)S(1)}, u32[]{:S(2)}, u32[]{:S(2)}) collective-permute-start(f32[2,128,512]{2,1,0:T(8,128)S(1)} %get-tuple-element.68), channel_id=1, source_target_pairs={{0,32},{16,48},{32,0},{48,16},{64,96},{80,112},{96,64},{112,80},{1... | collective-permute-start | bytes 1572872 | tf_op jit(solution)/shard_map/ppermute | solution.py:466
  74.8 0.0 collective-permute-done.15.got1
  74.8 0.1 begin.1
  74.9 2.0 %collective-permute-start.22 = (f32[128,512]{1,0:T(8,128)S(1)}, f32[128,512]{1,0:T(8,128)S(1)}, u32[]{:S(2)}, u32[]{:S(2)}) collective-permute-start(f32[128,512]{1,0:T(8,128)S(1)} %get-tuple-element.72), channel_id=1, source_target_pairs={{0,96},{16,112},{32,64},{48,80},{64,32},{80,48},{96,0},{112,16},{1... | collective-permute-start | bytes 786440 | tf_op jit(solution)/shard_map/ppermute | solution.py:466
  76.9 11.2 %collective-permute-done.18.got = f32[2,128,512]{2,1,0:T(8,128)S(1)} collective-permute-done((f32[2,128,512]{2,1,0:T(8,128)S(1)}, f32[2,128,512]{2,1,0:T(8,128)S(1)}, u32[]{:S(2)}, u32[]{:S(2)}) %collective-permute-start.18) | collective-permute-done | bytes 524320 | tf_op jit(solution)/shard_map/ppermute | solution.py:466
  88.2 0.1 add.4
  88.2 0.9 collective-permute-start.19
  89.1 0.0 collective-permute-done.20.got
  89.1 0.1 add.5
  89.2 1.4 %collective-permute-start.21 = (f32[128,512]{1,0:T(8,128)S(1)}, f32[128,512]{1,0:T(8,128)S(1)}, u32[]{:S(2)}, u32[]{:S(2)}) collective-permute-start(f32[128,512]{1,0:T(8,128)S(1)} %get-tuple-element.70), channel_id=1, source_target_pairs={{0,96},{16,112},{32,64},{48,80},{64,32},{80,48},{96,0},{112,16},{1... | collective-permute-start | bytes 786440 | tf_op jit(solution)/shard_map/ppermute | solution.py:466
  90.5 1.4 %collective-permute-done.22.refs_5_ = f32[128,512]{1,0:T(8,128)S(1)} collective-permute-done((f32[128,512]{1,0:T(8,128)S(1)}, f32[128,512]{1,0:T(8,128)S(1)}, u32[]{:S(2)}, u32[]{:S(2)}) %collective-permute-start.22) | collective-permute-done | bytes 262176 | tf_op jit(solution)/shard_map/ppermute | solution.py:466
  92.0 3.2 %collective-permute-start.16 = (f32[2,64,512]{2,1,0:T(8,128)S(1)}, f32[2,64,512]{2,1,0:T(8,128)S(1)}, u32[]{:S(2)}, u32[]{:S(2)}) collective-permute-start(f32[2,64,512]{2,1,0:T(8,128)S(1)} %get-tuple-element.61), channel_id=1, source_target_pairs={{0,16},{16,0},{32,48},{48,32},{64,80},{80,64},{96,112},{112,96},{1... | collective-permute-start | bytes 786440 | tf_op jit(solution)/shard_map/ppermute | solution.py:466
  95.2 0.0 collective-permute-done.19.refs_1_
  95.2 1.7 %collective-permute-done.21.refs_3_ = f32[128,512]{1,0:T(8,128)S(1)} collective-permute-done((f32[128,512]{1,0:T(8,128)S(1)}, f32[128,512]{1,0:T(8,128)S(1)}, u32[]{:S(2)}, u32[]{:S(2)}) %collective-permute-start.21) | collective-permute-done | bytes 262176 | tf_op jit(solution)/shard_map/ppermute | solution.py:466
  96.8 0.1 halve.1
  96.9 3.3 %collective-permute-start.23 = (f32[3,64,512]{2,1,0:T(8,128)S(1)}, f32[3,64,512]{2,1,0:T(8,128)S(1)}, u32[]{:S(2)}, u32[]{:S(2)}) collective-permute-start(f32[3,64,512]{2,1,0:T(8,128)S(1)} %get-tuple-element.74), channel_id=1, source_target_pairs={{0,16},{16,0},{32,48},{48,32},{64,80},{80,64},{96,112},{112,96},{1... | collective-permute-start | bytes 1179656 | tf_op jit(solution)/shard_map/ppermute | solution.py:466
  100.2 1.4 %collective-permute-done.16.got = f32[2,64,512]{2,1,0:T(8,128)S(1)} collective-permute-done((f32[2,64,512]{2,1,0:T(8,128)S(1)}, f32[2,64,512]{2,1,0:T(8,128)S(1)}, u32[]{:S(2)}, u32[]{:S(2)}) %collective-permute-start.16) | collective-permute-done | bytes 262176 | tf_op jit(solution)/shard_map/ppermute | solution.py:466
  101.6 0.3 collective-permute-start.17
  101.9 0.0 collective-permute-done.12.up
  101.9 0.0 collective-permute-done.13.down
  101.9 2.0 %fill.1 = (f32[2048,1024]{1,0:T(8,128)}, f32[8,128]{1,0:T(8,128)S(1)}) custom-call(f32[2048,1024]{1,0:T(8,128)} %get-tuple-element.55._, f32[2048,256]{1,0:T(8,128)S(1)} %collective-permute-done.12.up, f32[2048,256]{1,0:T(8,128)S(1)} %collective-permute-done.13.down), custom_call_target="tpu_custom_call", output_to_operand_aliasing={{0}: (0, {})} | custom-call | flops 1024 | bytes 1024 | tf_op jit(solution)/shard_map/fill/pallas_call | solution.py:427
  103.9 2.7 %collective-permute-done.17.early_got = f32[64,512]{1,0:T(8,128)S(1)} collective-permute-done((f32[64,512]{1,0:T(8,128)S(1)}, f32[64,512]{1,0:T(8,128)S(1)}, u32[]{:S(2)}, u32[]{:S(2)}) %collective-permute-start.17) | collective-permute-done | bytes 131104 | tf_op jit(solution)/shard_map/ppermute | solution.py:466
  106.6 0.0 collective-permute-done.23.got
  106.6 0.9 finish.1
  (7 shorter events, 0.1 us)
Async XLA Ops:
  0.6 17.1 %copy-start.1 = (s32[2,1,4]{2,1,0:T(1,128)S(1)}, s32[2,1,4]{2,1,0:T(1,128)}, u32[]{:S(2)}) copy-start(s32[2,1,4]{2,1,0:T(1,128)} %plan_ref.11) | copy-start | bytes 100
  0.6 17.1 %copy-start = (f32[2,2,512,512]{3,2,1,0:T(8,128)S(1)}, f32[2,2,512,512]{3,2,1,0:T(8,128)}, u32[]{:S(2)}) copy-start(f32[2,2,512,512]{3,2,1,0:T(8,128)} %rot_ref.3) | copy-start | bytes 12582916
  4.5 5.2 %collective-permute-start.2 = (f32[8,128]{1,0:T(8,128)S(1)}, f32[8,128]{1,0:T(8,128)S(1)}, u32[]{:S(2)}, u32[]{:S(2)}) collective-permute-start(f32[8,128]{1,0:T(8,128)S(1)} %get-tuple-element.41.a), channel_id=1, source_target_pairs={{0,64},{16,80},{32,96},{48,112},{64,0},{80,16},{96,32},{112,48},{1... | collective-permute-start | bytes 12296 | tf_op jit(solution)/shard_map/ppermute | solution.py:466
  7.7 4.8 %collective-permute-start.1 = (f32[8,128]{1,0:T(8,128)S(1)}, f32[8,128]{1,0:T(8,128)S(1)}, u32[]{:S(2)}, u32[]{:S(2)}) collective-permute-start(f32[8,128]{1,0:T(8,128)S(1)} %get-tuple-element.41.a), channel_id=1, source_target_pairs={{0,96},{16,112},{32,64},{48,80},{64,32},{80,48},{96,0},{112,16},{1... | collective-permute-start | bytes 12296 | tf_op jit(solution)/shard_map/ppermute | solution.py:466
  8.8 3.7 %collective-permute-start = (f32[8,128]{1,0:T(8,128)S(1)}, f32[8,128]{1,0:T(8,128)S(1)}, u32[]{:S(2)}, u32[]{:S(2)}) collective-permute-start(f32[8,128]{1,0:T(8,128)S(1)} %get-tuple-element.41.a), channel_id=1, source_target_pairs={{0,32},{16,48},{32,0},{48,16},{64,96},{80,112},{96,64},{112,80},{1... | collective-permute-start | bytes 12296 | tf_op jit(solution)/shard_map/ppermute | solution.py:466
  12.5 5.2 %collective-permute-start.3 = (f32[8,128]{1,0:T(8,128)S(1)}, f32[8,128]{1,0:T(8,128)S(1)}, u32[]{:S(2)}, u32[]{:S(2)}) collective-permute-start(f32[8,128]{1,0:T(8,128)S(1)} %add_four.2.here_ref), channel_id=1, source_target_pairs={{0,16},{16,0},{32,48},{48,32},{64,80},{80,64},{96,112},{112,96},{1... | collective-permute-start | bytes 12296 | tf_op jit(solution)/shard_map/ppermute | solution.py:466
  22.8 27.8 %collective-permute-start.4 = (f32[2048,256]{1,0:T(8,128)S(1)}, f32[2048,256]{1,0:T(8,128)S(1)}, u32[]{:S(2)}, u32[]{:S(2)}) collective-permute-start(f32[2048,256]{1,0:T(8,128)S(1)} %get-tuple-element.44.sent_ref), channel_id=1, source_target_pairs={{0,1},{1,2},{2,3},{3,4},{4,5},{5,6},{6,7},{7,8},{8,9},{9,10},{10,1... | collective-permute-start | bytes 6291464 | tf_op jit(solution)/shard_map/ppermute | solution.py:461
  22.8 27.7 %collective-permute-start.5 = (f32[2048,256]{1,0:T(8,128)S(1)}, f32[2048,256]{1,0:T(8,128)S(1)}, u32[]{:S(2)}, u32[]{:S(2)}) collective-permute-start(f32[2048,256]{1,0:T(8,128)S(1)} %get-tuple-element.45.sent_ref), channel_id=1, source_target_pairs={{0,15},{1,0},{2,1},{3,2},{4,3},{5,4},{6,5},{7,6},{8,7},{9,8},{10,9... | collective-permute-start | bytes 6291464 | tf_op jit(solution)/shard_map/ppermute | solution.py:461
  26.7 8.8 %collective-permute-start.6 = (f32[8,256]{1,0:T(8,128)S(1)}, f32[8,256]{1,0:T(8,128)S(1)}, u32[]{:S(2)}, u32[]{:S(2)}) collective-permute-start(f32[8,256]{1,0:T(8,128)S(1)} %get-tuple-element.47), channel_id=1, source_target_pairs={{0,33},{1,34},{2,35},{3,36},{4,37},{5,38},{6,39},{7,40},{8,41},{9,... | collective-permute-start | bytes 24584 | tf_op jit(solution)/shard_map/ppermute | solution.py:476
  26.7 8.8 %collective-permute-start.7 = (f32[8,256]{1,0:T(8,128)S(1)}, f32[8,256]{1,0:T(8,128)S(1)}, u32[]{:S(2)}, u32[]{:S(2)}) collective-permute-start(f32[8,256]{1,0:T(8,128)S(1)} %get-tuple-element.48), channel_id=1, source_target_pairs={{0,47},{1,32},{2,33},{3,34},{4,35},{5,36},{6,37},{7,38},{8,39},{9,... | collective-permute-start | bytes 24584 | tf_op jit(solution)/shard_map/ppermute | solution.py:476
  35.6 6.0 %collective-permute-start.10 = (f32[8,128]{1,0:T(8,128)S(1)}, f32[8,128]{1,0:T(8,128)S(1)}, u32[]{:S(2)}, u32[]{:S(2)}) collective-permute-start(f32[8,128]{1,0:T(8,128)S(1)} %mix.1.a), channel_id=1, source_target_pairs={{0,64},{16,80},{32,96},{48,112},{64,0},{80,16},{96,32},{112,48},{1... | collective-permute-start | bytes 12296 | tf_op jit(solution)/shard_map/ppermute | solution.py:466
  37.0 4.8 %collective-permute-start.9 = (f32[8,128]{1,0:T(8,128)S(1)}, f32[8,128]{1,0:T(8,128)S(1)}, u32[]{:S(2)}, u32[]{:S(2)}) collective-permute-start(f32[8,128]{1,0:T(8,128)S(1)} %mix.1.a), channel_id=1, source_target_pairs={{0,96},{16,112},{32,64},{48,80},{64,32},{80,48},{96,0},{112,16},{1... | collective-permute-start | bytes 12296 | tf_op jit(solution)/shard_map/ppermute | solution.py:466
  38.2 3.7 %collective-permute-start.8 = (f32[8,128]{1,0:T(8,128)S(1)}, f32[8,128]{1,0:T(8,128)S(1)}, u32[]{:S(2)}, u32[]{:S(2)}) collective-permute-start(f32[8,128]{1,0:T(8,128)S(1)} %mix.1.a), channel_id=1, source_target_pairs={{0,32},{16,48},{32,0},{48,16},{64,96},{80,112},{96,64},{112,80},{1... | collective-permute-start | bytes 12296 | tf_op jit(solution)/shard_map/ppermute | solution.py:466
  41.9 6.2 %collective-permute-start.11 = (f32[8,128]{1,0:T(8,128)S(1)}, f32[8,128]{1,0:T(8,128)S(1)}, u32[]{:S(2)}, u32[]{:S(2)}) collective-permute-start(f32[8,128]{1,0:T(8,128)S(1)} %add_four.3.here_ref), channel_id=1, source_target_pairs={{0,48},{16,32},{32,16},{48,0},{64,112},{80,96},{96,80},{112,64},{1... | collective-permute-start | bytes 12296 | tf_op jit(solution)/shard_map/ppermute | solution.py:466
  55.9 46.0 %collective-permute-start.12 = (f32[2048,256]{1,0:T(8,128)S(1)}, f32[2048,256]{1,0:T(8,128)S(1)}, u32[]{:S(2)}, u32[]{:S(2)}) collective-permute-start(f32[2048,256]{1,0:T(8,128)S(1)} %get-tuple-element.53.up), channel_id=1, source_target_pairs={{0,1},{1,2},{2,3},{3,4},{4,5},{5,6},{6,7},{7,8},{8,9},{9,10},{10,1... | collective-permute-start | bytes 6291464 | tf_op jit(solution)/shard_map/ppermute | solution.py:461
  56.1 45.8 %collective-permute-start.13 = (f32[2048,256]{1,0:T(8,128)S(1)}, f32[2048,256]{1,0:T(8,128)S(1)}, u32[]{:S(2)}, u32[]{:S(2)}) collective-permute-start(f32[2048,256]{1,0:T(8,128)S(1)} %get-tuple-element.54.down), channel_id=1, source_target_pairs={{0,15},{1,0},{2,1},{3,2},{4,3},{5,4},{6,5},{7,6},{8,7},{9,8},{10,9... | collective-permute-start | bytes 6291464 | tf_op jit(solution)/shard_map/ppermute | solution.py:461
  59.9 13.5 %collective-permute-start.14 = (f32[2,128,512]{2,1,0:T(8,128)S(1)}, f32[2,128,512]{2,1,0:T(8,128)S(1)}, u32[]{:S(2)}, u32[]{:S(2)}) collective-permute-start(f32[2,128,512]{2,1,0:T(8,128)S(1)} %get-tuple-element.57), channel_id=1, source_target_pairs={{0,96},{16,112},{32,64},{48,80},{64,32},{80,48},{96,0},{112,16},{1... | collective-permute-start | bytes 1572872 | tf_op jit(solution)/shard_map/ppermute | solution.py:466
  61.8 13.0 %collective-permute-start.15 = (f32[2,128,512]{2,1,0:T(8,128)S(1)}, f32[2,128,512]{2,1,0:T(8,128)S(1)}, u32[]{:S(2)}, u32[]{:S(2)}) collective-permute-start(f32[2,128,512]{2,1,0:T(8,128)S(1)} %get-tuple-element.58), channel_id=1, source_target_pairs={{0,32},{16,48},{32,0},{48,16},{64,96},{80,112},{96,64},{112,80},{1... | collective-permute-start | bytes 1572872 | tf_op jit(solution)/shard_map/ppermute | solution.py:466
  72.0 16.2 %collective-permute-start.18 = (f32[2,128,512]{2,1,0:T(8,128)S(1)}, f32[2,128,512]{2,1,0:T(8,128)S(1)}, u32[]{:S(2)}, u32[]{:S(2)}) collective-permute-start(f32[2,128,512]{2,1,0:T(8,128)S(1)} %get-tuple-element.64), channel_id=1, source_target_pairs={{0,96},{16,112},{32,64},{48,80},{64,32},{80,48},{96,0},{112,16},{1... | collective-permute-start | bytes 1572872 | tf_op jit(solution)/shard_map/ppermute | solution.py:466
  73.4 15.7 %collective-permute-start.20 = (f32[2,128,512]{2,1,0:T(8,128)S(1)}, f32[2,128,512]{2,1,0:T(8,128)S(1)}, u32[]{:S(2)}, u32[]{:S(2)}) collective-permute-start(f32[2,128,512]{2,1,0:T(8,128)S(1)} %get-tuple-element.68), channel_id=1, source_target_pairs={{0,32},{16,48},{32,0},{48,16},{64,96},{80,112},{96,64},{112,80},{1... | collective-permute-start | bytes 1572872 | tf_op jit(solution)/shard_map/ppermute | solution.py:466
  74.9 17.0 %collective-permute-start.22 = (f32[128,512]{1,0:T(8,128)S(1)}, f32[128,512]{1,0:T(8,128)S(1)}, u32[]{:S(2)}, u32[]{:S(2)}) collective-permute-start(f32[128,512]{1,0:T(8,128)S(1)} %get-tuple-element.72), channel_id=1, source_target_pairs={{0,96},{16,112},{32,64},{48,80},{64,32},{80,48},{96,0},{112,16},{1... | collective-permute-start | bytes 786440 | tf_op jit(solution)/shard_map/ppermute | solution.py:466
  88.2 6.9 %collective-permute-start.19 = (f32[128,512]{1,0:T(8,128)S(1)}, f32[128,512]{1,0:T(8,128)S(1)}, u32[]{:S(2)}, u32[]{:S(2)}) collective-permute-start(f32[128,512]{1,0:T(8,128)S(1)} %get-tuple-element.66), channel_id=1, source_target_pairs={{0,32},{16,48},{32,0},{48,16},{64,96},{80,112},{96,64},{112,80},{1... | collective-permute-start | bytes 786440 | tf_op jit(solution)/shard_map/ppermute | solution.py:466
  89.2 7.7 %collective-permute-start.21 = (f32[128,512]{1,0:T(8,128)S(1)}, f32[128,512]{1,0:T(8,128)S(1)}, u32[]{:S(2)}, u32[]{:S(2)}) collective-permute-start(f32[128,512]{1,0:T(8,128)S(1)} %get-tuple-element.70), channel_id=1, source_target_pairs={{0,96},{16,112},{32,64},{48,80},{64,32},{80,48},{96,0},{112,16},{1... | collective-permute-start | bytes 786440 | tf_op jit(solution)/shard_map/ppermute | solution.py:466
  92.0 9.6 %collective-permute-start.16 = (f32[2,64,512]{2,1,0:T(8,128)S(1)}, f32[2,64,512]{2,1,0:T(8,128)S(1)}, u32[]{:S(2)}, u32[]{:S(2)}) collective-permute-start(f32[2,64,512]{2,1,0:T(8,128)S(1)} %get-tuple-element.61), channel_id=1, source_target_pairs={{0,16},{16,0},{32,48},{48,32},{64,80},{80,64},{96,112},{112,96},{1... | collective-permute-start | bytes 786440 | tf_op jit(solution)/shard_map/ppermute | solution.py:466
  96.9 9.7 %collective-permute-start.23 = (f32[3,64,512]{2,1,0:T(8,128)S(1)}, f32[3,64,512]{2,1,0:T(8,128)S(1)}, u32[]{:S(2)}, u32[]{:S(2)}) collective-permute-start(f32[3,64,512]{2,1,0:T(8,128)S(1)} %get-tuple-element.74), channel_id=1, source_target_pairs={{0,16},{16,0},{32,48},{48,32},{64,80},{80,64},{96,112},{112,96},{1... | collective-permute-start | bytes 1179656 | tf_op jit(solution)/shard_map/ppermute | solution.py:466
  101.6 5.0 %collective-permute-start.17 = (f32[64,512]{1,0:T(8,128)S(1)}, f32[64,512]{1,0:T(8,128)S(1)}, u32[]{:S(2)}, u32[]{:S(2)}) collective-permute-start(f32[64,512]{1,0:T(8,128)S(1)} %get-tuple-element.63), channel_id=1, source_target_pairs={{0,32},{16,48},{32,0},{48,16},{64,96},{80,112},{96,64},{112,80},{1... | collective-permute-start | bytes 393224 | tf_op jit(solution)/shard_map/ppermute | solution.py:466
